TPU v7x, 128 devices: a whole 4x4x4 slice. The times are simulated.
128 devices in a mesh: prompt: 8 (over z, core), learner: 16 (over x, y).
Axes of the slice: x: 4, y: 4, z: 4, core: 2. Of those that a mesh axis runs over, the one named last changes fastest.
Arguments:
- prefix_k: bfloat16 [8, 2048, 512], P('prompt', 'learner'), may hold values from -6 to 6
- prefix_v: bfloat16 [8, 2048, 512], P('prompt', 'learner'), may hold values from -30 to 30
- queries: bfloat16 [128, 256, 2560], P(('prompt', 'learner')), may hold values from -6 to 6
- comp_k: bfloat16 [128, 256, 512], P(('prompt', 'learner')), may hold values from -6 to 6
- comp_v: bfloat16 [128, 256, 512], P(('prompt', 'learner')), may hold values from -30 to 30
- out_grad: bfloat16 [128, 256, 2560], P(('prompt', 'learner')), may hold values from -6 to 6
- lengths: int32 [128], replicated, may hold values from 128 to 256, as said below
- owner_map: int32 [8], replicated, may hold values from 0 to 7, each once
Outputs:
- attended: bfloat16 [128, 256, 2560], P(('prompt', 'learner'))
- grad_queries: bfloat16 [128, 256, 2560], P(('prompt', 'learner'))
- grad_comp_k: bfloat16 [128, 256, 512], P(('prompt', 'learner'))
- grad_comp_v: bfloat16 [128, 256, 512], P(('prompt', 'learner'))
- grad_prefix_k: float32 [8, 2048, 512], P('prompt', 'learner')
- grad_prefix_v: float32 [8, 2048, 512], P('prompt', 'learner')
Inputs may be any that keep to these rules, and one draw needn't show every extreme that they name: `lengths`: every length is a multiple of 128; among the 16 completions of each prompt one has length exactly 256. `owner_map`: a permutation of the prompt groups.
All inputs are finite; a program needn't handle non-finite values.
Results may differ from a plain program's by a relative error of at most 0.04.
Values may be sent and summed in bfloat16 or wider, within the bound.
No kernel may reach another device: no remote copies, remote signals or barrier semaphores. Data moves between devices by JAX's collectives and lax.ppermute only.
A program may use at most 192 MiB of HBM per device.

v0:
```python
import functools

import jax
import jax.numpy as jnp
from jax import lax
from jax.experimental import pallas as pl
from jax.experimental.pallas import tpu as pltpu
from jax.sharding import PartitionSpec as P

KV_HEADS = 4
HEAD_DIM = 128
COMP_LEN = 256
Q_PER_KV = 5
SHARD = 128
SIDE = 4
PREFIX = SIDE * SIDE * SHARD
TOTAL = PREFIX + COMP_LEN

INV_ROOT = HEAD_DIM**-0.5
EXP2_SCALE = INV_ROOT * 1.4426950408889634
VERY_LOW = -1e30

SHIFTS = (0, 1, 3, 2)

GATHER_GROUPS = ((0,), (1, 2, 3))
CALL_GROUPS = ((0,), (1,), (2,), (3,))
REDUCE_GROUPS = ((0, 1), (2, 3))

NN = (((1,), (0,)), ((), ()))
NT = (((1,), (1,)), ((), ()))


def mxu(left, right, dims):
    return lax.dot_general(left, right, dims, preferred_element_type=jnp.float32)


def attend_kernel(tile, n_alias, at_ref, q_ref, g_ref, ck_ref, cv_ref, *rest):
    kept, crossed = rest[0:4], rest[4]
    att_ref, dq_ref, dck_ref, dcv_ref, keep_ref, send_ref = rest[5 + n_alias : 11 + n_alias]
    keys, vals, acc_k, acc_v = rest[11 + n_alias :]
    core = at_ref[1]
    member = pl.program_id(1)
    own = pl.ds(PREFIX, COMP_LEN)

    def fill(mine, theirs):
        for a in range(SIDE):
            for b in range(SIDE):
                mine[pl.ds((a * SIDE + b) * SHARD, SHARD), :] = kept[a][0, b]
                theirs[pl.ds((b * SIDE + a) * SHARD, SHARD), :] = crossed[a, b]

    @pl.when((member == 0) & (core == 0))
    def _():
        fill(keys, vals)

    @pl.when((member == 0) & (core == 1))
    def _():
        fill(vals, keys)

    @pl.when(member == 0)
    def _():
        keys[own, :] = ck_ref[...]
        vals[own, :] = cv_ref[...]
        acc_k[...] = jnp.zeros_like(acc_k)
        acc_v[...] = jnp.zeros_like(acc_v)

    query = q_ref[...]
    grad = g_ref[...]
    spans = [pl.ds(t, tile) for t in range(0, PREFIX, tile)] + [own]
    row_no = lax.broadcasted_iota(jnp.int32, (COMP_LEN, COMP_LEN), 0)
    col_no = lax.broadcasted_iota(jnp.int32, (COMP_LEN, COMP_LEN), 1)
    scores = [mxu(query, keys[span, :], NT) for span in spans]
    scores[-1] = jnp.where(col_no <= row_no, scores[-1], VERY_LOW)
    top = functools.reduce(jnp.maximum, [jnp.max(s, axis=1, keepdims=True) for s in scores])
    top = top * EXP2_SCALE
    weights = [jnp.exp2(s * EXP2_SCALE - top) for s in scores]
    total = sum(jnp.sum(w, axis=1, keepdims=True) for w in weights)
    weights_bf = [w.astype(jnp.bfloat16) for w in weights]
    numer = sum(mxu(w, vals[span, :], NN) for w, span in zip(weights_bf, spans))
    live = lax.broadcasted_iota(jnp.int32, (COMP_LEN, 1), 0) < at_ref[0]
    inv_total = jnp.where(live, 1.0 / total, 0.0)
    attended = (numer * inv_total).astype(jnp.bfloat16)
    att_ref[...] = attended
    grad_wide = grad.astype(jnp.float32)
    dsum = jnp.sum(attended.astype(jnp.float32) * grad_wide, axis=1, keepdims=True)
    grad_t = (grad_wide * inv_total).astype(jnp.bfloat16).T
    query_t = (query.astype(jnp.float32) * (inv_total * INV_ROOT)).astype(jnp.bfloat16).T
    dq = 0.0
    for span, w, w_bf in zip(spans, weights, weights_bf):
        dweight = mxu(grad, vals[span, :], NT)
        dscore = (w * (dweight - dsum)).astype(jnp.bfloat16)
        dq = dq + mxu(dscore, keys[span, :], NN)
        acc_k[:, span] += mxu(query_t, dscore, NN)
        acc_v[:, span] += mxu(grad_t, w_bf, NN)
    dq_ref[...] = (dq * (inv_total * INV_ROOT)).astype(jnp.bfloat16)

    def empty(mine, theirs):
        for a in range(SIDE):
            for b in range(SIDE):
                cols = pl.ds((a * SIDE + b) * SHARD, SHARD)
                keep_ref[a, b] = mine[:, cols].T.astype(jnp.bfloat16)
                cols = pl.ds((b * SIDE + a) * SHARD, SHARD)
                send_ref[a, b] = theirs[:, cols].T.astype(jnp.bfloat16)

    @pl.when((member == Q_PER_KV - 1) & (core == 0))
    def _():
        empty(acc_k, acc_v)

    @pl.when((member == Q_PER_KV - 1) & (core == 1))
    def _():
        empty(acc_v, acc_k)

    @pl.when(member == Q_PER_KV - 1)
    def _():
        dck_ref[...] = acc_k[:, own].T.astype(jnp.bfloat16)
        dcv_ref[...] = acc_v[:, own].T.astype(jnp.bfloat16)


def attend(heads, at, rows_in, kept, crossed, in_at, out_at, out_heads, held, grads):
    first = heads[0]
    per_head = pl.BlockSpec(
        (COMP_LEN, HEAD_DIM), lambda h, j, _: (0, (h + first) * Q_PER_KV + j)
    )
    per_kv = pl.BlockSpec((COMP_LEN, HEAD_DIM), lambda h, j, _: (0, h + first))
    kept_in = pl.BlockSpec((1, SIDE, SHARD, HEAD_DIM), lambda h, j, _: (0, 0, 0, h + in_at))
    square = (SIDE, SIDE, SHARD, HEAD_DIM)
    crossed_in = pl.BlockSpec(square, lambda h, j, _: (0, 0, 0, h + in_at))
    square_out = pl.BlockSpec(square, lambda h, j, _: (0, 0, 0, h + out_at))
    wide = jax.ShapeDtypeStruct((COMP_LEN, KV_HEADS * Q_PER_KV * HEAD_DIM), jnp.bfloat16)
    narrow = jax.ShapeDtypeStruct((COMP_LEN, KV_HEADS * HEAD_DIM), jnp.bfloat16)
    part = jax.ShapeDtypeStruct((SIDE, SIDE, SHARD, out_heads * HEAD_DIM), jnp.bfloat16)
    extra, aliases = [], {}
    base = 1 + 4 + 5
    for out_no, item in enumerate((held or [None] * 4) + (grads or [None] * 2)):
        if item is not None:
            aliases[base + len(extra)] = out_no
            extra.append(item)
    return pl.pallas_call(
        functools.partial(attend_kernel, 1024, len(extra)),
        grid_spec=pltpu.PrefetchScalarGridSpec(
            num_scalar_prefetch=1,
            grid=(len(heads), Q_PER_KV),
            in_specs=[per_head, per_head, per_kv, per_kv]
            + [kept_in] * 4
            + [crossed_in]
            + [pl.BlockSpec(memory_space=pl.ANY)] * len(extra),
            out_specs=[per_head, per_head, per_kv, per_kv] + [square_out] * 2,
            scratch_shapes=[pltpu.VMEM((TOTAL, HEAD_DIM), jnp.bfloat16)] * 2
            + [pltpu.VMEM((HEAD_DIM, TOTAL), jnp.float32)] * 2,
        ),
        out_shape=[wide, wide, narrow, narrow] + [part] * 2,
        input_output_aliases=aliases,
        compiler_params=pltpu.CompilerParams(vmem_limit_bytes=60 * 2**20),
        cost_estimate=pl.CostEstimate(
            flops=len(heads) * 6 * 2 * Q_PER_KV * COMP_LEN * TOTAL * HEAD_DIM,
            bytes_accessed=len(heads) * 5 * 2**20,
            transcendentals=len(heads) * Q_PER_KV * COMP_LEN * TOTAL,
        ),
    )(at, *rows_in, *kept, crossed, *extra)


def move_plane(item, shift, first):
    pairs = []
    for p in range(8):
        along_x = (p % 2 == 0) == first
        for x in range(SIDE):
            for y in range(SIDE):
                to_x = (x + shift) % SIDE if along_x else x
                to_y = y if along_x else (y + shift) % SIDE
                pairs.append(((p * SIDE + x) * SIDE + y, (p * SIDE + to_x) * SIDE + to_y))
    return lax.ppermute(item, ("prompt", "learner"), pairs)


def move_z(item, shift):
    pairs = [(z * 2 + c, ((z + shift) % 4) * 2 + c) for z in range(4) for c in range(2)]
    return lax.ppermute(item, "prompt", pairs)


def swap_cores(item):
    return lax.ppermute(item, "prompt", [(p, p ^ 1) for p in range(8)])


def spread(item, first):
    return [move_plane(item, s, first) if s else item for s in SHIFTS]


class Place:
    def __init__(self, source_of):
        here = lax.axis_index("prompt")
        self.z, self.core = here // 2, here % 2
        self.mine = lax.dynamic_index_in_dim(source_of, here, 0, keepdims=False)
        self.other = lax.dynamic_index_in_dim(source_of, here ^ 1, 0, keepdims=False)

    def of(self, column, who):
        return lax.select_n((self.z - who // 2) % 4, *column)


def tie(*trees):
    return lax.optimization_barrier(trees)


def bring_column(item):
    return [item] + [move_z(item, s) for s in (1, 2, 3)]


def choose(column, place):
    mine, other = place.of(column, place.mine), place.of(column, place.other)
    on_first = place.core == 0
    send = jnp.stack([jnp.where(on_first, p[1], p[0]) for p in (other, mine)])
    keep = jnp.stack([jnp.where(on_first, p[0], p[1]) for p in (mine, other)])
    return keep, send


def join(keep, got, place):
    same_core = jnp.stack([place.mine, place.other]) % 2 == place.core
    return jnp.where(same_core[:, None, None], keep, got)


def bring_row(pair):
    return jnp.stack(spread(pair, True), axis=1)


def cross(kept):
    return swap_cores(jnp.stack([part[1] for part in kept]))


def return_row(keep, got):
    return [jnp.stack([keep[a], got[a]]) for a in range(SIDE)]


def move_back(items, first):
    return [move_plane(item, -s, first) if s else item for item, s in zip(items, SHIFTS)]


def add_up(items):
    return sum(item.astype(jnp.float32) for item in items).astype(jnp.bfloat16)


def give_back(row, place):
    pair = add_up(move_back([row[:, b] for b in range(SIDE)], True))
    column = [pair] + [move_z(pair, s) for s in (1, 2, 3)]

    def pick(who):
        both = place.of(column, who)
        return jnp.where(who % 2 == place.core, both[0], both[1])

    kept = pick(place.mine)
    crossed = swap_cores(pick(place.other))
    on_first = place.core == 0
    dk = jnp.where(on_first, kept, crossed)
    dv = jnp.where(on_first, crossed, kept)
    return dk.astype(jnp.float32), dv.astype(jnp.float32)


def body(prefix_k, prefix_v, queries, comp_k, comp_v, out_grad, lengths, owner_map):
    n_learn = lax.axis_size("learner")
    here = lax.axis_index("prompt")
    me = here * n_learn + lax.axis_index("learner")
    groups = jnp.arange(owner_map.shape[0], dtype=jnp.int32)
    holder = jnp.sum(jnp.where(owner_map[None, :] == groups[:, None], groups[None, :], 0), axis=1)
    my_len = lax.dynamic_index_in_dim(lengths, me, 0, keepdims=False)
    at = jnp.stack([my_len, here % 2])
    rows_in = [queries[0], out_grad[0], comp_k[0], comp_v[0]]

    place = Place(holder)
    first, rest = [
        jnp.stack([t[0, :, g[0] * HEAD_DIM : (g[-1] + 1) * HEAD_DIM] for t in (prefix_k, prefix_v)])
        for g in GATHER_GROUPS
    ]
    column = bring_column(first)
    keep, send = choose(column, place)
    send, rest = tie(send, rest)
    got = swap_cores(send)
    rest_column = bring_column(rest)
    row = bring_row(join(keep, got, place))
    rest_keep, rest_send = choose(rest_column, place)
    rest_send, row = tie(rest_send, row)
    kept = spread(row, False)
    rest_got = swap_cores(rest_send)
    rest_row = bring_row(join(rest_keep, rest_got, place))
    crossed = cross(kept)
    crossed, kept, rest_row = tie(crossed, kept, rest_row)
    rest_kept = spread(rest_row, False)

    width = len(REDUCE_GROUPS[0])

    def call(head, source, in_at, held, grads):
        outs = attend((head,), at, rows_in, *source, in_at, head % width, width, held, grads)
        return list(outs[:4]), list(outs[4:])

    held, _sums = call(0, (kept, crossed), 0, None, None)
    _sums, rest_kept = tie(_sums, rest_kept)
    rest_source = (rest_kept, cross(rest_kept))
    held, (keep, send) = call(1, rest_source, 0, held, _sums)
    got = swap_cores(send)
    held, _sums = call(2, rest_source, 1, held, None)
    held, got = tie(held, got)
    back = move_back(return_row(keep, got), False)
    held, (rest_keep, rest_send) = call(3, rest_source, 2, held, _sums)
    rest_send, back = tie(rest_send, back)
    rest_got = swap_cores(rest_send)
    place = Place(owner_map)
    rest_back = move_back(return_row(rest_keep, rest_got), False)
    grads = [give_back(add_up(b), place) for b in (back, rest_back)]
    attended, grad_queries, grad_comp_k, grad_comp_v = held
    return (
        attended[None],
        grad_queries[None],
        grad_comp_k[None],
        grad_comp_v[None],
        jnp.concatenate([dk for dk, _ in grads], axis=1)[None],
        jnp.concatenate([dv for _, dv in grads], axis=1)[None],
    )


def solution(mesh):
    by_prompt = P("prompt", "learner", None)
    by_completion = P(("prompt", "learner"), None, None)
    return jax.shard_map(
        body,
        mesh=mesh,
        in_specs=(by_prompt,) * 2 + (by_completion,) * 4 + (P(), P()),
        out_specs=(by_completion,) * 4 + (by_prompt,) * 2,
        check_vma=False,
    )
```

profile of v0, /device:TPU:1, one launch (start us, length us, event | category | flops | bytes accessed | tf_op | source)
XLA Modules:
  0.0 198.8 jit_solution(10789631911516047658)
XLA Ops:
  2.2 2.5 %collective-permute-start = (bf16[2,128,128]{2,1,0:T(8,128)(2,1)S(1)}, bf16[2,128,128]{2,1,0:T(8,128)(2,1)S(1)}, u32[]{:S(2)}, u32[]{:S(2)}) collective-permute-start(bf16[2,128,128]{2,1,0:T(8,128)(2,1)S(1)} %pad_maximum_fusion.13), channel_id=1, source_target_pairs={{0,32},{16,48},{32,64},{48,80},{64,96},{80,112},{96,0},{112,16},{1... | collective-permute-start | bytes 196616 | tf_op jit(solution)/shard_map/ppermute | solution.py:175
  4.7 3.3 %collective-permute-start.1 = (bf16[2,128,128]{2,1,0:T(8,128)(2,1)S(1)}, bf16[2,128,128]{2,1,0:T(8,128)(2,1)S(1)}, u32[]{:S(2)}, u32[]{:S(2)}) collective-permute-start(bf16[2,128,128]{2,1,0:T(8,128)(2,1)S(1)} %pad_maximum_fusion.13), channel_id=1, source_target_pairs={{0,64},{16,80},{32,96},{48,112},{64,0},{80,16},{96,32},{112,48},{1... | collective-permute-start | bytes 196616 | tf_op jit(solution)/shard_map/ppermute | solution.py:175
  22.6 2.2 %collective-permute-start.5 = (bf16[2,128,384]{2,1,0:T(8,128)(2,1)S(1)}, bf16[2,128,384]{2,1,0:T(8,128)(2,1)S(1)}, u32[]{:S(2)}, u32[]{:S(2)}) collective-permute-start(bf16[2,128,384]{2,1,0:T(8,128)(2,1)S(1)} %pad_maximum_fusion.11), channel_id=1, source_target_pairs={{0,96},{16,112},{32,0},{48,16},{64,32},{80,48},{96,64},{112,80},{1... | collective-permute-start | bytes 589832 | tf_op jit(solution)/shard_map/ppermute | solution.py:175
  28.3 3.1 %collective-permute-done.9 = bf16[2,128,128]{2,1,0:T(8,128)(2,1)S(1)} collective-permute-done((bf16[2,128,128]{2,1,0:T(8,128)(2,1)S(1)}, bf16[2,128,128]{2,1,0:T(8,128)(2,1)S(1)}, u32[]{:S(2)}, u32[]{:S(2)}) %collective-permute-start.9) | collective-permute-done | bytes 65568 | tf_op jit(solution)/shard_map/ppermute | solution.py:170
  31.4 2.0 %collective-permute-done.3 = bf16[2,128,384]{2,1,0:T(8,128)(2,1)S(1)} collective-permute-done((bf16[2,128,384]{2,1,0:T(8,128)(2,1)S(1)}, bf16[2,128,384]{2,1,0:T(8,128)(2,1)S(1)}, u32[]{:S(2)}, u32[]{:S(2)}) %collective-permute-start.3) | collective-permute-done | bytes 196640 | tf_op jit(solution)/shard_map/ppermute | solution.py:175
  35.2 2.2 %collective-permute-start.11 = (bf16[2,4,128,128]{3,2,1,0:T(8,128)(2,1)S(1)}, bf16[2,4,128,128]{3,2,1,0:T(8,128)(2,1)S(1)}, u32[]{:S(2)}, u32[]{:S(2)}) collective-permute-start(bf16[2,4,128,128]{3,2,1,0:T(8,128)(2,1)S(1)} %pad_maximum_fusion.10.rest_0_), channel_id=1, source_target_pairs={{0,3},{1,0},{2,1},{3,2},{4,7},{5,4},{6,5},{7,6},{8,11},{9,8},{10,9... | collective-permute-start | bytes 786440 | tf_op jit(solution)/shard_map/ppermute | solution.py:170
  43.5 1.8 collective-permute-done.12.rest_3_
  51.7 2.1 %collective-permute-done.15 = bf16[2,128,384]{2,1,0:T(8,128)(2,1)S(1)} collective-permute-done((bf16[2,128,384]{2,1,0:T(8,128)(2,1)S(1)}, bf16[2,128,384]{2,1,0:T(8,128)(2,1)S(1)}, u32[]{:S(2)}, u32[]{:S(2)}) %collective-permute-start.15) | collective-permute-done | bytes 196640 | tf_op jit(solution)/shard_map/ppermute | solution.py:170
  55.2 1.8 collective-permute-done.17
  58.2 1.9 collective-permute-start.19
  63.1 16.4 %shard_map.127 = (bf16[256,2560]{1,0:T(8,128)(2,1)}, bf16[256,2560]{1,0:T(8,128)(2,1)}, bf16[256,512]{1,0:T(8,128)(2,1)}, bf16[256,512]{1,0:T(8,128)(2,1)}, bf16...) custom-call(s32[2]{0:T(128)} %pad_add_fusion.at_ref, bf16[256,2560]{1,0:T(8,128)(2,1)} %bitcast.95, ...), custom_call_target="tpu_custom_call" | custom-call | flops 4529848320 | bytes 5242880 | tf_op jit(solution)/shard_map/pallas_call | solution.py:137
  82.9 3.0 %collective-permute-done.21.rest_4_ = bf16[4,4,128,384]{3,2,1,0:T(8,128)(2,1)S(1)} collective-permute-done((bf16[4,4,128,384]{3,2,1,0:T(8,128)(2,1)S(1)}, bf16[4,4,128,384]{3,2,1,0:T(8,128)(2,1)S(1)}, u32[]{:S(2)}, u32[]{:S(2)}) %collective-permute-start.21) | collective-permute-done | bytes 1572896 | tf_op jit(solution)/shard_map/ppermute | solution.py:179
  87.1 16.5 %shard_map.128 = (bf16[256,2560]{1,0:T(8,128)(2,1)}, bf16[256,2560]{1,0:T(8,128)(2,1)}, bf16[256,512]{1,0:T(8,128)(2,1)}, bf16[256,512]{1,0:T(8,128)(2,1)}, bf16...) custom-call(s32[2]{0:T(128)} %pad_add_fusion.at_ref, ...), custom_call_target="tpu_custom_call", output_to_operand_aliasing={{0}: (10, {}), {1}: (11, {}), {2}: (12, {}), {3}: (13, {}),... | custom-call | flops 4529848320 | bytes 5242880 | tf_op jit(solution)/shard_map/pallas_call | solution.py:137
  105.5 16.5 %shard_map.129 = (bf16[256,2560]{1,0:T(8,128)(2,1)}, bf16[256,2560]{1,0:T(8,128)(2,1)}, bf16[256,512]{1,0:T(8,128)(2,1)}, bf16[256,512]{1,0:T(8,128)(2,1)}, bf16...) custom-call(s32[2]{0:T(128)} %pad_add_fusion.at_ref, ...), custom_call_target="tpu_custom_call", output_to_operand_aliasing={{0}: (10, {}), {1}: (11, {}), {2}: (12, {}), {3}: (13, {})} | custom-call | flops 4529848320 | bytes 5242880 | tf_op jit(solution)/shard_map/pallas_call | solution.py:137
  122.2 1.8 collective-permute-start.25
  125.6 2.1 %collective-permute-start.23 = (bf16[2,4,128,256]{3,2,0,1:T(8,128)(2,1)}, bf16[2,4,128,256]{3,2,0,1:T(8,128)(2,1)S(1)}, u32[]{:S(2)}, u32[]{:S(2)}) collective-permute-start(bf16[2,4,128,256]{3,2,0,1:T(8,128)(2,1)} %pad_maximum_fusion.4), channel_id=1, source_target_pairs={{0,3},{1,0},{2,1},{3,2},{4,7},{5,4},{6,5},{7,6},{8,11},{9,8},{10,9... | collective-permute-start | bytes 1572872 | tf_op jit(solution)/shard_map/ppermute | solution.py:170
  127.7 16.5 %shard_map.130 = (bf16[256,2560]{1,0:T(8,128)(2,1)}, bf16[256,2560]{1,0:T(8,128)(2,1)}, bf16[256,512]{1,0:T(8,128)(2,1)}, bf16[256,512]{1,0:T(8,128)(2,1)}, bf16...) custom-call(s32[2]{0:T(128)} %pad_add_fusion.at_ref, ...), custom_call_target="tpu_custom_call", output_to_operand_aliasing={{0}: (10, {}), {1}: (11, {}), {2}: (12, {}), {3}: (13, {}),... | custom-call | flops 4529848320 | bytes 5242880 | tf_op jit(solution)/shard_map/pallas_call | solution.py:137
  144.3 2.1 %collective-permute-start.33 = (bf16[4,4,128,256]{3,2,1,0:T(8,128)(2,1)}, bf16[4,4,128,256]{3,2,1,0:T(8,128)(2,1)S(1)}, u32[]{:S(2)}, u32[]{:S(2)}) collective-permute-start(bf16[4,4,128,256]{3,2,1,0:T(8,128)(2,1)} %get-tuple-element.105), channel_id=1, source_target_pairs={{0,16},{16,0},{32,48},{48,32},{64,80},{80,64},{96,112},{112,96},{1... | collective-permute-start | bytes 3145736 | tf_op jit(solution)/shard_map/ppermute | solution.py:179
  156.0 4.1 %collective-permute-done.26 = bf16[2,128,256]{2,1,0:T(8,128)(2,1)S(1)} collective-permute-done((bf16[2,128,256]{2,1,0:T(8,128)(2,1)S(1)}, bf16[2,128,256]{2,1,0:T(8,128)(2,1)S(1)}, u32[]{:S(2)}, u32[]{:S(2)}) %collective-permute-start.26) | collective-permute-done | bytes 131104 | tf_op jit(solution)/shard_map/ppermute | solution.py:170
  167.9 3.1 %collective-permute-start.30 = (bf16[2,128,256]{2,1,0:T(8,128)(2,1)S(1)}, bf16[2,128,256]{2,1,0:T(8,128)(2,1)S(1)}, u32[]{:S(2)}, u32[]{:S(2)}) collective-permute-start(bf16[2,128,256]{2,1,0:T(8,128)(2,1)S(1)} %fusion.5), channel_id=1, source_target_pairs={{0,64},{16,80},{32,96},{48,112},{64,0},{80,16},{96,32},{112,48},{1... | collective-permute-start | bytes 393224 | tf_op jit(solution)/shard_map/ppermute | solution.py:175
  175.3 4.1 %collective-permute-done.38 = bf16[2,128,256]{2,1,0:T(8,128)(2,1)S(1)} collective-permute-done((bf16[2,128,256]{2,1,0:T(8,128)(2,1)S(1)}, bf16[2,128,256]{2,1,0:T(8,128)(2,1)S(1)}, u32[]{:S(2)}, u32[]{:S(2)}) %collective-permute-start.38) | collective-permute-done | bytes 131104 | tf_op jit(solution)/shard_map/ppermute | solution.py:170
  181.0 2.2 %collective-permute-start.42 = (bf16[2,128,256]{2,1,0:T(8,128)(2,1)S(1)}, bf16[2,128,256]{2,1,0:T(8,128)(2,1)S(1)}, u32[]{:S(2)}, u32[]{:S(2)}) collective-permute-start(bf16[2,128,256]{2,1,0:T(8,128)(2,1)S(1)} %fusion.2), channel_id=1, source_target_pairs={{0,96},{16,112},{32,0},{48,16},{64,32},{80,48},{96,64},{112,80},{1... | collective-permute-start | bytes 393224 | tf_op jit(solution)/shard_map/ppermute | solution.py:175
  183.2 9.4 %collective-permute-start.32 = (bf16[128,256]{1,0:T(8,128)(2,1)S(1)}, bf16[128,256]{1,0:T(8,128)(2,1)S(1)}, u32[]{:S(2)}, u32[]{:S(2)}) collective-permute-start(bf16[128,256]{1,0:T(8,128)(2,1)S(1)} %fusion.10), channel_id=1, source_target_pairs={{0,16},{16,0},{32,48},{48,32},{64,80},{80,64},{96,112},{112,96},{1... | collective-permute-start | bytes 196616 | tf_op jit(solution)/shard_map/ppermute | solution.py:179
  192.7 3.7 %collective-permute-start.43 = (bf16[128,256]{1,0:T(8,128)(2,1)S(1)}, bf16[128,256]{1,0:T(8,128)(2,1)S(1)}, u32[]{:S(2)}, u32[]{:S(2)}) collective-permute-start(bf16[128,256]{1,0:T(8,128)(2,1)S(1)} %fusion.8), channel_id=1, source_target_pairs={{0,16},{16,0},{32,48},{48,32},{64,80},{80,64},{96,112},{112,96},{1... | collective-permute-start | bytes 196616 | tf_op jit(solution)/shard_map/ppermute | solution.py:179
  (155 shorter events, 62.8 us)
Async XLA Ops:
  2.2 15.1 %collective-permute-start = (bf16[2,128,128]{2,1,0:T(8,128)(2,1)S(1)}, bf16[2,128,128]{2,1,0:T(8,128)(2,1)S(1)}, u32[]{:S(2)}, u32[]{:S(2)}) collective-permute-start(bf16[2,128,128]{2,1,0:T(8,128)(2,1)S(1)} %pad_maximum_fusion.13), channel_id=1, source_target_pairs={{0,32},{16,48},{32,64},{48,80},{64,96},{80,112},{96,0},{112,16},{1... | collective-permute-start | bytes 196616 | tf_op jit(solution)/shard_map/ppermute | solution.py:175
  4.7 12.5 %collective-permute-start.1 = (bf16[2,128,128]{2,1,0:T(8,128)(2,1)S(1)}, bf16[2,128,128]{2,1,0:T(8,128)(2,1)S(1)}, u32[]{:S(2)}, u32[]{:S(2)}) collective-permute-start(bf16[2,128,128]{2,1,0:T(8,128)(2,1)S(1)} %pad_maximum_fusion.13), channel_id=1, source_target_pairs={{0,64},{16,80},{32,96},{48,112},{64,0},{80,16},{96,32},{112,48},{1... | collective-permute-start | bytes 196616 | tf_op jit(solution)/shard_map/ppermute | solution.py:175
  8.0 9.2 %collective-permute-start.2 = (bf16[2,128,128]{2,1,0:T(8,128)(2,1)S(1)}, bf16[2,128,128]{2,1,0:T(8,128)(2,1)S(1)}, u32[]{:S(2)}, u32[]{:S(2)}) collective-permute-start(bf16[2,128,128]{2,1,0:T(8,128)(2,1)S(1)} %pad_maximum_fusion.13), channel_id=1, source_target_pairs={{0,96},{16,112},{32,0},{48,16},{64,32},{80,48},{96,64},{112,80},{1... | collective-permute-start | bytes 196616 | tf_op jit(solution)/shard_map/ppermute | solution.py:175
  21.7 11.7 %collective-permute-start.3 = (bf16[2,128,384]{2,1,0:T(8,128)(2,1)S(1)}, bf16[2,128,384]{2,1,0:T(8,128)(2,1)S(1)}, u32[]{:S(2)}, u32[]{:S(2)}) collective-permute-start(bf16[2,128,384]{2,1,0:T(8,128)(2,1)S(1)} %pad_maximum_fusion.11), channel_id=1, source_target_pairs={{0,32},{16,48},{32,64},{48,80},{64,96},{80,112},{96,0},{112,16},{1... | collective-permute-start | bytes 589832 | tf_op jit(solution)/shard_map/ppermute | solution.py:175
  22.5 11.0 %collective-permute-start.4 = (bf16[2,128,384]{2,1,0:T(8,128)(2,1)S(1)}, bf16[2,128,384]{2,1,0:T(8,128)(2,1)S(1)}, u32[]{:S(2)}, u32[]{:S(2)}) collective-permute-start(bf16[2,128,384]{2,1,0:T(8,128)(2,1)S(1)} %pad_maximum_fusion.11), channel_id=1, source_target_pairs={{0,64},{16,80},{32,96},{48,112},{64,0},{80,16},{96,32},{112,48},{1... | collective-permute-start | bytes 589832 | tf_op jit(solution)/shard_map/ppermute | solution.py:175
  22.6 11.1 %collective-permute-start.5 = (bf16[2,128,384]{2,1,0:T(8,128)(2,1)S(1)}, bf16[2,128,384]{2,1,0:T(8,128)(2,1)S(1)}, u32[]{:S(2)}, u32[]{:S(2)}) collective-permute-start(bf16[2,128,384]{2,1,0:T(8,128)(2,1)S(1)} %pad_maximum_fusion.11), channel_id=1, source_target_pairs={{0,96},{16,112},{32,0},{48,16},{64,32},{80,48},{96,64},{112,80},{1... | collective-permute-start | bytes 589832 | tf_op jit(solution)/shard_map/ppermute | solution.py:175
  35.2 8.3 %collective-permute-start.11 = (bf16[2,4,128,128]{3,2,1,0:T(8,128)(2,1)S(1)}, bf16[2,4,128,128]{3,2,1,0:T(8,128)(2,1)S(1)}, u32[]{:S(2)}, u32[]{:S(2)}) collective-permute-start(bf16[2,4,128,128]{3,2,1,0:T(8,128)(2,1)S(1)} %pad_maximum_fusion.10.rest_0_), channel_id=1, source_target_pairs={{0,3},{1,0},{2,1},{3,2},{4,7},{5,4},{6,5},{7,6},{8,11},{9,8},{10,9... | collective-permute-start | bytes 786440 | tf_op jit(solution)/shard_map/ppermute | solution.py:170
  38.5 8.8 %collective-permute-start.14 = (bf16[2,128,384]{2,1,0:T(8,128)(2,1)S(1)}, bf16[2,128,384]{2,1,0:T(8,128)(2,1)S(1)}, u32[]{:S(2)}, u32[]{:S(2)}) collective-permute-start(bf16[2,128,384]{2,1,0:T(8,128)(2,1)S(1)} %pad_maximum_fusion.12), channel_id=1, source_target_pairs={{0,16},{16,0},{32,48},{48,32},{64,80},{80,64},{96,112},{112,96},{1... | collective-permute-start | bytes 589832 | tf_op jit(solution)/shard_map/ppermute | solution.py:179
  46.1 11.1 %collective-permute-start.13 = (bf16[4,4,128,128]{3,2,1,0:T(8,128)(2,1)S(1)}, bf16[4,4,128,128]{3,2,1,0:T(8,128)(2,1)S(1)}, u32[]{:S(2)}, u32[]{:S(2)}) collective-permute-start(bf16[4,4,128,128]{3,2,1,0:T(8,128)(2,1)S(1)} %pad_maximum_fusion.2), channel_id=1, source_target_pairs={{0,16},{16,0},{32,48},{48,32},{64,80},{80,64},{96,112},{112,96},{1... | collective-permute-start | bytes 1572872 | tf_op jit(solution)/shard_map/ppermute | solution.py:179
  57.2 22.3 %collective-permute-start.18 = (bf16[2,4,128,384]{3,2,1,0:T(8,128)(2,1)S(1)}, bf16[2,4,128,384]{3,2,1,0:T(8,128)(2,1)S(1)}, u32[]{:S(2)}, u32[]{:S(2)}) collective-permute-start(bf16[2,4,128,384]{3,2,1,0:T(8,128)(2,1)S(1)} %pad_maximum_fusion.1.rest_0_), channel_id=1, source_target_pairs={{0,1},{1,2},{2,3},{3,0},{4,5},{5,6},{6,7},{7,4},{8,9},{9,10},{10,1... | collective-permute-start | bytes 2359304 | tf_op jit(solution)/shard_map/ppermute | solution.py:170
  58.2 21.4 %collective-permute-start.19 = (bf16[2,4,128,384]{3,2,1,0:T(8,128)(2,1)S(1)}, bf16[2,4,128,384]{3,2,1,0:T(8,128)(2,1)S(1)}, u32[]{:S(2)}, u32[]{:S(2)}) collective-permute-start(bf16[2,4,128,384]{3,2,1,0:T(8,128)(2,1)S(1)} %pad_maximum_fusion.1.rest_0_), channel_id=1, source_target_pairs={{0,3},{1,0},{2,1},{3,2},{4,7},{5,4},{6,5},{7,6},{8,11},{9,8},{10,9... | collective-permute-start | bytes 2359304 | tf_op jit(solution)/shard_map/ppermute | solution.py:170
  60.1 19.5 %collective-permute-start.20 = (bf16[2,4,128,384]{3,2,1,0:T(8,128)(2,1)S(1)}, bf16[2,4,128,384]{3,2,1,0:T(8,128)(2,1)S(1)}, u32[]{:S(2)}, u32[]{:S(2)}) collective-permute-start(bf16[2,4,128,384]{3,2,1,0:T(8,128)(2,1)S(1)} %pad_maximum_fusion.1.rest_0_), channel_id=1, source_target_pairs={{0,2},{1,3},{2,0},{3,1},{4,6},{5,7},{6,4},{7,5},{8,10},{9,11},{10,... | collective-permute-start | bytes 2359304 | tf_op jit(solution)/shard_map/ppermute | solution.py:170
  105.0 17.0 %collective-permute-start.22 = (bf16[4,4,128,256]{3,2,0,1:T(8,128)(2,1)S(1)}, bf16[4,4,128,256]{3,2,0,1:T(8,128)(2,1)S(1)}, u32[]{:S(2)}, u32[]{:S(2)}) collective-permute-start(bf16[4,4,128,256]{3,2,0,1:T(8,128)(2,1)S(1)} %copy.50), channel_id=1, source_target_pairs={{0,16},{16,0},{32,48},{48,32},{64,80},{80,64},{96,112},{112,96},{1... | collective-permute-start | bytes 3145736 | tf_op jit(solution)/shard_map/ppermute | solution.py:179
  122.2 22.1 %collective-permute-start.25 = (bf16[2,4,128,256]{3,2,0,1:T(8,128)(2,1)S(1)}, bf16[2,4,128,256]{3,2,0,1:T(8,128)(2,1)S(1)}, u32[]{:S(2)}, u32[]{:S(2)}) collective-permute-start(bf16[2,4,128,256]{3,2,0,1:T(8,128)(2,1)S(1)} %pad_maximum_fusion.6), channel_id=1, source_target_pairs={{0,2},{1,3},{2,0},{3,1},{4,6},{5,7},{6,4},{7,5},{8,10},{9,11},{10,... | collective-permute-start | bytes 1572872 | tf_op jit(solution)/shard_map/ppermute | solution.py:170
  124.0 20.2 %collective-permute-start.24 = (bf16[2,4,128,256]{3,2,0,1:T(8,128)(2,1)S(1)}, bf16[2,4,128,256]{3,2,0,1:T(8,128)(2,1)S(1)}, u32[]{:S(2)}, u32[]{:S(2)}) collective-permute-start(bf16[2,4,128,256]{3,2,0,1:T(8,128)(2,1)S(1)} %pad_maximum_fusion.5), channel_id=1, source_target_pairs={{0,1},{1,2},{2,3},{3,0},{4,5},{5,6},{6,7},{7,4},{8,9},{9,10},{10,1... | collective-permute-start | bytes 1572872 | tf_op jit(solution)/shard_map/ppermute | solution.py:170
  125.6 18.7 %collective-permute-start.23 = (bf16[2,4,128,256]{3,2,0,1:T(8,128)(2,1)}, bf16[2,4,128,256]{3,2,0,1:T(8,128)(2,1)S(1)}, u32[]{:S(2)}, u32[]{:S(2)}) collective-permute-start(bf16[2,4,128,256]{3,2,0,1:T(8,128)(2,1)} %pad_maximum_fusion.4), channel_id=1, source_target_pairs={{0,3},{1,0},{2,1},{3,2},{4,7},{5,4},{6,5},{7,6},{8,11},{9,8},{10,9... | collective-permute-start | bytes 1572872 | tf_op jit(solution)/shard_map/ppermute | solution.py:170
  149.7 21.3 %collective-permute-start.34 = (bf16[2,4,128,256]{3,2,1,0:T(8,128)(2,1)}, bf16[2,4,128,256]{3,2,1,0:T(8,128)(2,1)S(1)}, u32[]{:S(2)}, u32[]{:S(2)}) collective-permute-start(bf16[2,4,128,256]{3,2,1,0:T(8,128)(2,1)} %pad_maximum_fusion.7), channel_id=1, source_target_pairs={{0,3},{1,0},{2,1},{3,2},{4,7},{5,4},{6,5},{7,6},{8,11},{9,8},{10,9... | collective-permute-start | bytes 1572872 | tf_op jit(solution)/shard_map/ppermute | solution.py:170
  151.3 19.7 %collective-permute-start.35 = (bf16[2,4,128,256]{3,2,1,0:T(8,128)(2,1)S(1)}, bf16[2,4,128,256]{3,2,1,0:T(8,128)(2,1)S(1)}, u32[]{:S(2)}, u32[]{:S(2)}) collective-permute-start(bf16[2,4,128,256]{3,2,1,0:T(8,128)(2,1)S(1)} %pad_maximum_fusion.8), channel_id=1, source_target_pairs={{0,1},{1,2},{2,3},{3,0},{4,5},{5,6},{6,7},{7,4},{8,9},{9,10},{10,1... | collective-permute-start | bytes 1572872 | tf_op jit(solution)/shard_map/ppermute | solution.py:170
  152.3 18.8 %collective-permute-start.36 = (bf16[2,4,128,256]{3,2,1,0:T(8,128)(2,1)}, bf16[2,4,128,256]{3,2,1,0:T(8,128)(2,1)S(1)}, u32[]{:S(2)}, u32[]{:S(2)}) collective-permute-start(bf16[2,4,128,256]{3,2,1,0:T(8,128)(2,1)} %pad_maximum_fusion.9), channel_id=1, source_target_pairs={{0,2},{1,3},{2,0},{3,1},{4,6},{5,7},{6,4},{7,5},{8,10},{9,11},{10,... | collective-permute-start | bytes 1572872 | tf_op jit(solution)/shard_map/ppermute | solution.py:170
  154.5 11.2 %collective-permute-start.27 = (bf16[2,128,256]{2,1,0:T(8,128)(2,1)}, bf16[2,128,256]{2,1,0:T(8,128)(2,1)S(1)}, u32[]{:S(2)}, u32[]{:S(2)}) collective-permute-start(bf16[2,128,256]{2,1,0:T(8,128)(2,1)} %get-tuple-element.128), channel_id=1, source_target_pairs={{0,4},{1,5},{2,6},{3,7},{4,8},{5,9},{6,10},{7,11},{8,12},{9,13},{1... | collective-permute-start | bytes 393224 | tf_op jit(solution)/shard_map/ppermute | solution.py:170
  179.5 13.2 %collective-permute-start.40 = (bf16[2,128,256]{2,1,0:T(8,128)(2,1)S(1)}, bf16[2,128,256]{2,1,0:T(8,128)(2,1)S(1)}, u32[]{:S(2)}, u32[]{:S(2)}) collective-permute-start(bf16[2,128,256]{2,1,0:T(8,128)(2,1)S(1)} %fusion.2), channel_id=1, source_target_pairs={{0,32},{16,48},{32,64},{48,80},{64,96},{80,112},{96,0},{112,16},{1... | collective-permute-start | bytes 393224 | tf_op jit(solution)/shard_map/ppermute | solution.py:175
  180.7 12.0 %collective-permute-start.41 = (bf16[2,128,256]{2,1,0:T(8,128)(2,1)S(1)}, bf16[2,128,256]{2,1,0:T(8,128)(2,1)S(1)}, u32[]{:S(2)}, u32[]{:S(2)}) collective-permute-start(bf16[2,128,256]{2,1,0:T(8,128)(2,1)S(1)} %fusion.2), channel_id=1, source_target_pairs={{0,64},{16,80},{32,96},{48,112},{64,0},{80,16},{96,32},{112,48},{1... | collective-permute-start | bytes 393224 | tf_op jit(solution)/shard_map/ppermute | solution.py:175
  181.0 11.7 %collective-permute-start.42 = (bf16[2,128,256]{2,1,0:T(8,128)(2,1)S(1)}, bf16[2,128,256]{2,1,0:T(8,128)(2,1)S(1)}, u32[]{:S(2)}, u32[]{:S(2)}) collective-permute-start(bf16[2,128,256]{2,1,0:T(8,128)(2,1)S(1)} %fusion.2), channel_id=1, source_target_pairs={{0,96},{16,112},{32,0},{48,16},{64,32},{80,48},{96,64},{112,80},{1... | collective-permute-start | bytes 393224 | tf_op jit(solution)/shard_map/ppermute | solution.py:175
  183.2 13.2 %collective-permute-start.32 = (bf16[128,256]{1,0:T(8,128)(2,1)S(1)}, bf16[128,256]{1,0:T(8,128)(2,1)S(1)}, u32[]{:S(2)}, u32[]{:S(2)}) collective-permute-start(bf16[128,256]{1,0:T(8,128)(2,1)S(1)} %fusion.10), channel_id=1, source_target_pairs={{0,16},{16,0},{32,48},{48,32},{64,80},{80,64},{96,112},{112,96},{1... | collective-permute-start | bytes 196616 | tf_op jit(solution)/shard_map/ppermute | solution.py:179
  (33 other events, 176.7 us)
where the time goes:
time: 199 us
  starting transfers between devices  68 us (34%)
  Pallas kernels  65.9 us (33%)
  waiting for transfers between devices  31.1 us (16%)
  local copies, waits for them, and re-layouts  12.8 us (6%)
  between operations  11.4 us (6%)
  other arithmetic  9.58 us (5%)
    pallas_call x4, Pallas kernels, attend(): pl.pallas_call(functools.partial(attend_kernel, 1024, len(extra)), grid_s...  65.9 us
    ppermute x24, starting transfers between devices, move_plane(): return lax.ppermute(item, ('prompt', 'learner'), pairs)  29.2 us
    ppermute x24, waiting for transfers between devices, move_plane(): return lax.ppermute(item, ('prompt', 'learner'), pairs)  23.3 us
    ppermute x8, starting transfers between devices, swap_cores(): return lax.ppermute(item, 'prompt', [(p, p ^ 1) for p in range(8)])  21.8 us
    ppermute x12, starting transfers between devices, move_z(): return lax.ppermute(item, 'prompt', pairs)  17 us
    ppermute x8, waiting for transfers between devices, swap_cores(): return lax.ppermute(item, 'prompt', [(p, p ^ 1) for p in range(8)])  4.89 us
  transfers between devices with their start and end apart: 44, of which 19 were waited for; matrix products, arithmetic and copies ran while one was open for 6% of the time, Pallas kernels for 25%

commit v1 on v0

v1 whole, which is shorter than its diff:
```python
import functools

import jax
import jax.numpy as jnp
from jax import lax
from jax.experimental import pallas as pl
from jax.experimental.pallas import tpu as pltpu
from jax.sharding import PartitionSpec as P

KV_HEADS = 4
HEAD_DIM = 128
COMP_LEN = 256
Q_PER_KV = 5
SHARD = 128
SIDE = 4
PREFIX = SIDE * SIDE * SHARD
TOTAL = PREFIX + COMP_LEN

INV_ROOT = HEAD_DIM**-0.5
EXP2_SCALE = INV_ROOT * 1.4426950408889634
VERY_LOW = -1e30

SHIFTS = (0, 2, 1, 3)

GATHER_GROUPS = ((0,), (1, 2, 3))

NN = (((1,), (0,)), ((), ()))
NT = (((1,), (1,)), ((), ()))


def mxu(left, right, dims):
    return lax.dot_general(left, right, dims, preferred_element_type=jnp.float32)


def attend_kernel(tile, n_alias, at_ref, q_ref, g_ref, ck_ref, cv_ref, *rest):
    kept, crossed = rest[0:4], rest[4]
    att_ref, dq_ref, dck_ref, dcv_ref, keep_ref, send_ref = rest[5 + n_alias : 11 + n_alias]
    keys, vals, acc_k, acc_v = rest[11 + n_alias :]
    core = at_ref[1]
    own = pl.ds(PREFIX, COMP_LEN)
    spans = [pl.ds(t, tile) for t in range(0, PREFIX, tile)] + [own]

    def fill(mine, theirs):
        for a in range(SIDE):
            for b in range(SIDE):
                mine[pl.ds((a * SIDE + b) * SHARD, SHARD), :] = kept[a][0, b]
                theirs[pl.ds((b * SIDE + a) * SHARD, SHARD), :] = crossed[a, b]

    @pl.when(core == 0)
    def _():
        fill(keys, vals)

    @pl.when(core == 1)
    def _():
        fill(vals, keys)

    keys[own, :] = ck_ref[...]
    vals[own, :] = cv_ref[...]
    row_no = lax.broadcasted_iota(jnp.int32, (COMP_LEN, COMP_LEN), 0)
    col_no = lax.broadcasted_iota(jnp.int32, (COMP_LEN, COMP_LEN), 1)
    visible = col_no <= row_no
    live = lax.broadcasted_iota(jnp.int32, (COMP_LEN, 1), 0) < at_ref[0]

    def score(member):
        query = q_ref[:, pl.ds(member * HEAD_DIM, HEAD_DIM)]
        scores = [mxu(query, keys[span, :], NT) for span in spans]
        scores[-1] = jnp.where(visible, scores[-1], VERY_LOW)
        top = functools.reduce(jnp.maximum, [jnp.max(s, axis=1, keepdims=True) for s in scores])
        return query, scores, top * EXP2_SCALE

    def forward(member, scores, top):
        grad = g_ref[:, pl.ds(member * HEAD_DIM, HEAD_DIM)]
        dweights = [mxu(grad, vals[span, :], NT) for span in spans]
        weights = [jnp.exp2(s * EXP2_SCALE - top) for s in scores]
        total = sum(jnp.sum(w, axis=1, keepdims=True) for w in weights)
        weights_bf = [w.astype(jnp.bfloat16) for w in weights]
        numer = sum(mxu(w, vals[span, :], NN) for w, span in zip(weights_bf, spans))
        return grad, dweights, weights, weights_bf, total, numer

    def backward(member, query, grad, dweights, weights, weights_bf, total, numer):
        cols = pl.ds(member * HEAD_DIM, HEAD_DIM)
        inv_total = jnp.where(live, 1.0 / total, 0.0)
        attended = (numer * inv_total).astype(jnp.bfloat16)
        att_ref[:, cols] = attended
        grad_wide = grad.astype(jnp.float32)
        dsum = jnp.sum(attended.astype(jnp.float32) * grad_wide, axis=1, keepdims=True)
        grad_t = (grad_wide * inv_total).astype(jnp.bfloat16).T
        query_t = (query.astype(jnp.float32) * (inv_total * INV_ROOT)).astype(jnp.bfloat16).T
        dq = 0.0
        for span, dweight, w, w_bf in zip(spans, dweights, weights, weights_bf):
            dscore = (w * (dweight - dsum)).astype(jnp.bfloat16)
            dq = dq + mxu(dscore, keys[span, :], NN)
            dk, dv = mxu(query_t, dscore, NN), mxu(grad_t, w_bf, NN)
            if member:
                acc_k[:, span] += dk
                acc_v[:, span] += dv
            else:
                acc_k[:, span] = dk
                acc_v[:, span] = dv
        dq_ref[:, cols] = (dq * (inv_total * INV_ROOT)).astype(jnp.bfloat16)

    ahead = score(0)
    for member in range(Q_PER_KV):
        query, scores, top = ahead
        done = forward(member, scores, top)
        if member + 1 < Q_PER_KV:
            ahead = score(member + 1)
        backward(member, query, *done)

    def empty(mine, theirs):
        for a in range(SIDE):
            for b in range(SIDE):
                cols = pl.ds((a * SIDE + b) * SHARD, SHARD)
                keep_ref[a, b] = mine[:, cols].T.astype(jnp.bfloat16)
                cols = pl.ds((b * SIDE + a) * SHARD, SHARD)
                send_ref[a, b] = theirs[:, cols].T.astype(jnp.bfloat16)

    @pl.when(core == 0)
    def _():
        empty(acc_k, acc_v)

    @pl.when(core == 1)
    def _():
        empty(acc_v, acc_k)

    dck_ref[...] = acc_k[:, own].T.astype(jnp.bfloat16)
    dcv_ref[...] = acc_v[:, own].T.astype(jnp.bfloat16)


def attend(heads, at, rows_in, kept, crossed, in_at, out_at, out_heads, held, grads):
    first = heads[0]
    per_head = pl.BlockSpec(
        (COMP_LEN, Q_PER_KV * HEAD_DIM), lambda h, _: (0, h + first)
    )
    per_kv = pl.BlockSpec((COMP_LEN, HEAD_DIM), lambda h, _: (0, h + first))
    kept_in = pl.BlockSpec((1, SIDE, SHARD, HEAD_DIM), lambda h, _: (0, 0, 0, h + in_at))
    square = (SIDE, SIDE, SHARD, HEAD_DIM)
    crossed_in = pl.BlockSpec(square, lambda h, _: (0, 0, 0, h + in_at))
    square_out = pl.BlockSpec(square, lambda h, _: (0, 0, 0, h + out_at))
    wide = jax.ShapeDtypeStruct((COMP_LEN, KV_HEADS * Q_PER_KV * HEAD_DIM), jnp.bfloat16)
    narrow = jax.ShapeDtypeStruct((COMP_LEN, KV_HEADS * HEAD_DIM), jnp.bfloat16)
    part = jax.ShapeDtypeStruct((SIDE, SIDE, SHARD, out_heads * HEAD_DIM), jnp.bfloat16)
    extra, aliases = [], {}
    base = 1 + 4 + 5
    for out_no, item in enumerate((held or [None] * 4) + (grads or [None] * 2)):
        if item is not None:
            aliases[base + len(extra)] = out_no
            extra.append(item)
    return pl.pallas_call(
        functools.partial(attend_kernel, 512, len(extra)),
        grid_spec=pltpu.PrefetchScalarGridSpec(
            num_scalar_prefetch=1,
            grid=(len(heads),),
            in_specs=[per_head, per_head, per_kv, per_kv]
            + [kept_in] * 4
            + [crossed_in]
            + [pl.BlockSpec(memory_space=pl.ANY)] * len(extra),
            out_specs=[per_head, per_head, per_kv, per_kv] + [square_out] * 2,
            scratch_shapes=[pltpu.VMEM((TOTAL, HEAD_DIM), jnp.bfloat16)] * 2
            + [pltpu.VMEM((HEAD_DIM, TOTAL), jnp.float32)] * 2,
        ),
        out_shape=[wide, wide, narrow, narrow] + [part] * 2,
        input_output_aliases=aliases,
        compiler_params=pltpu.CompilerParams(vmem_limit_bytes=60 * 2**20),
        cost_estimate=pl.CostEstimate(
            flops=len(heads) * 6 * 2 * Q_PER_KV * COMP_LEN * TOTAL * HEAD_DIM,
            bytes_accessed=len(heads) * 5 * 2**20,
            transcendentals=len(heads) * Q_PER_KV * COMP_LEN * TOTAL,
        ),
    )(at, *rows_in, *kept, crossed, *extra)


def move_plane(item, shift, first):
    pairs = []
    for p in range(8):
        along_x = (p % 2 == 0) == first
        for x in range(SIDE):
            for y in range(SIDE):
                to_x = (x + shift) % SIDE if along_x else x
                to_y = y if along_x else (y + shift) % SIDE
                pairs.append(((p * SIDE + x) * SIDE + y, (p * SIDE + to_x) * SIDE + to_y))
    return lax.ppermute(item, ("prompt", "learner"), pairs)


def move_z(item, shift):
    pairs = [(z * 2 + c, ((z + shift) % 4) * 2 + c) for z in range(4) for c in range(2)]
    return lax.ppermute(item, "prompt", pairs)


def swap_cores(item):
    return lax.ppermute(item, "prompt", [(p, p ^ 1) for p in range(8)])


def spread(item, first):
    return [move_plane(item, s, first) if s else item for s in SHIFTS]


class Place:
    def __init__(self, source_of):
        here = lax.axis_index("prompt")
        spot = jnp.arange(source_of.shape[0], dtype=jnp.int32)
        mine = jnp.sum(jnp.where(spot == here, source_of, 0))
        other = jnp.sum(jnp.where(spot == (here ^ 1), source_of, 0))
        self.first = (here & 1) == 0
        self.steps = [((here >> 1) - (who >> 1)) & 3 for who in (mine, other)]
        self.same = [((who ^ here) & 1) == 0 for who in (mine, other)]

    def of(self, column, which):
        step = self.steps[which]
        low = jnp.where((step & 1) == 0, column[0], column[1])
        high = jnp.where((step & 1) == 0, column[2], column[3])
        return jnp.where(step < 2, low, high)


def tie(*trees):
    return lax.optimization_barrier(trees)


def bring_column(item):
    far, near, back = [move_z(item, s) for s in (2, 1, 3)]
    return [item, near, far, back]


def choose(column, place):
    mine, other = place.of(column, 0), place.of(column, 1)
    send = jnp.stack([jnp.where(place.first, p[1], p[0]) for p in (other, mine)])
    keep = jnp.stack([jnp.where(place.first, p[0], p[1]) for p in (mine, other)])
    return keep, send


def join(keep, got, place):
    return jnp.stack([jnp.where(place.same[i], keep[i], got[i]) for i in range(2)])


def bring_row(pair):
    return jnp.stack(spread(pair, True), axis=1)


def cross(kept):
    return swap_cores(jnp.stack([part[1] for part in kept]))


def return_row(keep, got):
    return [jnp.stack([keep[a], got[a]]) for a in range(SIDE)]


def move_back(items, first):
    return [move_plane(item, -s, first) if s else item for item, s in zip(items, SHIFTS)]


def add_up(items):
    return sum(item.astype(jnp.float32) for item in items).astype(jnp.bfloat16)


def give_back(row, place):
    pair = add_up(move_back([row[:, b] for b in range(SIDE)], True))
    column = bring_column(pair)

    def pick(which, same):
        both = place.of(column, which)
        return jnp.where(same, both[0], both[1])

    kept = pick(0, place.same[0])
    crossed = swap_cores(pick(1, place.same[1]))
    dk = jnp.where(place.first, kept, crossed)
    dv = jnp.where(place.first, crossed, kept)
    return dk.astype(jnp.float32)[None], dv.astype(jnp.float32)[None]


def body(prefix_k, prefix_v, queries, comp_k, comp_v, out_grad, lengths, owner_map):
    n_learn = lax.axis_size("learner")
    here = lax.axis_index("prompt")
    me = here * n_learn + lax.axis_index("learner")
    groups = jnp.arange(owner_map.shape[0], dtype=jnp.int32)
    holder = jnp.sum(jnp.where(owner_map[None, :] == groups[:, None], groups[None, :], 0), axis=1)
    my_len = lax.dynamic_index_in_dim(lengths, me, 0, keepdims=False)
    at = jnp.stack([my_len, here % 2])
    rows_in = [queries[0], out_grad[0], comp_k[0], comp_v[0]]

    place = Place(holder)
    keep, send = choose(bring_column(jnp.stack([prefix_k[0], prefix_v[0]])), place)
    row = bring_row(join(keep, swap_cores(send), place))
    rows = [row[..., g[0] * HEAD_DIM : (g[-1] + 1) * HEAD_DIM] for g in GATHER_GROUPS]
    kept = spread(rows[0], False)
    kept, rest_row = tie(kept, rows[1])
    crossed = cross(kept)
    rest_kept = spread(rest_row, False)

    def call(group, kept, crossed, held):
        outs = attend(group, at, rows_in, kept, crossed, 0, 0, len(group), held, None)
        return list(outs[:4]), list(outs[4:])

    held, (keep, send) = call(GATHER_GROUPS[0], kept, crossed, None)
    send, rest_kept = tie(send, rest_kept)
    got = swap_cores(send)
    rest_crossed = cross(rest_kept)
    rest_crossed, got = tie(rest_crossed, got)
    back = move_back(return_row(keep, got), False)
    held, (rest_keep, rest_send) = call(GATHER_GROUPS[1], rest_kept, rest_crossed, held)
    rest_send, back = tie(rest_send, back)
    rest_back = move_back(return_row(rest_keep, swap_cores(rest_send)), False)
    row = jnp.concatenate([add_up(back), add_up(rest_back)], axis=-1)
    grad_prefix_k, grad_prefix_v = give_back(row, Place(owner_map))
    attended, grad_queries, grad_comp_k, grad_comp_v = held
    return (
        attended[None],
        grad_queries[None],
        grad_comp_k[None],
        grad_comp_v[None],
        grad_prefix_k,
        grad_prefix_v,
    )


def solution(mesh):
    by_prompt = P("prompt", "learner", None)
    by_completion = P(("prompt", "learner"), None, None)
    return jax.shard_map(
        body,
        mesh=mesh,
        in_specs=(by_prompt,) * 2 + (by_completion,) * 4 + (P(), P()),
        out_specs=(by_completion,) * 4 + (by_prompt,) * 2,
        check_vma=False,
    )
```

time: 199 us -> 169 us (0.85)
  waiting for transfers between devices: 31.1 us -> 54.9 us
  starting transfers between devices: 68 us -> 45.9 us
  Pallas kernels: 65.9 us -> 48.7 us
  local copies, waits for them, and re-layouts: 12.8 us -> 6.33 us
  between operations: 11.4 us -> 6.27 us
  other arithmetic: 9.58 us -> 6.14 us
    pallas_call x4 -> x2, Pallas kernels: 65.9 us -> 48.7 us  [attend(): pl.pallas_call(functools.partial(attend_kernel, 512, len(extra)), grid_sp...]
    ppermute x24 -> x18, waiting for transfers between devices: 23.3 us -> 35.7 us  [move_plane(): return lax.ppermute(item, ('prompt', 'learner'), pairs)]
    ppermute x8 -> x6, starting transfers between devices: 21.8 us -> 10.6 us  [swap_cores(): return lax.ppermute(item, 'prompt', [(p, p ^ 1) for p in range(8)])]
    ppermute x12 -> x6, waiting for transfers between devices: 2.92 us -> 14.1 us  [move_z(): return lax.ppermute(item, 'prompt', pairs)]
    ppermute x12 -> x6, starting transfers between devices: 17 us -> 10.7 us  [move_z(): return lax.ppermute(item, 'prompt', pairs)]
    ppermute x24 -> x18, starting transfers between devices: 29.2 us -> 24.6 us  [move_plane(): return lax.ppermute(item, ('prompt', 'learner'), pairs)]
    slice x4 -> x0, local copies, waits for them, and re-layouts: 3.34 us -> none  [body(): t[0, :, g[0] * HEAD_DIM:(g[-1] + 1) * HEAD_DIM]]
    another operation x7, other arithmetic: 2.81 us -> 0.38 us  [return_row(): return [jnp.stack([keep[a], got[a]]) for a in range(SIDE)]]
  transfers between devices with their start and end apart: 44 -> 30, of which waited for: 19 -> 20; matrix products, arithmetic and copies ran while one was open for 6% -> 4% of each run, Pallas kernels for 25% -> 29%
where the time goes in v1:
time: 169 us; the launch traced here: 168 us
  waiting for transfers between devices  54.9 us (32%)
  Pallas kernels  48.7 us (29%)
  starting transfers between devices  45.9 us (27%)
  local copies, waits for them, and re-layouts  6.33 us (4%)
  between operations  6.27 us (4%)
  other arithmetic  6.14 us (4%)
    pallas_call x2, Pallas kernels, attend(): pl.pallas_call(functools.partial(attend_kernel, 512, len(extra)), grid_sp...  48.7 us
    ppermute x18, waiting for transfers between devices, move_plane(): return lax.ppermute(item, ('prompt', 'learner'), pairs)  35.7 us
    ppermute x18, starting transfers between devices, move_plane(): return lax.ppermute(item, ('prompt', 'learner'), pairs)  24.6 us
    ppermute x6, waiting for transfers between devices, move_z(): return lax.ppermute(item, 'prompt', pairs)  14.1 us
    ppermute x6, starting transfers between devices, move_z(): return lax.ppermute(item, 'prompt', pairs)  10.7 us
    ppermute x6, starting transfers between devices, swap_cores(): return lax.ppermute(item, 'prompt', [(p, p ^ 1) for p in range(8)])  10.6 us
    ppermute x6, waiting for transfers between devices, swap_cores(): return lax.ppermute(item, 'prompt', [(p, p ^ 1) for p in range(8)])  5.07 us
  transfers between devices with their start and end apart: 30, of which 20 were waited for; matrix products, arithmetic and copies ran while one was open for 4% of the time, Pallas kernels for 29%

profile of v1, /device:TPU:1, one launch (start us, length us, event | category | flops | bytes accessed | tf_op | source)
XLA Modules:
  0.0 168.2 jit_solution(8921967112669341806)
XLA Ops:
  2.5 2.5 %collective-permute-start = (bf16[2,128,512]{2,1,0:T(8,128)(2,1)S(1)}, bf16[2,128,512]{2,1,0:T(8,128)(2,1)S(1)}, u32[]{:S(2)}, u32[]{:S(2)}) collective-permute-start(bf16[2,128,512]{2,1,0:T(8,128)(2,1)S(1)} %constant_dynamic-update-slice_fusion), channel_id=1, source_target_pairs={{0,32},{16,48},{32,64},{48,80},{64,96},{80,112},{96,0},{112,16},{1... | collective-permute-start | bytes 786440 | tf_op jit(solution)/shard_map/ppermute | solution.py:187
  5.0 3.3 %collective-permute-start.1 = (bf16[2,128,512]{2,1,0:T(8,128)(2,1)S(1)}, bf16[2,128,512]{2,1,0:T(8,128)(2,1)S(1)}, u32[]{:S(2)}, u32[]{:S(2)}) collective-permute-start(bf16[2,128,512]{2,1,0:T(8,128)(2,1)S(1)} %constant_dynamic-update-slice_fusion), channel_id=1, source_target_pairs={{0,64},{16,80},{32,96},{48,112},{64,0},{80,16},{96,32},{112,48},{1... | collective-permute-start | bytes 786440 | tf_op jit(solution)/shard_map/ppermute | solution.py:187
  13.2 6.5 %collective-permute-done.1 = bf16[2,128,512]{2,1,0:T(8,128)(2,1)S(1)} collective-permute-done((bf16[2,128,512]{2,1,0:T(8,128)(2,1)S(1)}, bf16[2,128,512]{2,1,0:T(8,128)(2,1)S(1)}, u32[]{:S(2)}, u32[]{:S(2)}) %collective-permute-start.1) | collective-permute-done | bytes 262176 | tf_op jit(solution)/shard_map/ppermute | solution.py:187
  27.3 2.4 %collective-permute-done.5 = bf16[2,128,512]{2,1,0:T(8,128)(2,1)S(1)} collective-permute-done((bf16[2,128,512]{2,1,0:T(8,128)(2,1)S(1)}, bf16[2,128,512]{2,1,0:T(8,128)(2,1)S(1)}, u32[]{:S(2)}, u32[]{:S(2)}) %collective-permute-start.5) | collective-permute-done | bytes 262176 | tf_op jit(solution)/shard_map/ppermute | solution.py:182
  29.7 2.2 %collective-permute-done.6 = bf16[2,128,512]{2,1,0:T(8,128)(2,1)S(1)} collective-permute-done((bf16[2,128,512]{2,1,0:T(8,128)(2,1)S(1)}, bf16[2,128,512]{2,1,0:T(8,128)(2,1)S(1)}, u32[]{:S(2)}, u32[]{:S(2)}) %collective-permute-start.6) | collective-permute-done | bytes 262176 | tf_op jit(solution)/shard_map/ppermute | solution.py:182
  31.8 1.8 %collective-permute-done.4 = bf16[2,128,512]{2,1,0:T(8,128)(2,1)S(1)} collective-permute-done((bf16[2,128,512]{2,1,0:T(8,128)(2,1)S(1)}, bf16[2,128,512]{2,1,0:T(8,128)(2,1)S(1)}, u32[]{:S(2)}, u32[]{:S(2)}) %collective-permute-start.4) | collective-permute-done | bytes 262176 | tf_op jit(solution)/shard_map/ppermute | solution.py:182
  33.7 2.5 %collective-permute-start.7 = (bf16[2,4,128,128]{3,2,1,0:T(8,128)(2,1)S(1)}, bf16[2,4,128,128]{3,2,1,0:T(8,128)(2,1)S(1)}, u32[]{:S(2)}, u32[]{:S(2)}) collective-permute-start(bf16[2,4,128,128]{3,2,1,0:T(8,128)(2,1)S(1)} %pad_maximum_fusion.9.rest_0_), channel_id=1, source_target_pairs={{0,2},{1,3},{2,0},{3,1},{4,6},{5,7},{6,4},{7,5},{8,10},{9,11},{10,... | collective-permute-start | bytes 786440 | tf_op jit(solution)/shard_map/ppermute | solution.py:182
  36.6 2.4 %collective-permute-start.9 = (bf16[2,4,128,128]{3,2,1,0:T(8,128)(2,1)S(1)}, bf16[2,4,128,128]{3,2,1,0:T(8,128)(2,1)S(1)}, u32[]{:S(2)}, u32[]{:S(2)}) collective-permute-start(bf16[2,4,128,128]{3,2,1,0:T(8,128)(2,1)S(1)} %pad_maximum_fusion.9.rest_0_), channel_id=1, source_target_pairs={{0,3},{1,0},{2,1},{3,2},{4,7},{5,4},{6,5},{7,6},{8,11},{9,8},{10,9... | collective-permute-start | bytes 786440 | tf_op jit(solution)/shard_map/ppermute | solution.py:182
  39.0 1.8 %collective-permute-done.7.rest_1_ = bf16[2,4,128,128]{3,2,1,0:T(8,128)(2,1)S(1)} collective-permute-done((bf16[2,4,128,128]{3,2,1,0:T(8,128)(2,1)S(1)}, bf16[2,4,128,128]{3,2,1,0:T(8,128)(2,1)S(1)}, u32[]{:S(2)}, u32[]{:S(2)}) %collective-permute-start.7) | collective-permute-done | bytes 262176 | tf_op jit(solution)/shard_map/ppermute | solution.py:182
  40.8 2.8 %collective-permute-done.8.rest_2_ = bf16[2,4,128,128]{3,2,1,0:T(8,128)(2,1)S(1)} collective-permute-done((bf16[2,4,128,128]{3,2,1,0:T(8,128)(2,1)S(1)}, bf16[2,4,128,128]{3,2,1,0:T(8,128)(2,1)S(1)}, u32[]{:S(2)}, u32[]{:S(2)}) %collective-permute-start.8) | collective-permute-done | bytes 262176 | tf_op jit(solution)/shard_map/ppermute | solution.py:182
  44.6 2.0 %collective-permute-start.10 = (bf16[4,4,128,128]{3,2,1,0:T(8,128)(2,1)S(1)}, bf16[4,4,128,128]{3,2,1,0:T(8,128)(2,1)}, u32[]{:S(2)}, u32[]{:S(2)}) collective-permute-start(bf16[4,4,128,128]{3,2,1,0:T(8,128)(2,1)S(1)} %pad_maximum_fusion.7), channel_id=1, source_target_pairs={{0,16},{16,0},{32,48},{48,32},{64,80},{80,64},{96,112},{112,96},{1... | collective-permute-start | bytes 1572872 | tf_op jit(solution)/shard_map/ppermute | solution.py:191
  52.4 13.9 %shard_map.127 = (bf16[256,2560]{1,0:T(8,128)(2,1)}, bf16[256,2560]{1,0:T(8,128)(2,1)}, bf16[256,512]{1,0:T(8,128)(2,1)}, bf16[256,512]{1,0:T(8,128)(2,1)}, bf16...) custom-call(s32[2]{0:T(128)} %pad_add_fusion.at_ref, bf16[256,2560]{1,0:T(8,128)(2,1)} %bitcast.57, ...), custom_call_target="tpu_custom_call" | custom-call | flops 4529848320 | bytes 5242880 | tf_op jit(solution)/shard_map/pallas_call | solution.py:149
  71.3 3.1 %collective-permute-done.15 = bf16[4,4,128,128]{3,2,1,0:T(8,128)(2,1)S(1)} collective-permute-done((bf16[4,4,128,128]{3,2,1,0:T(8,128)(2,1)S(1)}, bf16[4,4,128,128]{3,2,1,0:T(8,128)(2,1)S(1)}, u32[]{:S(2)}, u32[]{:S(2)}) %collective-permute-start.15) | collective-permute-done | bytes 524320 | tf_op jit(solution)/shard_map/ppermute | solution.py:191
  78.1 34.8 %shard_map.128 = (bf16[256,2560]{1,0:T(8,128)(2,1)}, bf16[256,2560]{1,0:T(8,128)(2,1)}, bf16[256,512]{1,0:T(8,128)(2,1)}, bf16[256,512]{1,0:T(8,128)(2,1)}, bf16...) custom-call(s32[2]{0:T(128)} %pad_add_fusion.at_ref, ...), custom_call_target="tpu_custom_call", output_to_operand_aliasing={{0}: (10, {}), {1}: (11, {}), {2}: (12, {}), {3}: (13, {})} | custom-call | flops 13589544960 | bytes 15728640 | tf_op jit(solution)/shard_map/pallas_call | solution.py:149
  116.2 1.7 %collective-permute-done.19 = bf16[4,4,128,384]{3,2,1,0:T(8,128)(2,1)S(1)} collective-permute-done((bf16[4,4,128,384]{3,2,1,0:T(8,128)(2,1)}, bf16[4,4,128,384]{3,2,1,0:T(8,128)(2,1)S(1)}, u32[]{:S(2)}, u32[]{:S(2)}) %collective-permute-start.19) | collective-permute-done | bytes 1572896 | tf_op jit(solution)/shard_map/ppermute | solution.py:191
  120.0 2.0 %collective-permute-start.21 = (bf16[2,4,128,384]{3,2,1,0:T(8,128)(2,1)S(1)}, bf16[2,4,128,384]{3,2,1,0:T(8,128)(2,1)S(1)}, u32[]{:S(2)}, u32[]{:S(2)}) collective-permute-start(bf16[2,4,128,384]{3,2,1,0:T(8,128)(2,1)S(1)} %pad_maximum_fusion.5), channel_id=1, source_target_pairs={{0,3},{1,0},{2,1},{3,2},{4,7},{5,4},{6,5},{7,6},{8,11},{9,8},{10,9... | collective-permute-start | bytes 2359304 | tf_op jit(solution)/shard_map/ppermute | solution.py:182
  122.3 8.6 %collective-permute-done.20 = bf16[2,4,128,384]{3,2,1,0:T(8,128)(2,1)S(1)} collective-permute-done((bf16[2,4,128,384]{3,2,1,0:T(8,128)(2,1)S(1)}, bf16[2,4,128,384]{3,2,1,0:T(8,128)(2,1)S(1)}, u32[]{:S(2)}, u32[]{:S(2)}) %collective-permute-start.20) | collective-permute-done | bytes 786464 | tf_op jit(solution)/shard_map/ppermute | solution.py:182
  130.9 8.0 %collective-permute-done.21 = bf16[2,4,128,384]{3,2,1,0:T(8,128)(2,1)S(1)} collective-permute-done((bf16[2,4,128,384]{3,2,1,0:T(8,128)(2,1)S(1)}, bf16[2,4,128,384]{3,2,1,0:T(8,128)(2,1)S(1)}, u32[]{:S(2)}, u32[]{:S(2)}) %collective-permute-start.21) | collective-permute-done | bytes 786464 | tf_op jit(solution)/shard_map/ppermute | solution.py:182
  139.9 2.2 %collective-permute-start.23 = (bf16[2,128,512]{2,1,0:T(8,128)(2,1)S(1)}, bf16[2,128,512]{2,1,0:T(8,128)(2,1)S(1)}, u32[]{:S(2)}, u32[]{:S(2)}) collective-permute-start(bf16[2,128,512]{2,1,0:T(8,128)(2,1)S(1)} %get-tuple-element.78), channel_id=1, source_target_pairs={{0,8},{1,9},{2,10},{3,11},{4,12},{5,13},{6,14},{7,15},{8,0},{9,1},... | collective-permute-start | bytes 786440 | tf_op jit(solution)/shard_map/ppermute | solution.py:182
  143.5 3.5 %collective-permute-done.23 = bf16[2,128,512]{2,1,0:T(8,128)(2,1)S(1)} collective-permute-done((bf16[2,128,512]{2,1,0:T(8,128)(2,1)S(1)}, bf16[2,128,512]{2,1,0:T(8,128)(2,1)S(1)}, u32[]{:S(2)}, u32[]{:S(2)}) %collective-permute-start.23) | collective-permute-done | bytes 262176 | tf_op jit(solution)/shard_map/ppermute | solution.py:182
  147.0 1.9 %collective-permute-done.24 = bf16[2,128,512]{2,1,0:T(8,128)(2,1)S(1)} collective-permute-done((bf16[2,128,512]{2,1,0:T(8,128)(2,1)S(1)}, bf16[2,128,512]{2,1,0:T(8,128)(2,1)S(1)}, u32[]{:S(2)}, u32[]{:S(2)}) %collective-permute-start.24) | collective-permute-done | bytes 262176 | tf_op jit(solution)/shard_map/ppermute | solution.py:182
  151.0 2.1 %collective-permute-start.27 = (bf16[2,128,512]{2,1,0:T(8,128)(2,1)S(1)}, bf16[2,128,512]{2,1,0:T(8,128)(2,1)S(1)}, u32[]{:S(2)}, u32[]{:S(2)}) collective-permute-start(bf16[2,128,512]{2,1,0:T(8,128)(2,1)S(1)} %fusion.2), channel_id=1, source_target_pairs={{0,64},{16,80},{32,96},{48,112},{64,0},{80,16},{96,32},{112,48},{1... | collective-permute-start | bytes 786440 | tf_op jit(solution)/shard_map/ppermute | solution.py:187
  156.5 5.3 %collective-permute-done.27 = bf16[2,128,512]{2,1,0:T(8,128)(2,1)S(1)} collective-permute-done((bf16[2,128,512]{2,1,0:T(8,128)(2,1)S(1)}, bf16[2,128,512]{2,1,0:T(8,128)(2,1)S(1)}, u32[]{:S(2)}, u32[]{:S(2)}) %collective-permute-start.27) | collective-permute-done | bytes 262176 | tf_op jit(solution)/shard_map/ppermute | solution.py:187
  163.1 3.3 %collective-permute-start.29 = (bf16[128,512]{1,0:T(8,128)(2,1)S(1)}, bf16[128,512]{1,0:T(8,128)(2,1)S(1)}, u32[]{:S(2)}, u32[]{:S(2)}) collective-permute-start(bf16[128,512]{1,0:T(8,128)(2,1)S(1)} %fusion.10), channel_id=1, source_target_pairs={{0,16},{16,0},{32,48},{48,32},{64,80},{80,64},{96,112},{112,96},{1... | collective-permute-start | bytes 393224 | tf_op jit(solution)/shard_map/ppermute | solution.py:191
  (102 shorter events, 41.3 us)
Async XLA Ops:
  2.5 10.7 %collective-permute-start = (bf16[2,128,512]{2,1,0:T(8,128)(2,1)S(1)}, bf16[2,128,512]{2,1,0:T(8,128)(2,1)S(1)}, u32[]{:S(2)}, u32[]{:S(2)}) collective-permute-start(bf16[2,128,512]{2,1,0:T(8,128)(2,1)S(1)} %constant_dynamic-update-slice_fusion), channel_id=1, source_target_pairs={{0,32},{16,48},{32,64},{48,80},{64,96},{80,112},{96,0},{112,16},{1... | collective-permute-start | bytes 786440 | tf_op jit(solution)/shard_map/ppermute | solution.py:187
  5.0 14.6 %collective-permute-start.1 = (bf16[2,128,512]{2,1,0:T(8,128)(2,1)S(1)}, bf16[2,128,512]{2,1,0:T(8,128)(2,1)S(1)}, u32[]{:S(2)}, u32[]{:S(2)}) collective-permute-start(bf16[2,128,512]{2,1,0:T(8,128)(2,1)S(1)} %constant_dynamic-update-slice_fusion), channel_id=1, source_target_pairs={{0,64},{16,80},{32,96},{48,112},{64,0},{80,16},{96,32},{112,48},{1... | collective-permute-start | bytes 786440 | tf_op jit(solution)/shard_map/ppermute | solution.py:187
  8.3 11.3 %collective-permute-start.2 = (bf16[2,128,512]{2,1,0:T(8,128)(2,1)S(1)}, bf16[2,128,512]{2,1,0:T(8,128)(2,1)S(1)}, u32[]{:S(2)}, u32[]{:S(2)}) collective-permute-start(bf16[2,128,512]{2,1,0:T(8,128)(2,1)S(1)} %constant_dynamic-update-slice_fusion), channel_id=1, source_target_pairs={{0,96},{16,112},{32,0},{48,16},{64,32},{80,48},{96,64},{112,80},{1... | collective-permute-start | bytes 786440 | tf_op jit(solution)/shard_map/ppermute | solution.py:187
  22.8 6.9 %collective-permute-start.5 = (bf16[2,128,512]{2,1,0:T(8,128)(2,1)S(1)}, bf16[2,128,512]{2,1,0:T(8,128)(2,1)S(1)}, u32[]{:S(2)}, u32[]{:S(2)}) collective-permute-start(bf16[2,128,512]{2,1,0:T(8,128)(2,1)S(1)} %get-tuple-element.94), channel_id=1, source_target_pairs={{0,4},{1,5},{2,6},{3,7},{4,8},{5,9},{6,10},{7,11},{8,12},{9,13},{1... | collective-permute-start | bytes 786440 | tf_op jit(solution)/shard_map/ppermute | solution.py:182
  24.2 7.6 %collective-permute-start.6 = (bf16[2,128,512]{2,1,0:T(8,128)(2,1)S(1)}, bf16[2,128,512]{2,1,0:T(8,128)(2,1)S(1)}, u32[]{:S(2)}, u32[]{:S(2)}) collective-permute-start(bf16[2,128,512]{2,1,0:T(8,128)(2,1)S(1)} %get-tuple-element.94), channel_id=1, source_target_pairs={{0,12},{1,13},{2,14},{3,15},{4,0},{5,1},{6,2},{7,3},{8,4},{9,5},{1... | collective-permute-start | bytes 786440 | tf_op jit(solution)/shard_map/ppermute | solution.py:182
  25.7 8.0 %collective-permute-start.4 = (bf16[2,128,512]{2,1,0:T(8,128)(2,1)S(1)}, bf16[2,128,512]{2,1,0:T(8,128)(2,1)S(1)}, u32[]{:S(2)}, u32[]{:S(2)}) collective-permute-start(bf16[2,128,512]{2,1,0:T(8,128)(2,1)S(1)} %get-tuple-element.94), channel_id=1, source_target_pairs={{0,8},{1,9},{2,10},{3,11},{4,12},{5,13},{6,14},{7,15},{8,0},{9,1},... | collective-permute-start | bytes 786440 | tf_op jit(solution)/shard_map/ppermute | solution.py:182
  33.7 7.1 %collective-permute-start.7 = (bf16[2,4,128,128]{3,2,1,0:T(8,128)(2,1)S(1)}, bf16[2,4,128,128]{3,2,1,0:T(8,128)(2,1)S(1)}, u32[]{:S(2)}, u32[]{:S(2)}) collective-permute-start(bf16[2,4,128,128]{3,2,1,0:T(8,128)(2,1)S(1)} %pad_maximum_fusion.9.rest_0_), channel_id=1, source_target_pairs={{0,2},{1,3},{2,0},{3,1},{4,6},{5,7},{6,4},{7,5},{8,10},{9,11},{10,... | collective-permute-start | bytes 786440 | tf_op jit(solution)/shard_map/ppermute | solution.py:182
  36.3 7.4 %collective-permute-start.8 = (bf16[2,4,128,128]{3,2,1,0:T(8,128)(2,1)S(1)}, bf16[2,4,128,128]{3,2,1,0:T(8,128)(2,1)S(1)}, u32[]{:S(2)}, u32[]{:S(2)}) collective-permute-start(bf16[2,4,128,128]{3,2,1,0:T(8,128)(2,1)S(1)} %pad_maximum_fusion.9.rest_0_), channel_id=1, source_target_pairs={{0,1},{1,2},{2,3},{3,0},{4,5},{5,6},{6,7},{7,4},{8,9},{9,10},{10,1... | collective-permute-start | bytes 786440 | tf_op jit(solution)/shard_map/ppermute | solution.py:182
  36.6 7.1 %collective-permute-start.9 = (bf16[2,4,128,128]{3,2,1,0:T(8,128)(2,1)S(1)}, bf16[2,4,128,128]{3,2,1,0:T(8,128)(2,1)S(1)}, u32[]{:S(2)}, u32[]{:S(2)}) collective-permute-start(bf16[2,4,128,128]{3,2,1,0:T(8,128)(2,1)S(1)} %pad_maximum_fusion.9.rest_0_), channel_id=1, source_target_pairs={{0,3},{1,0},{2,1},{3,2},{4,7},{5,4},{6,5},{7,6},{8,11},{9,8},{10,9... | collective-permute-start | bytes 786440 | tf_op jit(solution)/shard_map/ppermute | solution.py:182
  44.6 7.8 %collective-permute-start.10 = (bf16[4,4,128,128]{3,2,1,0:T(8,128)(2,1)S(1)}, bf16[4,4,128,128]{3,2,1,0:T(8,128)(2,1)}, u32[]{:S(2)}, u32[]{:S(2)}) collective-permute-start(bf16[4,4,128,128]{3,2,1,0:T(8,128)(2,1)S(1)} %pad_maximum_fusion.7), channel_id=1, source_target_pairs={{0,16},{16,0},{32,48},{48,32},{64,80},{80,64},{96,112},{112,96},{1... | collective-permute-start | bytes 1572872 | tf_op jit(solution)/shard_map/ppermute | solution.py:191
  46.6 19.7 %collective-permute-start.11 = (bf16[2,4,128,384]{3,2,1,0:T(8,128)(2,1)S(1)}, bf16[2,4,128,384]{3,2,1,0:T(8,128)(2,1)S(1)}, u32[]{:S(2)}, u32[]{:S(2)}) collective-permute-start(bf16[2,4,128,384]{3,2,1,0:T(8,128)(2,1)S(1)} %pad_maximum_fusion.1.rest_0_), channel_id=1, source_target_pairs={{0,2},{1,3},{2,0},{3,1},{4,6},{5,7},{6,4},{7,5},{8,10},{9,11},{10,... | collective-permute-start | bytes 2359304 | tf_op jit(solution)/shard_map/ppermute | solution.py:182
  47.8 19.8 %collective-permute-start.12 = (bf16[2,4,128,384]{3,2,1,0:T(8,128)(2,1)S(1)}, bf16[2,4,128,384]{3,2,1,0:T(8,128)(2,1)S(1)}, u32[]{:S(2)}, u32[]{:S(2)}) collective-permute-start(bf16[2,4,128,384]{3,2,1,0:T(8,128)(2,1)S(1)} %pad_maximum_fusion.1.rest_0_), channel_id=1, source_target_pairs={{0,1},{1,2},{2,3},{3,0},{4,5},{5,6},{6,7},{7,4},{8,9},{9,10},{10,1... | collective-permute-start | bytes 2359304 | tf_op jit(solution)/shard_map/ppermute | solution.py:182
  49.1 18.5 %collective-permute-start.13 = (bf16[2,4,128,384]{3,2,1,0:T(8,128)(2,1)S(1)}, bf16[2,4,128,384]{3,2,1,0:T(8,128)(2,1)}, u32[]{:S(2)}, u32[]{:S(2)}) collective-permute-start(bf16[2,4,128,384]{3,2,1,0:T(8,128)(2,1)S(1)} %pad_maximum_fusion.1.rest_0_), channel_id=1, source_target_pairs={{0,3},{1,0},{2,1},{3,2},{4,7},{5,4},{6,5},{7,6},{8,11},{9,8},{10,9... | collective-permute-start | bytes 2359304 | tf_op jit(solution)/shard_map/ppermute | solution.py:182
  74.5 38.6 %collective-permute-start.18 = (bf16[2,4,128,128]{3,2,1,0:T(8,128)(2,1)S(1)}, bf16[2,4,128,128]{3,2,1,0:T(8,128)(2,1)S(1)}, u32[]{:S(2)}, u32[]{:S(2)}) collective-permute-start(bf16[2,4,128,128]{3,2,1,0:T(8,128)(2,1)S(1)} %pad_maximum_fusion.15), channel_id=1, source_target_pairs={{0,1},{1,2},{2,3},{3,0},{4,5},{5,6},{6,7},{7,4},{8,9},{9,10},{10,1... | collective-permute-start | bytes 786440 | tf_op jit(solution)/shard_map/ppermute | solution.py:182
  75.9 37.1 %collective-permute-start.17 = (bf16[2,4,128,128]{3,2,1,0:T(8,128)(2,1)S(1)}, bf16[2,4,128,128]{3,2,1,0:T(8,128)(2,1)S(1)}, u32[]{:S(2)}, u32[]{:S(2)}) collective-permute-start(bf16[2,4,128,128]{3,2,1,0:T(8,128)(2,1)S(1)} %pad_maximum_fusion.14), channel_id=1, source_target_pairs={{0,3},{1,0},{2,1},{3,2},{4,7},{5,4},{6,5},{7,6},{8,11},{9,8},{10,9... | collective-permute-start | bytes 786440 | tf_op jit(solution)/shard_map/ppermute | solution.py:182
  77.6 35.5 %collective-permute-start.16 = (bf16[2,4,128,128]{3,2,1,0:T(8,128)(2,1)S(1)}, bf16[2,4,128,128]{3,2,1,0:T(8,128)(2,1)S(1)}, u32[]{:S(2)}, u32[]{:S(2)}) collective-permute-start(bf16[2,4,128,128]{3,2,1,0:T(8,128)(2,1)S(1)} %pad_maximum_fusion.13), channel_id=1, source_target_pairs={{0,2},{1,3},{2,0},{3,1},{4,6},{5,7},{6,4},{7,5},{8,10},{9,11},{10,... | collective-permute-start | bytes 786440 | tf_op jit(solution)/shard_map/ppermute | solution.py:182
  118.2 12.8 %collective-permute-start.20 = (bf16[2,4,128,384]{3,2,1,0:T(8,128)(2,1)S(1)}, bf16[2,4,128,384]{3,2,1,0:T(8,128)(2,1)S(1)}, u32[]{:S(2)}, u32[]{:S(2)}) collective-permute-start(bf16[2,4,128,384]{3,2,1,0:T(8,128)(2,1)S(1)} %pad_maximum_fusion.4), channel_id=1, source_target_pairs={{0,2},{1,3},{2,0},{3,1},{4,6},{5,7},{6,4},{7,5},{8,10},{9,11},{10,... | collective-permute-start | bytes 2359304 | tf_op jit(solution)/shard_map/ppermute | solution.py:182
  120.0 19.0 %collective-permute-start.21 = (bf16[2,4,128,384]{3,2,1,0:T(8,128)(2,1)S(1)}, bf16[2,4,128,384]{3,2,1,0:T(8,128)(2,1)S(1)}, u32[]{:S(2)}, u32[]{:S(2)}) collective-permute-start(bf16[2,4,128,384]{3,2,1,0:T(8,128)(2,1)S(1)} %pad_maximum_fusion.5), channel_id=1, source_target_pairs={{0,3},{1,0},{2,1},{3,2},{4,7},{5,4},{6,5},{7,6},{8,11},{9,8},{10,9... | collective-permute-start | bytes 2359304 | tf_op jit(solution)/shard_map/ppermute | solution.py:182
  122.1 17.3 %collective-permute-start.22 = (bf16[2,4,128,384]{3,2,1,0:T(8,128)(2,1)S(1)}, bf16[2,4,128,384]{3,2,1,0:T(8,128)(2,1)S(1)}, u32[]{:S(2)}, u32[]{:S(2)}) collective-permute-start(bf16[2,4,128,384]{3,2,1,0:T(8,128)(2,1)S(1)} %pad_maximum_fusion.6), channel_id=1, source_target_pairs={{0,1},{1,2},{2,3},{3,0},{4,5},{5,6},{6,7},{7,4},{8,9},{9,10},{10,1... | collective-permute-start | bytes 2359304 | tf_op jit(solution)/shard_map/ppermute | solution.py:182
  139.9 7.1 %collective-permute-start.23 = (bf16[2,128,512]{2,1,0:T(8,128)(2,1)S(1)}, bf16[2,128,512]{2,1,0:T(8,128)(2,1)S(1)}, u32[]{:S(2)}, u32[]{:S(2)}) collective-permute-start(bf16[2,128,512]{2,1,0:T(8,128)(2,1)S(1)} %get-tuple-element.78), channel_id=1, source_target_pairs={{0,8},{1,9},{2,10},{3,11},{4,12},{5,13},{6,14},{7,15},{8,0},{9,1},... | collective-permute-start | bytes 786440 | tf_op jit(solution)/shard_map/ppermute | solution.py:182
  142.0 6.8 %collective-permute-start.24 = (bf16[2,128,512]{2,1,0:T(8,128)(2,1)S(1)}, bf16[2,128,512]{2,1,0:T(8,128)(2,1)S(1)}, u32[]{:S(2)}, u32[]{:S(2)}) collective-permute-start(bf16[2,128,512]{2,1,0:T(8,128)(2,1)S(1)} %get-tuple-element.80), channel_id=1, source_target_pairs={{0,12},{1,13},{2,14},{3,15},{4,0},{5,1},{6,2},{7,3},{8,4},{9,5},{1... | collective-permute-start | bytes 786440 | tf_op jit(solution)/shard_map/ppermute | solution.py:182
  143.2 6.7 %collective-permute-start.25 = (bf16[2,128,512]{2,1,0:T(8,128)(2,1)S(1)}, bf16[2,128,512]{2,1,0:T(8,128)(2,1)S(1)}, u32[]{:S(2)}, u32[]{:S(2)}) collective-permute-start(bf16[2,128,512]{2,1,0:T(8,128)(2,1)S(1)} %get-tuple-element.79), channel_id=1, source_target_pairs={{0,4},{1,5},{2,6},{3,7},{4,8},{5,9},{6,10},{7,11},{8,12},{9,13},{1... | collective-permute-start | bytes 786440 | tf_op jit(solution)/shard_map/ppermute | solution.py:182
  151.0 10.8 %collective-permute-start.27 = (bf16[2,128,512]{2,1,0:T(8,128)(2,1)S(1)}, bf16[2,128,512]{2,1,0:T(8,128)(2,1)S(1)}, u32[]{:S(2)}, u32[]{:S(2)}) collective-permute-start(bf16[2,128,512]{2,1,0:T(8,128)(2,1)S(1)} %fusion.2), channel_id=1, source_target_pairs={{0,64},{16,80},{32,96},{48,112},{64,0},{80,16},{96,32},{112,48},{1... | collective-permute-start | bytes 786440 | tf_op jit(solution)/shard_map/ppermute | solution.py:187
  153.2 9.8 %collective-permute-start.28 = (bf16[2,128,512]{2,1,0:T(8,128)(2,1)S(1)}, bf16[2,128,512]{2,1,0:T(8,128)(2,1)S(1)}, u32[]{:S(2)}, u32[]{:S(2)}) collective-permute-start(bf16[2,128,512]{2,1,0:T(8,128)(2,1)S(1)} %fusion.2), channel_id=1, source_target_pairs={{0,96},{16,112},{32,0},{48,16},{64,32},{80,48},{96,64},{112,80},{1... | collective-permute-start | bytes 786440 | tf_op jit(solution)/shard_map/ppermute | solution.py:187
  (17 other events, 108.4 us)

commit v2 on v1

--- a/solution.py
+++ b/solution.py
@@ -22,7 +22,7 @@
 
 SHIFTS = (0, 2, 1, 3)
 
-GATHER_GROUPS = ((0,), (1, 2, 3))
+GATHER_GROUPS = ((0, 1), (2, 3))
 
 NN = (((1,), (0,)), ((), ()))
 NT = (((1,), (1,)), ((), ()))
@@ -32,11 +32,13 @@
     return lax.dot_general(left, right, dims, preferred_element_type=jnp.float32)
 
 
-def attend_kernel(tile, n_alias, at_ref, q_ref, g_ref, ck_ref, cv_ref, *rest):
+def attend_kernel(tile, n_alias, len_ref, q_ref, g_ref, ck_ref, cv_ref, *rest):
     kept, crossed = rest[0:4], rest[4]
     att_ref, dq_ref, dck_ref, dcv_ref, keep_ref, send_ref = rest[5 + n_alias : 11 + n_alias]
     keys, vals, acc_k, acc_v = rest[11 + n_alias :]
-    core = at_ref[1]
+    here = lax.axis_index("prompt")
+    core = here & 1
+    length = len_ref[here * lax.axis_size("learner") + lax.axis_index("learner")]
     own = pl.ds(PREFIX, COMP_LEN)
     spans = [pl.ds(t, tile) for t in range(0, PREFIX, tile)] + [own]
 
@@ -59,23 +61,21 @@
     row_no = lax.broadcasted_iota(jnp.int32, (COMP_LEN, COMP_LEN), 0)
     col_no = lax.broadcasted_iota(jnp.int32, (COMP_LEN, COMP_LEN), 1)
     visible = col_no <= row_no
-    live = lax.broadcasted_iota(jnp.int32, (COMP_LEN, 1), 0) < at_ref[0]
-
-    def score(member):
+    live = lax.broadcasted_iota(jnp.int32, (COMP_LEN, 1), 0) < length
+
+    def forward(member):
         query = q_ref[:, pl.ds(member * HEAD_DIM, HEAD_DIM)]
         scores = [mxu(query, keys[span, :], NT) for span in spans]
         scores[-1] = jnp.where(visible, scores[-1], VERY_LOW)
         top = functools.reduce(jnp.maximum, [jnp.max(s, axis=1, keepdims=True) for s in scores])
-        return query, scores, top * EXP2_SCALE
-
-    def forward(member, scores, top):
+        top = top * EXP2_SCALE
         grad = g_ref[:, pl.ds(member * HEAD_DIM, HEAD_DIM)]
         dweights = [mxu(grad, vals[span, :], NT) for span in spans]
         weights = [jnp.exp2(s * EXP2_SCALE - top) for s in scores]
         total = sum(jnp.sum(w, axis=1, keepdims=True) for w in weights)
         weights_bf = [w.astype(jnp.bfloat16) for w in weights]
         numer = sum(mxu(w, vals[span, :], NN) for w, span in zip(weights_bf, spans))
-        return grad, dweights, weights, weights_bf, total, numer
+        return query, grad, dweights, weights, weights_bf, total, numer
 
     def backward(member, query, grad, dweights, weights, weights_bf, total, numer):
         cols = pl.ds(member * HEAD_DIM, HEAD_DIM)
@@ -99,13 +99,11 @@
                 acc_v[:, span] = dv
         dq_ref[:, cols] = (dq * (inv_total * INV_ROOT)).astype(jnp.bfloat16)
 
-    ahead = score(0)
+    done = forward(0)
     for member in range(Q_PER_KV):
-        query, scores, top = ahead
-        done = forward(member, scores, top)
-        if member + 1 < Q_PER_KV:
-            ahead = score(member + 1)
-        backward(member, query, *done)
+        ahead = forward(member + 1) if member + 1 < Q_PER_KV else None
+        backward(member, *done)
+        done = ahead
 
     def empty(mine, theirs):
         for a in range(SIDE):
@@ -127,7 +125,7 @@
     dcv_ref[...] = acc_v[:, own].T.astype(jnp.bfloat16)
 
 
-def attend(heads, at, rows_in, kept, crossed, in_at, out_at, out_heads, held, grads):
+def attend(heads, lengths, rows_in, kept, crossed, in_at, out_at, out_heads, held, grads):
     first = heads[0]
     per_head = pl.BlockSpec(
         (COMP_LEN, Q_PER_KV * HEAD_DIM), lambda h, _: (0, h + first)
@@ -167,7 +165,7 @@
             bytes_accessed=len(heads) * 5 * 2**20,
             transcendentals=len(heads) * Q_PER_KV * COMP_LEN * TOTAL,
         ),
-    )(at, *rows_in, *kept, crossed, *extra)
+    )(lengths, *rows_in, *kept, crossed, *extra)
 
 
 def move_plane(item, shift, first):
@@ -268,17 +266,13 @@
 
 
 def body(prefix_k, prefix_v, queries, comp_k, comp_v, out_grad, lengths, owner_map):
-    n_learn = lax.axis_size("learner")
-    here = lax.axis_index("prompt")
-    me = here * n_learn + lax.axis_index("learner")
     groups = jnp.arange(owner_map.shape[0], dtype=jnp.int32)
     holder = jnp.sum(jnp.where(owner_map[None, :] == groups[:, None], groups[None, :], 0), axis=1)
-    my_len = lax.dynamic_index_in_dim(lengths, me, 0, keepdims=False)
-    at = jnp.stack([my_len, here % 2])
     rows_in = [queries[0], out_grad[0], comp_k[0], comp_v[0]]
 
     place = Place(holder)
-    keep, send = choose(bring_column(jnp.stack([prefix_k[0], prefix_v[0]])), place)
+    is_key = lax.broadcasted_iota(jnp.int32, (2, 1, 1), 0) == 0
+    keep, send = choose(bring_column(jnp.where(is_key, prefix_k, prefix_v)), place)
     row = bring_row(join(keep, swap_cores(send), place))
     rows = [row[..., g[0] * HEAD_DIM : (g[-1] + 1) * HEAD_DIM] for g in GATHER_GROUPS]
     kept = spread(rows[0], False)
@@ -287,14 +281,15 @@
     rest_kept = spread(rest_row, False)
 
     def call(group, kept, crossed, held):
-        outs = attend(group, at, rows_in, kept, crossed, 0, 0, len(group), held, None)
+        outs = attend(group, lengths, rows_in, kept, crossed, 0, 0, len(group), held, None)
         return list(outs[:4]), list(outs[4:])
 
     held, (keep, send) = call(GATHER_GROUPS[0], kept, crossed, None)
     send, rest_kept = tie(send, rest_kept)
     got = swap_cores(send)
-    rest_crossed = cross(rest_kept)
-    rest_crossed, got = tie(rest_crossed, got)
+    handed = jnp.stack([part[1] for part in rest_kept])
+    handed, got = tie(handed, got)
+    rest_crossed = swap_cores(handed)
     back = move_back(return_row(keep, got), False)
     held, (rest_keep, rest_send) = call(GATHER_GROUPS[1], rest_kept, rest_crossed, held)
     rest_send, back = tie(rest_send, back)

time: 169 us -> 162 us (0.959)
  waiting for transfers between devices: 54.9 us -> 51.5 us
  local copies, waits for them, and re-layouts: 6.33 us -> 4.43 us
    ppermute x18, waiting for transfers between devices: 35.7 us -> 33.3 us  [move_plane(): return lax.ppermute(item, ('prompt', 'learner'), pairs)]
  transfers between devices with their start and end apart: 30 -> 30, of which waited for: 20 -> 19; matrix products, arithmetic and copies ran while one was open for 4% -> 3% of each run, Pallas kernels for 29% -> 29%
where the time goes in v2:
time: 162 us
  waiting for transfers between devices  51.5 us (32%)
  Pallas kernels  47.2 us (29%)
  starting transfers between devices  45.5 us (28%)
  other arithmetic  6.82 us (4%)
  between operations  6.29 us (4%)
  local copies, waits for them, and re-layouts  4.43 us (3%)
    pallas_call x2, Pallas kernels, attend(): pl.pallas_call(functools.partial(attend_kernel, 512, len(extra)), grid_sp...  47.2 us
    ppermute x18, waiting for transfers between devices, move_plane(): return lax.ppermute(item, ('prompt', 'learner'), pairs)  33.3 us
    ppermute x18, starting transfers between devices, move_plane(): return lax.ppermute(item, ('prompt', 'learner'), pairs)  25.6 us
    ppermute x6, waiting for transfers between devices, move_z(): return lax.ppermute(item, 'prompt', pairs)  14.2 us
    ppermute x6, starting transfers between devices, move_z(): return lax.ppermute(item, 'prompt', pairs)  10.7 us
    ppermute x6, starting transfers between devices, swap_cores(): return lax.ppermute(item, 'prompt', [(p, p ^ 1) for p in range(8)])  9.2 us
    ppermute x6, waiting for transfers between devices, swap_cores(): return lax.ppermute(item, 'prompt', [(p, p ^ 1) for p in range(8)])  3.96 us
  transfers between devices with their start and end apart: 30, of which 19 were waited for; matrix products, arithmetic and copies ran while one was open for 3% of the time, Pallas kernels for 29%

profile of v2, /device:TPU:1, one launch (start us, length us, event | category | flops | bytes accessed | tf_op | source)
XLA Modules:
  0.0 161.8 jit_solution(325953918604980629)
XLA Ops:
  1.7 2.5 %collective-permute-start = (bf16[2,128,512]{2,1,0:T(8,128)(2,1)S(1)}, bf16[2,128,512]{2,1,0:T(8,128)(2,1)S(1)}, u32[]{:S(2)}, u32[]{:S(2)}) collective-permute-start(bf16[2,128,512]{2,1,0:T(8,128)(2,1)S(1)} %broadcast_select_fusion), channel_id=1, source_target_pairs={{0,32},{16,48},{32,64},{48,80},{64,96},{80,112},{96,0},{112,16},{1... | collective-permute-start | bytes 786440 | tf_op jit(solution)/shard_map/ppermute | solution.py:185
  4.2 3.3 %collective-permute-start.1 = (bf16[2,128,512]{2,1,0:T(8,128)(2,1)S(1)}, bf16[2,128,512]{2,1,0:T(8,128)(2,1)S(1)}, u32[]{:S(2)}, u32[]{:S(2)}) collective-permute-start(bf16[2,128,512]{2,1,0:T(8,128)(2,1)S(1)} %broadcast_select_fusion), channel_id=1, source_target_pairs={{0,64},{16,80},{32,96},{48,112},{64,0},{80,16},{96,32},{112,48},{1... | collective-permute-start | bytes 786440 | tf_op jit(solution)/shard_map/ppermute | solution.py:185
  12.4 6.5 %collective-permute-done.1 = bf16[2,128,512]{2,1,0:T(8,128)(2,1)S(1)} collective-permute-done((bf16[2,128,512]{2,1,0:T(8,128)(2,1)S(1)}, bf16[2,128,512]{2,1,0:T(8,128)(2,1)S(1)}, u32[]{:S(2)}, u32[]{:S(2)}) %collective-permute-start.1) | collective-permute-done | bytes 262176 | tf_op jit(solution)/shard_map/ppermute | solution.py:185
  20.1 1.6 %collective-permute-start.3 = (bf16[2,128,512]{2,1,0:T(8,128)(2,1)S(1)}, bf16[2,128,512]{2,1,0:T(8,128)(2,1)S(1)}, u32[]{:S(2)}, u32[]{:S(2)}) collective-permute-start(bf16[2,128,512]{2,1,0:T(8,128)(2,1)S(1)} %pad_maximum_fusion.11), channel_id=1, source_target_pairs={{0,16},{16,0},{32,48},{48,32},{64,80},{80,64},{96,112},{112,96},{1... | collective-permute-start | bytes 786440 | tf_op jit(solution)/shard_map/ppermute | solution.py:189
  27.6 2.4 %collective-permute-done.5 = bf16[2,128,512]{2,1,0:T(8,128)(2,1)S(1)} collective-permute-done((bf16[2,128,512]{2,1,0:T(8,128)(2,1)S(1)}, bf16[2,128,512]{2,1,0:T(8,128)(2,1)S(1)}, u32[]{:S(2)}, u32[]{:S(2)}) %collective-permute-start.5) | collective-permute-done | bytes 262176 | tf_op jit(solution)/shard_map/ppermute | solution.py:180
  30.0 2.2 %collective-permute-done.6 = bf16[2,128,512]{2,1,0:T(8,128)(2,1)S(1)} collective-permute-done((bf16[2,128,512]{2,1,0:T(8,128)(2,1)S(1)}, bf16[2,128,512]{2,1,0:T(8,128)(2,1)S(1)}, u32[]{:S(2)}, u32[]{:S(2)}) %collective-permute-start.6) | collective-permute-done | bytes 262176 | tf_op jit(solution)/shard_map/ppermute | solution.py:180
  32.1 1.8 %collective-permute-done.4 = bf16[2,128,512]{2,1,0:T(8,128)(2,1)S(1)} collective-permute-done((bf16[2,128,512]{2,1,0:T(8,128)(2,1)S(1)}, bf16[2,128,512]{2,1,0:T(8,128)(2,1)S(1)}, u32[]{:S(2)}, u32[]{:S(2)}) %collective-permute-start.4) | collective-permute-done | bytes 262176 | tf_op jit(solution)/shard_map/ppermute | solution.py:180
  34.2 2.5 %collective-permute-start.7 = (bf16[2,4,128,256]{3,2,1,0:T(8,128)(2,1)S(1)}, bf16[2,4,128,256]{3,2,1,0:T(8,128)(2,1)S(1)}, u32[]{:S(2)}, u32[]{:S(2)}) collective-permute-start(bf16[2,4,128,256]{3,2,1,0:T(8,128)(2,1)S(1)} %get-tuple-element.35.rest_0_), channel_id=1, source_target_pairs={{0,2},{1,3},{2,0},{3,1},{4,6},{5,7},{6,4},{7,5},{8,10},{9,11},{10,... | collective-permute-start | bytes 1572872 | tf_op jit(solution)/shard_map/ppermute | solution.py:180
  37.1 2.4 %collective-permute-start.9 = (bf16[2,4,128,256]{3,2,1,0:T(8,128)(2,1)S(1)}, bf16[2,4,128,256]{3,2,1,0:T(8,128)(2,1)S(1)}, u32[]{:S(2)}, u32[]{:S(2)}) collective-permute-start(bf16[2,4,128,256]{3,2,1,0:T(8,128)(2,1)S(1)} %get-tuple-element.35.rest_0_), channel_id=1, source_target_pairs={{0,3},{1,0},{2,1},{3,2},{4,7},{5,4},{6,5},{7,6},{8,11},{9,8},{10,9... | collective-permute-start | bytes 1572872 | tf_op jit(solution)/shard_map/ppermute | solution.py:180
  39.4 4.7 %collective-permute-done.7.rest_1_ = bf16[2,4,128,256]{3,2,1,0:T(8,128)(2,1)S(1)} collective-permute-done((bf16[2,4,128,256]{3,2,1,0:T(8,128)(2,1)S(1)}, bf16[2,4,128,256]{3,2,1,0:T(8,128)(2,1)S(1)}, u32[]{:S(2)}, u32[]{:S(2)}) %collective-permute-start.7) | collective-permute-done | bytes 524320 | tf_op jit(solution)/shard_map/ppermute | solution.py:180
  44.2 5.6 %collective-permute-done.8.rest_2_ = bf16[2,4,128,256]{3,2,1,0:T(8,128)(2,1)S(1)} collective-permute-done((bf16[2,4,128,256]{3,2,1,0:T(8,128)(2,1)S(1)}, bf16[2,4,128,256]{3,2,1,0:T(8,128)(2,1)S(1)}, u32[]{:S(2)}, u32[]{:S(2)}) %collective-permute-start.8) | collective-permute-done | bytes 524320 | tf_op jit(solution)/shard_map/ppermute | solution.py:180
  50.8 1.8 %collective-permute-start.10 = (bf16[4,4,128,256]{3,2,1,0:T(8,128)(2,1)S(1)}, bf16[4,4,128,256]{3,2,1,0:T(8,128)(2,1)S(1)}, u32[]{:S(2)}, u32[]{:S(2)}) collective-permute-start(bf16[4,4,128,256]{3,2,1,0:T(8,128)(2,1)S(1)} %pad_maximum_fusion.1), channel_id=1, source_target_pairs={{0,16},{16,0},{32,48},{48,32},{64,80},{80,64},{96,112},{112,96},{1... | collective-permute-start | bytes 3145736 | tf_op jit(solution)/shard_map/ppermute | solution.py:189
  57.5 23.6 %shard_map.127 = (bf16[256,2560]{1,0:T(8,128)(2,1)}, bf16[256,2560]{1,0:T(8,128)(2,1)}, bf16[256,512]{1,0:T(8,128)(2,1)}, bf16[256,512]{1,0:T(8,128)(2,1)}, bf16...) custom-call(s32[128]{0:T(128)} %len_ref.3, bf16[256,2560]{1,0:T(8,128)(2,1)} %bitcast.59, ...), custom_call_target="tpu_custom_call" | custom-call | flops 9059696640 | bytes 10485760 | tf_op jit(solution)/shard_map/pallas_call | solution.py:147
  83.1 2.2 %collective-permute-done.14 = bf16[4,4,128,256]{3,2,1,0:T(8,128)(2,1)S(1)} collective-permute-done((bf16[4,4,128,256]{3,2,1,0:T(8,128)(2,1)}, bf16[4,4,128,256]{3,2,1,0:T(8,128)(2,1)S(1)}, u32[]{:S(2)}, u32[]{:S(2)}) %collective-permute-start.14) | collective-permute-done | bytes 1048608 | tf_op jit(solution)/shard_map/ppermute | solution.py:189
  90.6 23.6 %shard_map.128 = (bf16[256,2560]{1,0:T(8,128)(2,1)}, bf16[256,2560]{1,0:T(8,128)(2,1)}, bf16[256,512]{1,0:T(8,128)(2,1)}, bf16[256,512]{1,0:T(8,128)(2,1)}, bf16...) custom-call(s32[128]{0:T(128)} %len_ref.3, ...), custom_call_target="tpu_custom_call", output_to_operand_aliasing={{0}: (10, {}), {1}: (11, {}), {2}: (12, {}), {3}: (13, {})} | custom-call | flops 9059696640 | bytes 10485760 | tf_op jit(solution)/shard_map/pallas_call | solution.py:147
  117.6 2.5 %collective-permute-start.20 = (bf16[2,4,128,256]{3,2,1,0:T(8,128)(2,1)S(1)}, bf16[2,4,128,256]{3,2,1,0:T(8,128)(2,1)S(1)}, u32[]{:S(2)}, u32[]{:S(2)}) collective-permute-start(bf16[2,4,128,256]{3,2,1,0:T(8,128)(2,1)S(1)} %pad_maximum_fusion.7), channel_id=1, source_target_pairs={{0,2},{1,3},{2,0},{3,1},{4,6},{5,7},{6,4},{7,5},{8,10},{9,11},{10,... | collective-permute-start | bytes 1572872 | tf_op jit(solution)/shard_map/ppermute | solution.py:180
  122.2 5.4 %collective-permute-done.20 = bf16[2,4,128,256]{3,2,1,0:T(8,128)(2,1)S(1)} collective-permute-done((bf16[2,4,128,256]{3,2,1,0:T(8,128)(2,1)S(1)}, bf16[2,4,128,256]{3,2,1,0:T(8,128)(2,1)S(1)}, u32[]{:S(2)}, u32[]{:S(2)}) %collective-permute-start.20) | collective-permute-done | bytes 524320 | tf_op jit(solution)/shard_map/ppermute | solution.py:180
  127.6 5.1 %collective-permute-done.21 = bf16[2,4,128,256]{3,2,1,0:T(8,128)(2,1)S(1)} collective-permute-done((bf16[2,4,128,256]{3,2,1,0:T(8,128)(2,1)S(1)}, bf16[2,4,128,256]{3,2,1,0:T(8,128)(2,1)S(1)}, u32[]{:S(2)}, u32[]{:S(2)}) %collective-permute-start.21) | collective-permute-done | bytes 524320 | tf_op jit(solution)/shard_map/ppermute | solution.py:180
  133.5 2.8 %collective-permute-start.23 = (bf16[2,128,512]{2,1,0:T(8,128)(2,1)S(1)}, bf16[2,128,512]{2,1,0:T(8,128)(2,1)S(1)}, u32[]{:S(2)}, u32[]{:S(2)}) collective-permute-start(bf16[2,128,512]{2,1,0:T(8,128)(2,1)S(1)} %get-tuple-element.70), channel_id=1, source_target_pairs={{0,8},{1,9},{2,10},{3,11},{4,12},{5,13},{6,14},{7,15},{8,0},{9,1},... | collective-permute-start | bytes 786440 | tf_op jit(solution)/shard_map/ppermute | solution.py:180
  137.8 2.8 %collective-permute-done.23 = bf16[2,128,512]{2,1,0:T(8,128)(2,1)S(1)} collective-permute-done((bf16[2,128,512]{2,1,0:T(8,128)(2,1)S(1)}, bf16[2,128,512]{2,1,0:T(8,128)(2,1)S(1)}, u32[]{:S(2)}, u32[]{:S(2)}) %collective-permute-start.23) | collective-permute-done | bytes 262176 | tf_op jit(solution)/shard_map/ppermute | solution.py:180
  140.6 1.9 %collective-permute-done.24 = bf16[2,128,512]{2,1,0:T(8,128)(2,1)S(1)} collective-permute-done((bf16[2,128,512]{2,1,0:T(8,128)(2,1)S(1)}, bf16[2,128,512]{2,1,0:T(8,128)(2,1)S(1)}, u32[]{:S(2)}, u32[]{:S(2)}) %collective-permute-start.24) | collective-permute-done | bytes 262176 | tf_op jit(solution)/shard_map/ppermute | solution.py:180
  144.6 2.1 %collective-permute-start.27 = (bf16[2,128,512]{2,1,0:T(8,128)(2,1)S(1)}, bf16[2,128,512]{2,1,0:T(8,128)(2,1)S(1)}, u32[]{:S(2)}, u32[]{:S(2)}) collective-permute-start(bf16[2,128,512]{2,1,0:T(8,128)(2,1)S(1)} %fusion.2), channel_id=1, source_target_pairs={{0,64},{16,80},{32,96},{48,112},{64,0},{80,16},{96,32},{112,48},{1... | collective-permute-start | bytes 786440 | tf_op jit(solution)/shard_map/ppermute | solution.py:185
  150.1 5.4 %collective-permute-done.27 = bf16[2,128,512]{2,1,0:T(8,128)(2,1)S(1)} collective-permute-done((bf16[2,128,512]{2,1,0:T(8,128)(2,1)S(1)}, bf16[2,128,512]{2,1,0:T(8,128)(2,1)S(1)}, u32[]{:S(2)}, u32[]{:S(2)}) %collective-permute-start.27) | collective-permute-done | bytes 262176 | tf_op jit(solution)/shard_map/ppermute | solution.py:185
  156.7 3.2 %collective-permute-start.29 = (bf16[128,512]{1,0:T(8,128)(2,1)S(1)}, bf16[128,512]{1,0:T(8,128)(2,1)S(1)}, u32[]{:S(2)}, u32[]{:S(2)}) collective-permute-start(bf16[128,512]{1,0:T(8,128)(2,1)S(1)} %fusion.10), channel_id=1, source_target_pairs={{0,16},{16,0},{32,48},{48,32},{64,80},{80,64},{96,112},{112,96},{1... | collective-permute-start | bytes 393224 | tf_op jit(solution)/shard_map/ppermute | solution.py:189
  (100 shorter events, 37.4 us)
Async XLA Ops:
  1.7 10.7 %collective-permute-start = (bf16[2,128,512]{2,1,0:T(8,128)(2,1)S(1)}, bf16[2,128,512]{2,1,0:T(8,128)(2,1)S(1)}, u32[]{:S(2)}, u32[]{:S(2)}) collective-permute-start(bf16[2,128,512]{2,1,0:T(8,128)(2,1)S(1)} %broadcast_select_fusion), channel_id=1, source_target_pairs={{0,32},{16,48},{32,64},{48,80},{64,96},{80,112},{96,0},{112,16},{1... | collective-permute-start | bytes 786440 | tf_op jit(solution)/shard_map/ppermute | solution.py:185
  4.2 14.6 %collective-permute-start.1 = (bf16[2,128,512]{2,1,0:T(8,128)(2,1)S(1)}, bf16[2,128,512]{2,1,0:T(8,128)(2,1)S(1)}, u32[]{:S(2)}, u32[]{:S(2)}) collective-permute-start(bf16[2,128,512]{2,1,0:T(8,128)(2,1)S(1)} %broadcast_select_fusion), channel_id=1, source_target_pairs={{0,64},{16,80},{32,96},{48,112},{64,0},{80,16},{96,32},{112,48},{1... | collective-permute-start | bytes 786440 | tf_op jit(solution)/shard_map/ppermute | solution.py:185
  7.5 11.3 %collective-permute-start.2 = (bf16[2,128,512]{2,1,0:T(8,128)(2,1)S(1)}, bf16[2,128,512]{2,1,0:T(8,128)(2,1)S(1)}, u32[]{:S(2)}, u32[]{:S(2)}) collective-permute-start(bf16[2,128,512]{2,1,0:T(8,128)(2,1)S(1)} %broadcast_select_fusion), channel_id=1, source_target_pairs={{0,96},{16,112},{32,0},{48,16},{64,32},{80,48},{96,64},{112,80},{1... | collective-permute-start | bytes 786440 | tf_op jit(solution)/shard_map/ppermute | solution.py:185
  23.1 6.9 %collective-permute-start.5 = (bf16[2,128,512]{2,1,0:T(8,128)(2,1)S(1)}, bf16[2,128,512]{2,1,0:T(8,128)(2,1)S(1)}, u32[]{:S(2)}, u32[]{:S(2)}) collective-permute-start(bf16[2,128,512]{2,1,0:T(8,128)(2,1)S(1)} %get-tuple-element.96), channel_id=1, source_target_pairs={{0,4},{1,5},{2,6},{3,7},{4,8},{5,9},{6,10},{7,11},{8,12},{9,13},{1... | collective-permute-start | bytes 786440 | tf_op jit(solution)/shard_map/ppermute | solution.py:180
  24.5 7.6 %collective-permute-start.6 = (bf16[2,128,512]{2,1,0:T(8,128)(2,1)S(1)}, bf16[2,128,512]{2,1,0:T(8,128)(2,1)S(1)}, u32[]{:S(2)}, u32[]{:S(2)}) collective-permute-start(bf16[2,128,512]{2,1,0:T(8,128)(2,1)S(1)} %get-tuple-element.96), channel_id=1, source_target_pairs={{0,12},{1,13},{2,14},{3,15},{4,0},{5,1},{6,2},{7,3},{8,4},{9,5},{1... | collective-permute-start | bytes 786440 | tf_op jit(solution)/shard_map/ppermute | solution.py:180
  26.0 8.0 %collective-permute-start.4 = (bf16[2,128,512]{2,1,0:T(8,128)(2,1)S(1)}, bf16[2,128,512]{2,1,0:T(8,128)(2,1)S(1)}, u32[]{:S(2)}, u32[]{:S(2)}) collective-permute-start(bf16[2,128,512]{2,1,0:T(8,128)(2,1)S(1)} %get-tuple-element.96), channel_id=1, source_target_pairs={{0,8},{1,9},{2,10},{3,11},{4,12},{5,13},{6,14},{7,15},{8,0},{9,1},... | collective-permute-start | bytes 786440 | tf_op jit(solution)/shard_map/ppermute | solution.py:180
  34.2 10.0 %collective-permute-start.7 = (bf16[2,4,128,256]{3,2,1,0:T(8,128)(2,1)S(1)}, bf16[2,4,128,256]{3,2,1,0:T(8,128)(2,1)S(1)}, u32[]{:S(2)}, u32[]{:S(2)}) collective-permute-start(bf16[2,4,128,256]{3,2,1,0:T(8,128)(2,1)S(1)} %get-tuple-element.35.rest_0_), channel_id=1, source_target_pairs={{0,2},{1,3},{2,0},{3,1},{4,6},{5,7},{6,4},{7,5},{8,10},{9,11},{10,... | collective-permute-start | bytes 1572872 | tf_op jit(solution)/shard_map/ppermute | solution.py:180
  36.8 13.0 %collective-permute-start.8 = (bf16[2,4,128,256]{3,2,1,0:T(8,128)(2,1)S(1)}, bf16[2,4,128,256]{3,2,1,0:T(8,128)(2,1)S(1)}, u32[]{:S(2)}, u32[]{:S(2)}) collective-permute-start(bf16[2,4,128,256]{3,2,1,0:T(8,128)(2,1)S(1)} %get-tuple-element.35.rest_0_), channel_id=1, source_target_pairs={{0,1},{1,2},{2,3},{3,0},{4,5},{5,6},{6,7},{7,4},{8,9},{9,10},{10,1... | collective-permute-start | bytes 1572872 | tf_op jit(solution)/shard_map/ppermute | solution.py:180
  37.1 12.7 %collective-permute-start.9 = (bf16[2,4,128,256]{3,2,1,0:T(8,128)(2,1)S(1)}, bf16[2,4,128,256]{3,2,1,0:T(8,128)(2,1)S(1)}, u32[]{:S(2)}, u32[]{:S(2)}) collective-permute-start(bf16[2,4,128,256]{3,2,1,0:T(8,128)(2,1)S(1)} %get-tuple-element.35.rest_0_), channel_id=1, source_target_pairs={{0,3},{1,0},{2,1},{3,2},{4,7},{5,4},{6,5},{7,6},{8,11},{9,8},{10,9... | collective-permute-start | bytes 1572872 | tf_op jit(solution)/shard_map/ppermute | solution.py:180
  52.6 28.6 %collective-permute-start.11 = (bf16[2,4,128,256]{3,2,1,0:T(8,128)(2,1)S(1)}, bf16[2,4,128,256]{3,2,1,0:T(8,128)(2,1)S(1)}, u32[]{:S(2)}, u32[]{:S(2)}) collective-permute-start(bf16[2,4,128,256]{3,2,1,0:T(8,128)(2,1)S(1)} %get-tuple-element.41.rest_0_), channel_id=1, source_target_pairs={{0,2},{1,3},{2,0},{3,1},{4,6},{5,7},{6,4},{7,5},{8,10},{9,11},{10,... | collective-permute-start | bytes 1572872 | tf_op jit(solution)/shard_map/ppermute | solution.py:180
  53.9 27.3 %collective-permute-start.12 = (bf16[2,4,128,256]{3,2,1,0:T(8,128)(2,1)S(1)}, bf16[2,4,128,256]{3,2,1,0:T(8,128)(2,1)S(1)}, u32[]{:S(2)}, u32[]{:S(2)}) collective-permute-start(bf16[2,4,128,256]{3,2,1,0:T(8,128)(2,1)S(1)} %get-tuple-element.41.rest_0_), channel_id=1, source_target_pairs={{0,1},{1,2},{2,3},{3,0},{4,5},{5,6},{6,7},{7,4},{8,9},{9,10},{10,1... | collective-permute-start | bytes 1572872 | tf_op jit(solution)/shard_map/ppermute | solution.py:180
  55.1 26.0 %collective-permute-start.13 = (bf16[2,4,128,256]{3,2,1,0:T(8,128)(2,1)S(1)}, bf16[2,4,128,256]{3,2,1,0:T(8,128)(2,1)S(1)}, u32[]{:S(2)}, u32[]{:S(2)}) collective-permute-start(bf16[2,4,128,256]{3,2,1,0:T(8,128)(2,1)S(1)} %get-tuple-element.41.rest_0_), channel_id=1, source_target_pairs={{0,3},{1,0},{2,1},{3,2},{4,7},{5,4},{6,5},{7,6},{8,11},{9,8},{10,9... | collective-permute-start | bytes 1572872 | tf_op jit(solution)/shard_map/ppermute | solution.py:180
  85.9 28.4 %collective-permute-start.18 = (bf16[2,4,128,256]{3,2,1,0:T(8,128)(2,1)S(1)}, bf16[2,4,128,256]{3,2,1,0:T(8,128)(2,1)S(1)}, u32[]{:S(2)}, u32[]{:S(2)}) collective-permute-start(bf16[2,4,128,256]{3,2,1,0:T(8,128)(2,1)S(1)} %pad_maximum_fusion.6), channel_id=1, source_target_pairs={{0,1},{1,2},{2,3},{3,0},{4,5},{5,6},{6,7},{7,4},{8,9},{9,10},{10,1... | collective-permute-start | bytes 1572872 | tf_op jit(solution)/shard_map/ppermute | solution.py:180
  87.4 26.9 %collective-permute-start.17 = (bf16[2,4,128,256]{3,2,1,0:T(8,128)(2,1)S(1)}, bf16[2,4,128,256]{3,2,1,0:T(8,128)(2,1)S(1)}, u32[]{:S(2)}, u32[]{:S(2)}) collective-permute-start(bf16[2,4,128,256]{3,2,1,0:T(8,128)(2,1)S(1)} %pad_maximum_fusion.5), channel_id=1, source_target_pairs={{0,3},{1,0},{2,1},{3,2},{4,7},{5,4},{6,5},{7,6},{8,11},{9,8},{10,9... | collective-permute-start | bytes 1572872 | tf_op jit(solution)/shard_map/ppermute | solution.py:180
  89.0 25.3 %collective-permute-start.16 = (bf16[2,4,128,256]{3,2,1,0:T(8,128)(2,1)S(1)}, bf16[2,4,128,256]{3,2,1,0:T(8,128)(2,1)S(1)}, u32[]{:S(2)}, u32[]{:S(2)}) collective-permute-start(bf16[2,4,128,256]{3,2,1,0:T(8,128)(2,1)S(1)} %pad_maximum_fusion.4), channel_id=1, source_target_pairs={{0,2},{1,3},{2,0},{3,1},{4,6},{5,7},{6,4},{7,5},{8,10},{9,11},{10,... | collective-permute-start | bytes 1572872 | tf_op jit(solution)/shard_map/ppermute | solution.py:180
  117.6 10.0 %collective-permute-start.20 = (bf16[2,4,128,256]{3,2,1,0:T(8,128)(2,1)S(1)}, bf16[2,4,128,256]{3,2,1,0:T(8,128)(2,1)S(1)}, u32[]{:S(2)}, u32[]{:S(2)}) collective-permute-start(bf16[2,4,128,256]{3,2,1,0:T(8,128)(2,1)S(1)} %pad_maximum_fusion.7), channel_id=1, source_target_pairs={{0,2},{1,3},{2,0},{3,1},{4,6},{5,7},{6,4},{7,5},{8,10},{9,11},{10,... | collective-permute-start | bytes 1572872 | tf_op jit(solution)/shard_map/ppermute | solution.py:180
  120.2 12.4 %collective-permute-start.21 = (bf16[2,4,128,256]{3,2,1,0:T(8,128)(2,1)S(1)}, bf16[2,4,128,256]{3,2,1,0:T(8,128)(2,1)S(1)}, u32[]{:S(2)}, u32[]{:S(2)}) collective-permute-start(bf16[2,4,128,256]{3,2,1,0:T(8,128)(2,1)S(1)} %pad_maximum_fusion.8), channel_id=1, source_target_pairs={{0,3},{1,0},{2,1},{3,2},{4,7},{5,4},{6,5},{7,6},{8,11},{9,8},{10,9... | collective-permute-start | bytes 1572872 | tf_op jit(solution)/shard_map/ppermute | solution.py:180
  121.3 11.9 %collective-permute-start.22 = (bf16[2,4,128,256]{3,2,1,0:T(8,128)(2,1)S(1)}, bf16[2,4,128,256]{3,2,1,0:T(8,128)(2,1)S(1)}, u32[]{:S(2)}, u32[]{:S(2)}) collective-permute-start(bf16[2,4,128,256]{3,2,1,0:T(8,128)(2,1)S(1)} %pad_maximum_fusion.9), channel_id=1, source_target_pairs={{0,1},{1,2},{2,3},{3,0},{4,5},{5,6},{6,7},{7,4},{8,9},{9,10},{10,1... | collective-permute-start | bytes 1572872 | tf_op jit(solution)/shard_map/ppermute | solution.py:180
  133.5 7.1 %collective-permute-start.23 = (bf16[2,128,512]{2,1,0:T(8,128)(2,1)S(1)}, bf16[2,128,512]{2,1,0:T(8,128)(2,1)S(1)}, u32[]{:S(2)}, u32[]{:S(2)}) collective-permute-start(bf16[2,128,512]{2,1,0:T(8,128)(2,1)S(1)} %get-tuple-element.70), channel_id=1, source_target_pairs={{0,8},{1,9},{2,10},{3,11},{4,12},{5,13},{6,14},{7,15},{8,0},{9,1},... | collective-permute-start | bytes 786440 | tf_op jit(solution)/shard_map/ppermute | solution.py:180
  136.3 6.2 %collective-permute-start.24 = (bf16[2,128,512]{2,1,0:T(8,128)(2,1)S(1)}, bf16[2,128,512]{2,1,0:T(8,128)(2,1)S(1)}, u32[]{:S(2)}, u32[]{:S(2)}) collective-permute-start(bf16[2,128,512]{2,1,0:T(8,128)(2,1)S(1)} %get-tuple-element.72), channel_id=1, source_target_pairs={{0,12},{1,13},{2,14},{3,15},{4,0},{5,1},{6,2},{7,3},{8,4},{9,5},{1... | collective-permute-start | bytes 786440 | tf_op jit(solution)/shard_map/ppermute | solution.py:180
  136.3 7.1 %collective-permute-start.25 = (bf16[2,128,512]{2,1,0:T(8,128)(2,1)S(1)}, bf16[2,128,512]{2,1,0:T(8,128)(2,1)S(1)}, u32[]{:S(2)}, u32[]{:S(2)}) collective-permute-start(bf16[2,128,512]{2,1,0:T(8,128)(2,1)S(1)} %get-tuple-element.71), channel_id=1, source_target_pairs={{0,4},{1,5},{2,6},{3,7},{4,8},{5,9},{6,10},{7,11},{8,12},{9,13},{1... | collective-permute-start | bytes 786440 | tf_op jit(solution)/shard_map/ppermute | solution.py:180
  143.6 6.5 %collective-permute-start.26 = (bf16[2,128,512]{2,1,0:T(8,128)(2,1)S(1)}, bf16[2,128,512]{2,1,0:T(8,128)(2,1)S(1)}, u32[]{:S(2)}, u32[]{:S(2)}) collective-permute-start(bf16[2,128,512]{2,1,0:T(8,128)(2,1)S(1)} %fusion.2), channel_id=1, source_target_pairs={{0,32},{16,48},{32,64},{48,80},{64,96},{80,112},{96,0},{112,16},{1... | collective-permute-start | bytes 786440 | tf_op jit(solution)/shard_map/ppermute | solution.py:185
  144.6 10.9 %collective-permute-start.27 = (bf16[2,128,512]{2,1,0:T(8,128)(2,1)S(1)}, bf16[2,128,512]{2,1,0:T(8,128)(2,1)S(1)}, u32[]{:S(2)}, u32[]{:S(2)}) collective-permute-start(bf16[2,128,512]{2,1,0:T(8,128)(2,1)S(1)} %fusion.2), channel_id=1, source_target_pairs={{0,64},{16,80},{32,96},{48,112},{64,0},{80,16},{96,32},{112,48},{1... | collective-permute-start | bytes 786440 | tf_op jit(solution)/shard_map/ppermute | solution.py:185
  146.7 9.9 %collective-permute-start.28 = (bf16[2,128,512]{2,1,0:T(8,128)(2,1)S(1)}, bf16[2,128,512]{2,1,0:T(8,128)(2,1)S(1)}, u32[]{:S(2)}, u32[]{:S(2)}) collective-permute-start(bf16[2,128,512]{2,1,0:T(8,128)(2,1)S(1)} %fusion.2), channel_id=1, source_target_pairs={{0,96},{16,112},{32,0},{48,16},{64,32},{80,48},{96,64},{112,80},{1... | collective-permute-start | bytes 786440 | tf_op jit(solution)/shard_map/ppermute | solution.py:185
  (17 other events, 107.1 us)

commit v3 on v2

--- a/solution.py
+++ b/solution.py
@@ -40,13 +40,14 @@
     core = here & 1
     length = len_ref[here * lax.axis_size("learner") + lax.axis_index("learner")]
     own = pl.ds(PREFIX, COMP_LEN)
+    width = pl.ds(0, HEAD_DIM)
     spans = [pl.ds(t, tile) for t in range(0, PREFIX, tile)] + [own]
 
     def fill(mine, theirs):
         for a in range(SIDE):
             for b in range(SIDE):
-                mine[pl.ds((a * SIDE + b) * SHARD, SHARD), :] = kept[a][0, b]
-                theirs[pl.ds((b * SIDE + a) * SHARD, SHARD), :] = crossed[a, b]
+                mine[pl.ds((a * SIDE + b) * SHARD, SHARD), width] = kept[a][0, b]
+                theirs[pl.ds((b * SIDE + a) * SHARD, SHARD), width] = crossed[a, b]
 
     @pl.when(core == 0)
     def _():
@@ -57,7 +58,8 @@
         fill(vals, keys)
 
     keys[own, :] = ck_ref[...]
-    vals[own, :] = cv_ref[...]
+    vals[own, width] = cv_ref[...]
+    vals[:, pl.ds(HEAD_DIM, HEAD_DIM)] = jnp.ones((TOTAL, HEAD_DIM), jnp.bfloat16)
     row_no = lax.broadcasted_iota(jnp.int32, (COMP_LEN, COMP_LEN), 0)
     col_no = lax.broadcasted_iota(jnp.int32, (COMP_LEN, COMP_LEN), 1)
     visible = col_no <= row_no
@@ -70,11 +72,11 @@
         top = functools.reduce(jnp.maximum, [jnp.max(s, axis=1, keepdims=True) for s in scores])
         top = top * EXP2_SCALE
         grad = g_ref[:, pl.ds(member * HEAD_DIM, HEAD_DIM)]
-        dweights = [mxu(grad, vals[span, :], NT) for span in spans]
+        dweights = [mxu(grad, vals[span, width], NT) for span in spans]
         weights = [jnp.exp2(s * EXP2_SCALE - top) for s in scores]
-        total = sum(jnp.sum(w, axis=1, keepdims=True) for w in weights)
         weights_bf = [w.astype(jnp.bfloat16) for w in weights]
         numer = sum(mxu(w, vals[span, :], NN) for w, span in zip(weights_bf, spans))
+        numer, total = numer[:, :HEAD_DIM], numer[:, HEAD_DIM : HEAD_DIM + 1]
         return query, grad, dweights, weights, weights_bf, total, numer
 
     def backward(member, query, grad, dweights, weights, weights_bf, total, numer):
@@ -145,7 +147,7 @@
             aliases[base + len(extra)] = out_no
             extra.append(item)
     return pl.pallas_call(
-        functools.partial(attend_kernel, 512, len(extra)),
+        functools.partial(attend_kernel, 256, len(extra)),
         grid_spec=pltpu.PrefetchScalarGridSpec(
             num_scalar_prefetch=1,
             grid=(len(heads),),
@@ -154,7 +156,10 @@
             + [crossed_in]
             + [pl.BlockSpec(memory_space=pl.ANY)] * len(extra),
             out_specs=[per_head, per_head, per_kv, per_kv] + [square_out] * 2,
-            scratch_shapes=[pltpu.VMEM((TOTAL, HEAD_DIM), jnp.bfloat16)] * 2
+            scratch_shapes=[
+                pltpu.VMEM((TOTAL, HEAD_DIM), jnp.bfloat16),
+                pltpu.VMEM((TOTAL, 2 * HEAD_DIM), jnp.bfloat16),
+            ]
             + [pltpu.VMEM((HEAD_DIM, TOTAL), jnp.float32)] * 2,
         ),
         out_shape=[wide, wide, narrow, narrow] + [part] * 2,

time: 162 us -> 159 us (0.981)
  Pallas kernels: 47.2 us -> 44.2 us
    pallas_call x2, Pallas kernels: 47.2 us -> 44.2 us  [attend(): pl.pallas_call(functools.partial(attend_kernel, 256, len(extra)), grid_sp...]
  transfers between devices with their start and end apart: 30 -> 30, of which waited for: 19 -> 19; matrix products, arithmetic and copies ran while one was open for 3% -> 3% of each run, Pallas kernels for 29% -> 28%
where the time goes in v3:
time: 159 us; the launch traced here: 158 us
  waiting for transfers between devices  51.3 us (32%)
  starting transfers between devices  45.5 us (29%)
  Pallas kernels  44.2 us (28%)
  other arithmetic  6.82 us (4%)
  between operations  6.28 us (4%)
  local copies, waits for them, and re-layouts  4.43 us (3%)
    pallas_call x2, Pallas kernels, attend(): pl.pallas_call(functools.partial(attend_kernel, 256, len(extra)), grid_sp...  44.2 us
    ppermute x18, waiting for transfers between devices, move_plane(): return lax.ppermute(item, ('prompt', 'learner'), pairs)  33.1 us
    ppermute x18, starting transfers between devices, move_plane(): return lax.ppermute(item, ('prompt', 'learner'), pairs)  25.9 us
    ppermute x6, waiting for transfers between devices, move_z(): return lax.ppermute(item, 'prompt', pairs)  14.2 us
    ppermute x6, starting transfers between devices, move_z(): return lax.ppermute(item, 'prompt', pairs)  10.7 us
    ppermute x6, starting transfers between devices, swap_cores(): return lax.ppermute(item, 'prompt', [(p, p ^ 1) for p in range(8)])  8.92 us
    ppermute x6, waiting for transfers between devices, swap_cores(): return lax.ppermute(item, 'prompt', [(p, p ^ 1) for p in range(8)])  3.98 us
  transfers between devices with their start and end apart: 30, of which 19 were waited for; matrix products, arithmetic and copies ran while one was open for 3% of the time, Pallas kernels for 28%

profile of v3, /device:TPU:1, one launch (start us, length us, event | category | flops | bytes accessed | tf_op | source)
XLA Modules:
  0.0 158.5 jit_solution(10501306277577666397)
XLA Ops:
  1.7 2.5 %collective-permute-start = (bf16[2,128,512]{2,1,0:T(8,128)(2,1)S(1)}, bf16[2,128,512]{2,1,0:T(8,128)(2,1)S(1)}, u32[]{:S(2)}, u32[]{:S(2)}) collective-permute-start(bf16[2,128,512]{2,1,0:T(8,128)(2,1)S(1)} %broadcast_select_fusion), channel_id=1, source_target_pairs={{0,32},{16,48},{32,64},{48,80},{64,96},{80,112},{96,0},{112,16},{1... | collective-permute-start | bytes 786440 | tf_op jit(solution)/shard_map/ppermute | solution.py:190
  4.2 3.3 %collective-permute-start.1 = (bf16[2,128,512]{2,1,0:T(8,128)(2,1)S(1)}, bf16[2,128,512]{2,1,0:T(8,128)(2,1)S(1)}, u32[]{:S(2)}, u32[]{:S(2)}) collective-permute-start(bf16[2,128,512]{2,1,0:T(8,128)(2,1)S(1)} %broadcast_select_fusion), channel_id=1, source_target_pairs={{0,64},{16,80},{32,96},{48,112},{64,0},{80,16},{96,32},{112,48},{1... | collective-permute-start | bytes 786440 | tf_op jit(solution)/shard_map/ppermute | solution.py:190
  12.4 6.5 %collective-permute-done.1 = bf16[2,128,512]{2,1,0:T(8,128)(2,1)S(1)} collective-permute-done((bf16[2,128,512]{2,1,0:T(8,128)(2,1)S(1)}, bf16[2,128,512]{2,1,0:T(8,128)(2,1)S(1)}, u32[]{:S(2)}, u32[]{:S(2)}) %collective-permute-start.1) | collective-permute-done | bytes 262176 | tf_op jit(solution)/shard_map/ppermute | solution.py:190
  20.1 1.6 %collective-permute-start.3 = (bf16[2,128,512]{2,1,0:T(8,128)(2,1)S(1)}, bf16[2,128,512]{2,1,0:T(8,128)(2,1)S(1)}, u32[]{:S(2)}, u32[]{:S(2)}) collective-permute-start(bf16[2,128,512]{2,1,0:T(8,128)(2,1)S(1)} %pad_maximum_fusion.11), channel_id=1, source_target_pairs={{0,16},{16,0},{32,48},{48,32},{64,80},{80,64},{96,112},{112,96},{1... | collective-permute-start | bytes 786440 | tf_op jit(solution)/shard_map/ppermute | solution.py:194
  27.6 2.4 %collective-permute-done.5 = bf16[2,128,512]{2,1,0:T(8,128)(2,1)S(1)} collective-permute-done((bf16[2,128,512]{2,1,0:T(8,128)(2,1)S(1)}, bf16[2,128,512]{2,1,0:T(8,128)(2,1)S(1)}, u32[]{:S(2)}, u32[]{:S(2)}) %collective-permute-start.5) | collective-permute-done | bytes 262176 | tf_op jit(solution)/shard_map/ppermute | solution.py:185
  30.0 2.2 %collective-permute-done.6 = bf16[2,128,512]{2,1,0:T(8,128)(2,1)S(1)} collective-permute-done((bf16[2,128,512]{2,1,0:T(8,128)(2,1)S(1)}, bf16[2,128,512]{2,1,0:T(8,128)(2,1)S(1)}, u32[]{:S(2)}, u32[]{:S(2)}) %collective-permute-start.6) | collective-permute-done | bytes 262176 | tf_op jit(solution)/shard_map/ppermute | solution.py:185
  32.1 1.8 %collective-permute-done.4 = bf16[2,128,512]{2,1,0:T(8,128)(2,1)S(1)} collective-permute-done((bf16[2,128,512]{2,1,0:T(8,128)(2,1)S(1)}, bf16[2,128,512]{2,1,0:T(8,128)(2,1)S(1)}, u32[]{:S(2)}, u32[]{:S(2)}) %collective-permute-start.4) | collective-permute-done | bytes 262176 | tf_op jit(solution)/shard_map/ppermute | solution.py:185
  34.2 2.5 %collective-permute-start.7 = (bf16[2,4,128,256]{3,2,1,0:T(8,128)(2,1)S(1)}, bf16[2,4,128,256]{3,2,1,0:T(8,128)(2,1)S(1)}, u32[]{:S(2)}, u32[]{:S(2)}) collective-permute-start(bf16[2,4,128,256]{3,2,1,0:T(8,128)(2,1)S(1)} %get-tuple-element.35.rest_0_), channel_id=1, source_target_pairs={{0,2},{1,3},{2,0},{3,1},{4,6},{5,7},{6,4},{7,5},{8,10},{9,11},{10,... | collective-permute-start | bytes 1572872 | tf_op jit(solution)/shard_map/ppermute | solution.py:185
  37.1 2.4 %collective-permute-start.9 = (bf16[2,4,128,256]{3,2,1,0:T(8,128)(2,1)S(1)}, bf16[2,4,128,256]{3,2,1,0:T(8,128)(2,1)S(1)}, u32[]{:S(2)}, u32[]{:S(2)}) collective-permute-start(bf16[2,4,128,256]{3,2,1,0:T(8,128)(2,1)S(1)} %get-tuple-element.35.rest_0_), channel_id=1, source_target_pairs={{0,3},{1,0},{2,1},{3,2},{4,7},{5,4},{6,5},{7,6},{8,11},{9,8},{10,9... | collective-permute-start | bytes 1572872 | tf_op jit(solution)/shard_map/ppermute | solution.py:185
  39.4 4.7 %collective-permute-done.7.rest_1_ = bf16[2,4,128,256]{3,2,1,0:T(8,128)(2,1)S(1)} collective-permute-done((bf16[2,4,128,256]{3,2,1,0:T(8,128)(2,1)S(1)}, bf16[2,4,128,256]{3,2,1,0:T(8,128)(2,1)S(1)}, u32[]{:S(2)}, u32[]{:S(2)}) %collective-permute-start.7) | collective-permute-done | bytes 524320 | tf_op jit(solution)/shard_map/ppermute | solution.py:185
  44.2 5.6 %collective-permute-done.8.rest_2_ = bf16[2,4,128,256]{3,2,1,0:T(8,128)(2,1)S(1)} collective-permute-done((bf16[2,4,128,256]{3,2,1,0:T(8,128)(2,1)S(1)}, bf16[2,4,128,256]{3,2,1,0:T(8,128)(2,1)S(1)}, u32[]{:S(2)}, u32[]{:S(2)}) %collective-permute-start.8) | collective-permute-done | bytes 524320 | tf_op jit(solution)/shard_map/ppermute | solution.py:185
  50.8 1.8 %collective-permute-start.10 = (bf16[4,4,128,256]{3,2,1,0:T(8,128)(2,1)S(1)}, bf16[4,4,128,256]{3,2,1,0:T(8,128)(2,1)S(1)}, u32[]{:S(2)}, u32[]{:S(2)}) collective-permute-start(bf16[4,4,128,256]{3,2,1,0:T(8,128)(2,1)S(1)} %pad_maximum_fusion.1), channel_id=1, source_target_pairs={{0,16},{16,0},{32,48},{48,32},{64,80},{80,64},{96,112},{112,96},{1... | collective-permute-start | bytes 3145736 | tf_op jit(solution)/shard_map/ppermute | solution.py:194
  57.5 22.1 %shard_map.127 = (bf16[256,2560]{1,0:T(8,128)(2,1)}, bf16[256,2560]{1,0:T(8,128)(2,1)}, bf16[256,512]{1,0:T(8,128)(2,1)}, bf16[256,512]{1,0:T(8,128)(2,1)}, bf16...) custom-call(s32[128]{0:T(128)} %len_ref.3, bf16[256,2560]{1,0:T(8,128)(2,1)} %bitcast.59, ...), custom_call_target="tpu_custom_call" | custom-call | flops 9059696640 | bytes 10485760 | tf_op jit(solution)/shard_map/pallas_call | solution.py:149
  81.5 2.2 %collective-permute-done.14 = bf16[4,4,128,256]{3,2,1,0:T(8,128)(2,1)S(1)} collective-permute-done((bf16[4,4,128,256]{3,2,1,0:T(8,128)(2,1)}, bf16[4,4,128,256]{3,2,1,0:T(8,128)(2,1)S(1)}, u32[]{:S(2)}, u32[]{:S(2)}) %collective-permute-start.14) | collective-permute-done | bytes 1048608 | tf_op jit(solution)/shard_map/ppermute | solution.py:194
  89.1 22.1 %shard_map.128 = (bf16[256,2560]{1,0:T(8,128)(2,1)}, bf16[256,2560]{1,0:T(8,128)(2,1)}, bf16[256,512]{1,0:T(8,128)(2,1)}, bf16[256,512]{1,0:T(8,128)(2,1)}, bf16...) custom-call(s32[128]{0:T(128)} %len_ref.3, ...), custom_call_target="tpu_custom_call", output_to_operand_aliasing={{0}: (10, {}), {1}: (11, {}), {2}: (12, {}), {3}: (13, {})} | custom-call | flops 9059696640 | bytes 10485760 | tf_op jit(solution)/shard_map/pallas_call | solution.py:149
  114.3 2.5 %collective-permute-start.20 = (bf16[2,4,128,256]{3,2,1,0:T(8,128)(2,1)S(1)}, bf16[2,4,128,256]{3,2,1,0:T(8,128)(2,1)S(1)}, u32[]{:S(2)}, u32[]{:S(2)}) collective-permute-start(bf16[2,4,128,256]{3,2,1,0:T(8,128)(2,1)S(1)} %pad_maximum_fusion.7), channel_id=1, source_target_pairs={{0,2},{1,3},{2,0},{3,1},{4,6},{5,7},{6,4},{7,5},{8,10},{9,11},{10,... | collective-permute-start | bytes 1572872 | tf_op jit(solution)/shard_map/ppermute | solution.py:185
  119.1 5.2 %collective-permute-done.20 = bf16[2,4,128,256]{3,2,1,0:T(8,128)(2,1)S(1)} collective-permute-done((bf16[2,4,128,256]{3,2,1,0:T(8,128)(2,1)S(1)}, bf16[2,4,128,256]{3,2,1,0:T(8,128)(2,1)S(1)}, u32[]{:S(2)}, u32[]{:S(2)}) %collective-permute-start.20) | collective-permute-done | bytes 524320 | tf_op jit(solution)/shard_map/ppermute | solution.py:185
  124.3 5.0 %collective-permute-done.21 = bf16[2,4,128,256]{3,2,1,0:T(8,128)(2,1)S(1)} collective-permute-done((bf16[2,4,128,256]{3,2,1,0:T(8,128)(2,1)S(1)}, bf16[2,4,128,256]{3,2,1,0:T(8,128)(2,1)S(1)}, u32[]{:S(2)}, u32[]{:S(2)}) %collective-permute-start.21) | collective-permute-done | bytes 524320 | tf_op jit(solution)/shard_map/ppermute | solution.py:185
  130.2 2.8 %collective-permute-start.23 = (bf16[2,128,512]{2,1,0:T(8,128)(2,1)S(1)}, bf16[2,128,512]{2,1,0:T(8,128)(2,1)S(1)}, u32[]{:S(2)}, u32[]{:S(2)}) collective-permute-start(bf16[2,128,512]{2,1,0:T(8,128)(2,1)S(1)} %get-tuple-element.70), channel_id=1, source_target_pairs={{0,8},{1,9},{2,10},{3,11},{4,12},{5,13},{6,14},{7,15},{8,0},{9,1},... | collective-permute-start | bytes 786440 | tf_op jit(solution)/shard_map/ppermute | solution.py:185
  134.5 2.8 %collective-permute-done.23 = bf16[2,128,512]{2,1,0:T(8,128)(2,1)S(1)} collective-permute-done((bf16[2,128,512]{2,1,0:T(8,128)(2,1)S(1)}, bf16[2,128,512]{2,1,0:T(8,128)(2,1)S(1)}, u32[]{:S(2)}, u32[]{:S(2)}) %collective-permute-start.23) | collective-permute-done | bytes 262176 | tf_op jit(solution)/shard_map/ppermute | solution.py:185
  137.3 1.8 %collective-permute-done.24 = bf16[2,128,512]{2,1,0:T(8,128)(2,1)S(1)} collective-permute-done((bf16[2,128,512]{2,1,0:T(8,128)(2,1)S(1)}, bf16[2,128,512]{2,1,0:T(8,128)(2,1)S(1)}, u32[]{:S(2)}, u32[]{:S(2)}) %collective-permute-start.24) | collective-permute-done | bytes 262176 | tf_op jit(solution)/shard_map/ppermute | solution.py:185
  141.2 2.1 %collective-permute-start.27 = (bf16[2,128,512]{2,1,0:T(8,128)(2,1)S(1)}, bf16[2,128,512]{2,1,0:T(8,128)(2,1)S(1)}, u32[]{:S(2)}, u32[]{:S(2)}) collective-permute-start(bf16[2,128,512]{2,1,0:T(8,128)(2,1)S(1)} %fusion.2), channel_id=1, source_target_pairs={{0,64},{16,80},{32,96},{48,112},{64,0},{80,16},{96,32},{112,48},{1... | collective-permute-start | bytes 786440 | tf_op jit(solution)/shard_map/ppermute | solution.py:190
  146.7 5.4 %collective-permute-done.27 = bf16[2,128,512]{2,1,0:T(8,128)(2,1)S(1)} collective-permute-done((bf16[2,128,512]{2,1,0:T(8,128)(2,1)S(1)}, bf16[2,128,512]{2,1,0:T(8,128)(2,1)S(1)}, u32[]{:S(2)}, u32[]{:S(2)}) %collective-permute-start.27) | collective-permute-done | bytes 262176 | tf_op jit(solution)/shard_map/ppermute | solution.py:190
  153.4 3.2 %collective-permute-start.29 = (bf16[128,512]{1,0:T(8,128)(2,1)S(1)}, bf16[128,512]{1,0:T(8,128)(2,1)S(1)}, u32[]{:S(2)}, u32[]{:S(2)}) collective-permute-start(bf16[128,512]{1,0:T(8,128)(2,1)S(1)} %fusion.10), channel_id=1, source_target_pairs={{0,16},{16,0},{32,48},{48,32},{64,80},{80,64},{96,112},{112,96},{1... | collective-permute-start | bytes 393224 | tf_op jit(solution)/shard_map/ppermute | solution.py:194
  (100 shorter events, 37.5 us)
Async XLA Ops:
  1.7 10.7 %collective-permute-start = (bf16[2,128,512]{2,1,0:T(8,128)(2,1)S(1)}, bf16[2,128,512]{2,1,0:T(8,128)(2,1)S(1)}, u32[]{:S(2)}, u32[]{:S(2)}) collective-permute-start(bf16[2,128,512]{2,1,0:T(8,128)(2,1)S(1)} %broadcast_select_fusion), channel_id=1, source_target_pairs={{0,32},{16,48},{32,64},{48,80},{64,96},{80,112},{96,0},{112,16},{1... | collective-permute-start | bytes 786440 | tf_op jit(solution)/shard_map/ppermute | solution.py:190
  4.2 14.6 %collective-permute-start.1 = (bf16[2,128,512]{2,1,0:T(8,128)(2,1)S(1)}, bf16[2,128,512]{2,1,0:T(8,128)(2,1)S(1)}, u32[]{:S(2)}, u32[]{:S(2)}) collective-permute-start(bf16[2,128,512]{2,1,0:T(8,128)(2,1)S(1)} %broadcast_select_fusion), channel_id=1, source_target_pairs={{0,64},{16,80},{32,96},{48,112},{64,0},{80,16},{96,32},{112,48},{1... | collective-permute-start | bytes 786440 | tf_op jit(solution)/shard_map/ppermute | solution.py:190
  7.5 11.3 %collective-permute-start.2 = (bf16[2,128,512]{2,1,0:T(8,128)(2,1)S(1)}, bf16[2,128,512]{2,1,0:T(8,128)(2,1)S(1)}, u32[]{:S(2)}, u32[]{:S(2)}) collective-permute-start(bf16[2,128,512]{2,1,0:T(8,128)(2,1)S(1)} %broadcast_select_fusion), channel_id=1, source_target_pairs={{0,96},{16,112},{32,0},{48,16},{64,32},{80,48},{96,64},{112,80},{1... | collective-permute-start | bytes 786440 | tf_op jit(solution)/shard_map/ppermute | solution.py:190
  23.1 6.9 %collective-permute-start.5 = (bf16[2,128,512]{2,1,0:T(8,128)(2,1)S(1)}, bf16[2,128,512]{2,1,0:T(8,128)(2,1)S(1)}, u32[]{:S(2)}, u32[]{:S(2)}) collective-permute-start(bf16[2,128,512]{2,1,0:T(8,128)(2,1)S(1)} %get-tuple-element.96), channel_id=1, source_target_pairs={{0,4},{1,5},{2,6},{3,7},{4,8},{5,9},{6,10},{7,11},{8,12},{9,13},{1... | collective-permute-start | bytes 786440 | tf_op jit(solution)/shard_map/ppermute | solution.py:185
  24.5 7.6 %collective-permute-start.6 = (bf16[2,128,512]{2,1,0:T(8,128)(2,1)S(1)}, bf16[2,128,512]{2,1,0:T(8,128)(2,1)S(1)}, u32[]{:S(2)}, u32[]{:S(2)}) collective-permute-start(bf16[2,128,512]{2,1,0:T(8,128)(2,1)S(1)} %get-tuple-element.96), channel_id=1, source_target_pairs={{0,12},{1,13},{2,14},{3,15},{4,0},{5,1},{6,2},{7,3},{8,4},{9,5},{1... | collective-permute-start | bytes 786440 | tf_op jit(solution)/shard_map/ppermute | solution.py:185
  26.0 8.0 %collective-permute-start.4 = (bf16[2,128,512]{2,1,0:T(8,128)(2,1)S(1)}, bf16[2,128,512]{2,1,0:T(8,128)(2,1)S(1)}, u32[]{:S(2)}, u32[]{:S(2)}) collective-permute-start(bf16[2,128,512]{2,1,0:T(8,128)(2,1)S(1)} %get-tuple-element.96), channel_id=1, source_target_pairs={{0,8},{1,9},{2,10},{3,11},{4,12},{5,13},{6,14},{7,15},{8,0},{9,1},... | collective-permute-start | bytes 786440 | tf_op jit(solution)/shard_map/ppermute | solution.py:185
  34.2 10.0 %collective-permute-start.7 = (bf16[2,4,128,256]{3,2,1,0:T(8,128)(2,1)S(1)}, bf16[2,4,128,256]{3,2,1,0:T(8,128)(2,1)S(1)}, u32[]{:S(2)}, u32[]{:S(2)}) collective-permute-start(bf16[2,4,128,256]{3,2,1,0:T(8,128)(2,1)S(1)} %get-tuple-element.35.rest_0_), channel_id=1, source_target_pairs={{0,2},{1,3},{2,0},{3,1},{4,6},{5,7},{6,4},{7,5},{8,10},{9,11},{10,... | collective-permute-start | bytes 1572872 | tf_op jit(solution)/shard_map/ppermute | solution.py:185
  36.8 13.0 %collective-permute-start.8 = (bf16[2,4,128,256]{3,2,1,0:T(8,128)(2,1)S(1)}, bf16[2,4,128,256]{3,2,1,0:T(8,128)(2,1)S(1)}, u32[]{:S(2)}, u32[]{:S(2)}) collective-permute-start(bf16[2,4,128,256]{3,2,1,0:T(8,128)(2,1)S(1)} %get-tuple-element.35.rest_0_), channel_id=1, source_target_pairs={{0,1},{1,2},{2,3},{3,0},{4,5},{5,6},{6,7},{7,4},{8,9},{9,10},{10,1... | collective-permute-start | bytes 1572872 | tf_op jit(solution)/shard_map/ppermute | solution.py:185
  37.1 12.7 %collective-permute-start.9 = (bf16[2,4,128,256]{3,2,1,0:T(8,128)(2,1)S(1)}, bf16[2,4,128,256]{3,2,1,0:T(8,128)(2,1)S(1)}, u32[]{:S(2)}, u32[]{:S(2)}) collective-permute-start(bf16[2,4,128,256]{3,2,1,0:T(8,128)(2,1)S(1)} %get-tuple-element.35.rest_0_), channel_id=1, source_target_pairs={{0,3},{1,0},{2,1},{3,2},{4,7},{5,4},{6,5},{7,6},{8,11},{9,8},{10,9... | collective-permute-start | bytes 1572872 | tf_op jit(solution)/shard_map/ppermute | solution.py:185
  52.6 27.0 %collective-permute-start.11 = (bf16[2,4,128,256]{3,2,1,0:T(8,128)(2,1)S(1)}, bf16[2,4,128,256]{3,2,1,0:T(8,128)(2,1)S(1)}, u32[]{:S(2)}, u32[]{:S(2)}) collective-permute-start(bf16[2,4,128,256]{3,2,1,0:T(8,128)(2,1)S(1)} %get-tuple-element.41.rest_0_), channel_id=1, source_target_pairs={{0,2},{1,3},{2,0},{3,1},{4,6},{5,7},{6,4},{7,5},{8,10},{9,11},{10,... | collective-permute-start | bytes 1572872 | tf_op jit(solution)/shard_map/ppermute | solution.py:185
  53.9 25.8 %collective-permute-start.12 = (bf16[2,4,128,256]{3,2,1,0:T(8,128)(2,1)S(1)}, bf16[2,4,128,256]{3,2,1,0:T(8,128)(2,1)S(1)}, u32[]{:S(2)}, u32[]{:S(2)}) collective-permute-start(bf16[2,4,128,256]{3,2,1,0:T(8,128)(2,1)S(1)} %get-tuple-element.41.rest_0_), channel_id=1, source_target_pairs={{0,1},{1,2},{2,3},{3,0},{4,5},{5,6},{6,7},{7,4},{8,9},{9,10},{10,1... | collective-permute-start | bytes 1572872 | tf_op jit(solution)/shard_map/ppermute | solution.py:185
  55.1 24.5 %collective-permute-start.13 = (bf16[2,4,128,256]{3,2,1,0:T(8,128)(2,1)S(1)}, bf16[2,4,128,256]{3,2,1,0:T(8,128)(2,1)S(1)}, u32[]{:S(2)}, u32[]{:S(2)}) collective-permute-start(bf16[2,4,128,256]{3,2,1,0:T(8,128)(2,1)S(1)} %get-tuple-element.41.rest_0_), channel_id=1, source_target_pairs={{0,3},{1,0},{2,1},{3,2},{4,7},{5,4},{6,5},{7,6},{8,11},{9,8},{10,9... | collective-permute-start | bytes 1572872 | tf_op jit(solution)/shard_map/ppermute | solution.py:185
  84.3 26.9 %collective-permute-start.18 = (bf16[2,4,128,256]{3,2,1,0:T(8,128)(2,1)S(1)}, bf16[2,4,128,256]{3,2,1,0:T(8,128)(2,1)S(1)}, u32[]{:S(2)}, u32[]{:S(2)}) collective-permute-start(bf16[2,4,128,256]{3,2,1,0:T(8,128)(2,1)S(1)} %pad_maximum_fusion.6), channel_id=1, source_target_pairs={{0,1},{1,2},{2,3},{3,0},{4,5},{5,6},{6,7},{7,4},{8,9},{9,10},{10,1... | collective-permute-start | bytes 1572872 | tf_op jit(solution)/shard_map/ppermute | solution.py:185
  85.6 25.6 %collective-permute-start.17 = (bf16[2,4,128,256]{3,2,1,0:T(8,128)(2,1)S(1)}, bf16[2,4,128,256]{3,2,1,0:T(8,128)(2,1)S(1)}, u32[]{:S(2)}, u32[]{:S(2)}) collective-permute-start(bf16[2,4,128,256]{3,2,1,0:T(8,128)(2,1)S(1)} %pad_maximum_fusion.5), channel_id=1, source_target_pairs={{0,3},{1,0},{2,1},{3,2},{4,7},{5,4},{6,5},{7,6},{8,11},{9,8},{10,9... | collective-permute-start | bytes 1572872 | tf_op jit(solution)/shard_map/ppermute | solution.py:185
  87.2 24.0 %collective-permute-start.16 = (bf16[2,4,128,256]{3,2,1,0:T(8,128)(2,1)S(1)}, bf16[2,4,128,256]{3,2,1,0:T(8,128)(2,1)S(1)}, u32[]{:S(2)}, u32[]{:S(2)}) collective-permute-start(bf16[2,4,128,256]{3,2,1,0:T(8,128)(2,1)S(1)} %pad_maximum_fusion.4), channel_id=1, source_target_pairs={{0,2},{1,3},{2,0},{3,1},{4,6},{5,7},{6,4},{7,5},{8,10},{9,11},{10,... | collective-permute-start | bytes 1572872 | tf_op jit(solution)/shard_map/ppermute | solution.py:185
  114.3 10.0 %collective-permute-start.20 = (bf16[2,4,128,256]{3,2,1,0:T(8,128)(2,1)S(1)}, bf16[2,4,128,256]{3,2,1,0:T(8,128)(2,1)S(1)}, u32[]{:S(2)}, u32[]{:S(2)}) collective-permute-start(bf16[2,4,128,256]{3,2,1,0:T(8,128)(2,1)S(1)} %pad_maximum_fusion.7), channel_id=1, source_target_pairs={{0,2},{1,3},{2,0},{3,1},{4,6},{5,7},{6,4},{7,5},{8,10},{9,11},{10,... | collective-permute-start | bytes 1572872 | tf_op jit(solution)/shard_map/ppermute | solution.py:185
  116.9 12.4 %collective-permute-start.21 = (bf16[2,4,128,256]{3,2,1,0:T(8,128)(2,1)S(1)}, bf16[2,4,128,256]{3,2,1,0:T(8,128)(2,1)S(1)}, u32[]{:S(2)}, u32[]{:S(2)}) collective-permute-start(bf16[2,4,128,256]{3,2,1,0:T(8,128)(2,1)S(1)} %pad_maximum_fusion.8), channel_id=1, source_target_pairs={{0,3},{1,0},{2,1},{3,2},{4,7},{5,4},{6,5},{7,6},{8,11},{9,8},{10,9... | collective-permute-start | bytes 1572872 | tf_op jit(solution)/shard_map/ppermute | solution.py:185
  117.9 11.9 %collective-permute-start.22 = (bf16[2,4,128,256]{3,2,1,0:T(8,128)(2,1)S(1)}, bf16[2,4,128,256]{3,2,1,0:T(8,128)(2,1)S(1)}, u32[]{:S(2)}, u32[]{:S(2)}) collective-permute-start(bf16[2,4,128,256]{3,2,1,0:T(8,128)(2,1)S(1)} %pad_maximum_fusion.9), channel_id=1, source_target_pairs={{0,1},{1,2},{2,3},{3,0},{4,5},{5,6},{6,7},{7,4},{8,9},{9,10},{10,1... | collective-permute-start | bytes 1572872 | tf_op jit(solution)/shard_map/ppermute | solution.py:185
  130.2 7.1 %collective-permute-start.23 = (bf16[2,128,512]{2,1,0:T(8,128)(2,1)S(1)}, bf16[2,128,512]{2,1,0:T(8,128)(2,1)S(1)}, u32[]{:S(2)}, u32[]{:S(2)}) collective-permute-start(bf16[2,128,512]{2,1,0:T(8,128)(2,1)S(1)} %get-tuple-element.70), channel_id=1, source_target_pairs={{0,8},{1,9},{2,10},{3,11},{4,12},{5,13},{6,14},{7,15},{8,0},{9,1},... | collective-permute-start | bytes 786440 | tf_op jit(solution)/shard_map/ppermute | solution.py:185
  133.0 6.1 %collective-permute-start.24 = (bf16[2,128,512]{2,1,0:T(8,128)(2,1)S(1)}, bf16[2,128,512]{2,1,0:T(8,128)(2,1)S(1)}, u32[]{:S(2)}, u32[]{:S(2)}) collective-permute-start(bf16[2,128,512]{2,1,0:T(8,128)(2,1)S(1)} %get-tuple-element.72), channel_id=1, source_target_pairs={{0,12},{1,13},{2,14},{3,15},{4,0},{5,1},{6,2},{7,3},{8,4},{9,5},{1... | collective-permute-start | bytes 786440 | tf_op jit(solution)/shard_map/ppermute | solution.py:185
  133.0 7.1 %collective-permute-start.25 = (bf16[2,128,512]{2,1,0:T(8,128)(2,1)S(1)}, bf16[2,128,512]{2,1,0:T(8,128)(2,1)S(1)}, u32[]{:S(2)}, u32[]{:S(2)}) collective-permute-start(bf16[2,128,512]{2,1,0:T(8,128)(2,1)S(1)} %get-tuple-element.71), channel_id=1, source_target_pairs={{0,4},{1,5},{2,6},{3,7},{4,8},{5,9},{6,10},{7,11},{8,12},{9,13},{1... | collective-permute-start | bytes 786440 | tf_op jit(solution)/shard_map/ppermute | solution.py:185
  140.2 6.5 %collective-permute-start.26 = (bf16[2,128,512]{2,1,0:T(8,128)(2,1)S(1)}, bf16[2,128,512]{2,1,0:T(8,128)(2,1)S(1)}, u32[]{:S(2)}, u32[]{:S(2)}) collective-permute-start(bf16[2,128,512]{2,1,0:T(8,128)(2,1)S(1)} %fusion.2), channel_id=1, source_target_pairs={{0,32},{16,48},{32,64},{48,80},{64,96},{80,112},{96,0},{112,16},{1... | collective-permute-start | bytes 786440 | tf_op jit(solution)/shard_map/ppermute | solution.py:190
  141.2 10.9 %collective-permute-start.27 = (bf16[2,128,512]{2,1,0:T(8,128)(2,1)S(1)}, bf16[2,128,512]{2,1,0:T(8,128)(2,1)S(1)}, u32[]{:S(2)}, u32[]{:S(2)}) collective-permute-start(bf16[2,128,512]{2,1,0:T(8,128)(2,1)S(1)} %fusion.2), channel_id=1, source_target_pairs={{0,64},{16,80},{32,96},{48,112},{64,0},{80,16},{96,32},{112,48},{1... | collective-permute-start | bytes 786440 | tf_op jit(solution)/shard_map/ppermute | solution.py:190
  143.4 9.9 %collective-permute-start.28 = (bf16[2,128,512]{2,1,0:T(8,128)(2,1)S(1)}, bf16[2,128,512]{2,1,0:T(8,128)(2,1)S(1)}, u32[]{:S(2)}, u32[]{:S(2)}) collective-permute-start(bf16[2,128,512]{2,1,0:T(8,128)(2,1)S(1)} %fusion.2), channel_id=1, source_target_pairs={{0,96},{16,112},{32,0},{48,16},{64,32},{80,48},{96,64},{112,80},{1... | collective-permute-start | bytes 786440 | tf_op jit(solution)/shard_map/ppermute | solution.py:190
  (17 other events, 105.3 us)

commit v4 on v3

--- a/solution.py
+++ b/solution.py
@@ -164,7 +164,7 @@
         ),
         out_shape=[wide, wide, narrow, narrow] + [part] * 2,
         input_output_aliases=aliases,
-        compiler_params=pltpu.CompilerParams(vmem_limit_bytes=60 * 2**20),
+        compiler_params=pltpu.CompilerParams(vmem_limit_bytes=48 * 2**20),
         cost_estimate=pl.CostEstimate(
             flops=len(heads) * 6 * 2 * Q_PER_KV * COMP_LEN * TOTAL * HEAD_DIM,
             bytes_accessed=len(heads) * 5 * 2**20,

time: 159 us -> 154 us (0.969)
  local copies, waits for them, and re-layouts: 4.43 us -> 0.59 us
  Pallas kernels: 44.2 us -> 42.5 us
    unnamed x22 -> x6, local copies, waits for them, and re-layouts: 2.71 us -> 0.02 us
    pallas_call x2, Pallas kernels: 44.2 us -> 42.5 us  [attend(): pl.pallas_call(functools.partial(attend_kernel, 256, len(extra)), grid_sp...]
  transfers between devices with their start and end apart: 30 -> 30, of which waited for: 19 -> 19; matrix products, arithmetic and copies ran while one was open for 3% -> 2% of each run, Pallas kernels for 28% -> 28%
where the time goes in v4:
time: 154 us
  waiting for transfers between devices  51.9 us (34%)
  starting transfers between devices  45.8 us (30%)
  Pallas kernels  42.5 us (28%)
  other arithmetic  6.85 us (4%)
  between operations  6.21 us (4%)
    pallas_call x2, Pallas kernels, attend(): pl.pallas_call(functools.partial(attend_kernel, 256, len(extra)), grid_sp...  42.5 us
    ppermute x18, waiting for transfers between devices, move_plane(): return lax.ppermute(item, ('prompt', 'learner'), pairs)  33.1 us
    ppermute x18, starting transfers between devices, move_plane(): return lax.ppermute(item, ('prompt', 'learner'), pairs)  25.9 us
    ppermute x6, waiting for transfers between devices, move_z(): return lax.ppermute(item, 'prompt', pairs)  14.1 us
    ppermute x6, starting transfers between devices, move_z(): return lax.ppermute(item, 'prompt', pairs)  10.7 us
    ppermute x6, starting transfers between devices, swap_cores(): return lax.ppermute(item, 'prompt', [(p, p ^ 1) for p in range(8)])  9.14 us
    ppermute x6, waiting for transfers between devices, swap_cores(): return lax.ppermute(item, 'prompt', [(p, p ^ 1) for p in range(8)])  4.76 us
  transfers between devices with their start and end apart: 30, of which 19 were waited for; matrix products, arithmetic and copies ran while one was open for 2% of the time, Pallas kernels for 28%

profile of v4, /device:TPU:1, one launch (start us, length us, event | category | flops | bytes accessed | tf_op | source)
XLA Modules:
  0.0 153.9 jit_solution(10927079573841604404)
XLA Ops:
  1.7 2.5 %collective-permute-start = (bf16[2,128,512]{2,1,0:T(8,128)(2,1)S(1)}, bf16[2,128,512]{2,1,0:T(8,128)(2,1)S(1)}, u32[]{:S(2)}, u32[]{:S(2)}) collective-permute-start(bf16[2,128,512]{2,1,0:T(8,128)(2,1)S(1)} %broadcast_select_fusion), channel_id=1, source_target_pairs={{0,32},{16,48},{32,64},{48,80},{64,96},{80,112},{96,0},{112,16},{1... | collective-permute-start | bytes 786440 | tf_op jit(solution)/shard_map/ppermute | solution.py:190
  4.2 3.3 %collective-permute-start.1 = (bf16[2,128,512]{2,1,0:T(8,128)(2,1)S(1)}, bf16[2,128,512]{2,1,0:T(8,128)(2,1)S(1)}, u32[]{:S(2)}, u32[]{:S(2)}) collective-permute-start(bf16[2,128,512]{2,1,0:T(8,128)(2,1)S(1)} %broadcast_select_fusion), channel_id=1, source_target_pairs={{0,64},{16,80},{32,96},{48,112},{64,0},{80,16},{96,32},{112,48},{1... | collective-permute-start | bytes 786440 | tf_op jit(solution)/shard_map/ppermute | solution.py:190
  12.4 6.5 %collective-permute-done.1 = bf16[2,128,512]{2,1,0:T(8,128)(2,1)S(1)} collective-permute-done((bf16[2,128,512]{2,1,0:T(8,128)(2,1)S(1)}, bf16[2,128,512]{2,1,0:T(8,128)(2,1)S(1)}, u32[]{:S(2)}, u32[]{:S(2)}) %collective-permute-start.1) | collective-permute-done | bytes 262176 | tf_op jit(solution)/shard_map/ppermute | solution.py:190
  27.5 2.4 %collective-permute-done.5 = bf16[2,128,512]{2,1,0:T(8,128)(2,1)S(1)} collective-permute-done((bf16[2,128,512]{2,1,0:T(8,128)(2,1)S(1)}, bf16[2,128,512]{2,1,0:T(8,128)(2,1)S(1)}, u32[]{:S(2)}, u32[]{:S(2)}) %collective-permute-start.5) | collective-permute-done | bytes 262176 | tf_op jit(solution)/shard_map/ppermute | solution.py:185
  30.0 2.2 %collective-permute-done.6 = bf16[2,128,512]{2,1,0:T(8,128)(2,1)S(1)} collective-permute-done((bf16[2,128,512]{2,1,0:T(8,128)(2,1)S(1)}, bf16[2,128,512]{2,1,0:T(8,128)(2,1)S(1)}, u32[]{:S(2)}, u32[]{:S(2)}) %collective-permute-start.6) | collective-permute-done | bytes 262176 | tf_op jit(solution)/shard_map/ppermute | solution.py:185
  32.1 1.8 %collective-permute-done.4 = bf16[2,128,512]{2,1,0:T(8,128)(2,1)S(1)} collective-permute-done((bf16[2,128,512]{2,1,0:T(8,128)(2,1)S(1)}, bf16[2,128,512]{2,1,0:T(8,128)(2,1)S(1)}, u32[]{:S(2)}, u32[]{:S(2)}) %collective-permute-start.4) | collective-permute-done | bytes 262176 | tf_op jit(solution)/shard_map/ppermute | solution.py:185
  34.2 2.5 %collective-permute-start.7 = (bf16[2,4,128,256]{3,2,1,0:T(8,128)(2,1)S(1)}, bf16[2,4,128,256]{3,2,1,0:T(8,128)(2,1)S(1)}, u32[]{:S(2)}, u32[]{:S(2)}) collective-permute-start(bf16[2,4,128,256]{3,2,1,0:T(8,128)(2,1)S(1)} %get-tuple-element.35.rest_0_), channel_id=1, source_target_pairs={{0,2},{1,3},{2,0},{3,1},{4,6},{5,7},{6,4},{7,5},{8,10},{9,11},{10,... | collective-permute-start | bytes 1572872 | tf_op jit(solution)/shard_map/ppermute | solution.py:185
  37.0 2.4 %collective-permute-start.9 = (bf16[2,4,128,256]{3,2,1,0:T(8,128)(2,1)S(1)}, bf16[2,4,128,256]{3,2,1,0:T(8,128)(2,1)S(1)}, u32[]{:S(2)}, u32[]{:S(2)}) collective-permute-start(bf16[2,4,128,256]{3,2,1,0:T(8,128)(2,1)S(1)} %get-tuple-element.35.rest_0_), channel_id=1, source_target_pairs={{0,3},{1,0},{2,1},{3,2},{4,7},{5,4},{6,5},{7,6},{8,11},{9,8},{10,9... | collective-permute-start | bytes 1572872 | tf_op jit(solution)/shard_map/ppermute | solution.py:185
  39.4 4.7 %collective-permute-done.7.rest_1_ = bf16[2,4,128,256]{3,2,1,0:T(8,128)(2,1)S(1)} collective-permute-done((bf16[2,4,128,256]{3,2,1,0:T(8,128)(2,1)S(1)}, bf16[2,4,128,256]{3,2,1,0:T(8,128)(2,1)S(1)}, u32[]{:S(2)}, u32[]{:S(2)}) %collective-permute-start.7) | collective-permute-done | bytes 524320 | tf_op jit(solution)/shard_map/ppermute | solution.py:185
  44.1 5.6 %collective-permute-done.8.rest_2_ = bf16[2,4,128,256]{3,2,1,0:T(8,128)(2,1)S(1)} collective-permute-done((bf16[2,4,128,256]{3,2,1,0:T(8,128)(2,1)S(1)}, bf16[2,4,128,256]{3,2,1,0:T(8,128)(2,1)S(1)}, u32[]{:S(2)}, u32[]{:S(2)}) %collective-permute-start.8) | collective-permute-done | bytes 524320 | tf_op jit(solution)/shard_map/ppermute | solution.py:185
  50.0 2.1 %collective-permute-start.10 = (bf16[4,4,128,256]{3,2,1,0:T(8,128)(2,1)S(1)}, bf16[4,4,128,256]{3,2,1,0:T(8,128)(2,1)S(1)}, u32[]{:S(2)}, u32[]{:S(2)}) collective-permute-start(bf16[4,4,128,256]{3,2,1,0:T(8,128)(2,1)S(1)} %pad_maximum_fusion.1), channel_id=1, source_target_pairs={{0,16},{16,0},{32,48},{48,32},{64,80},{80,64},{96,112},{112,96},{1... | collective-permute-start | bytes 3145736 | tf_op jit(solution)/shard_map/ppermute | solution.py:194
  56.1 21.3 %shard_map.127 = (bf16[256,2560]{1,0:T(8,128)(2,1)}, bf16[256,2560]{1,0:T(8,128)(2,1)}, bf16[256,512]{1,0:T(8,128)(2,1)}, bf16[256,512]{1,0:T(8,128)(2,1)}, bf16...) custom-call(s32[128]{0:T(128)S(1)} %copy-done.2, bf16[256,2560]{1,0:T(8,128)(2,1)} %bitcast.63, ...), custom_call_target="tpu_custom_call" | custom-call | flops 9059696640 | bytes 10485760 | tf_op jit(solution)/shard_map/pallas_call | solution.py:149
  79.1 2.0 %collective-permute-done.14 = bf16[4,4,128,256]{3,2,1,0:T(8,128)(2,1)S(1)} collective-permute-done((bf16[4,4,128,256]{3,2,1,0:T(8,128)(2,1)S(1)}, bf16[4,4,128,256]{3,2,1,0:T(8,128)(2,1)S(1)}, u32[]{:S(2)}, u32[]{:S(2)}) %collective-permute-start.14) | collective-permute-done | bytes 1048608 | tf_op jit(solution)/shard_map/ppermute | solution.py:194
  83.0 1.8 %collective-permute-start.17 = (bf16[2,4,128,256]{3,2,1,0:T(8,128)(2,1)S(1)}, bf16[2,4,128,256]{3,2,1,0:T(8,128)(2,1)S(1)}, u32[]{:S(2)}, u32[]{:S(2)}) collective-permute-start(bf16[2,4,128,256]{3,2,1,0:T(8,128)(2,1)S(1)} %pad_maximum_fusion.5), channel_id=1, source_target_pairs={{0,3},{1,0},{2,1},{3,2},{4,7},{5,4},{6,5},{7,6},{8,11},{9,8},{10,9... | collective-permute-start | bytes 1572872 | tf_op jit(solution)/shard_map/ppermute | solution.py:185
  85.6 21.3 %shard_map.128 = (bf16[256,2560]{1,0:T(8,128)(2,1)}, bf16[256,2560]{1,0:T(8,128)(2,1)}, bf16[256,512]{1,0:T(8,128)(2,1)}, bf16[256,512]{1,0:T(8,128)(2,1)}, bf16...) custom-call(s32[128]{0:T(128)S(1)} %copy-done.2, ...), custom_call_target="tpu_custom_call", output_to_operand_aliasing={{0}: (10, {}), {1}: (11, {}), {2}: (12, {}), {3}: (13, {})} | custom-call | flops 9059696640 | bytes 10485760 | tf_op jit(solution)/shard_map/pallas_call | solution.py:149
  107.2 2.4 %collective-permute-done.19 = bf16[4,4,128,256]{3,2,1,0:T(8,128)(2,1)S(1)} collective-permute-done((bf16[4,4,128,256]{3,2,1,0:T(8,128)(2,1)S(1)}, bf16[4,4,128,256]{3,2,1,0:T(8,128)(2,1)S(1)}, u32[]{:S(2)}, u32[]{:S(2)}) %collective-permute-start.19) | collective-permute-done | bytes 1048608 | tf_op jit(solution)/shard_map/ppermute | solution.py:194
  109.7 2.5 %collective-permute-start.20 = (bf16[2,4,128,256]{3,2,1,0:T(8,128)(2,1)S(1)}, bf16[2,4,128,256]{3,2,1,0:T(8,128)(2,1)S(1)}, u32[]{:S(2)}, u32[]{:S(2)}) collective-permute-start(bf16[2,4,128,256]{3,2,1,0:T(8,128)(2,1)S(1)} %pad_maximum_fusion.7), channel_id=1, source_target_pairs={{0,2},{1,3},{2,0},{3,1},{4,6},{5,7},{6,4},{7,5},{8,10},{9,11},{10,... | collective-permute-start | bytes 1572872 | tf_op jit(solution)/shard_map/ppermute | solution.py:185
  114.5 5.1 %collective-permute-done.20 = bf16[2,4,128,256]{3,2,1,0:T(8,128)(2,1)S(1)} collective-permute-done((bf16[2,4,128,256]{3,2,1,0:T(8,128)(2,1)S(1)}, bf16[2,4,128,256]{3,2,1,0:T(8,128)(2,1)S(1)}, u32[]{:S(2)}, u32[]{:S(2)}) %collective-permute-start.20) | collective-permute-done | bytes 524320 | tf_op jit(solution)/shard_map/ppermute | solution.py:185
  119.7 5.1 %collective-permute-done.21 = bf16[2,4,128,256]{3,2,1,0:T(8,128)(2,1)S(1)} collective-permute-done((bf16[2,4,128,256]{3,2,1,0:T(8,128)(2,1)S(1)}, bf16[2,4,128,256]{3,2,1,0:T(8,128)(2,1)S(1)}, u32[]{:S(2)}, u32[]{:S(2)}) %collective-permute-start.21) | collective-permute-done | bytes 524320 | tf_op jit(solution)/shard_map/ppermute | solution.py:185
  125.6 2.8 %collective-permute-start.23 = (bf16[2,128,512]{2,1,0:T(8,128)(2,1)S(1)}, bf16[2,128,512]{2,1,0:T(8,128)(2,1)S(1)}, u32[]{:S(2)}, u32[]{:S(2)}) collective-permute-start(bf16[2,128,512]{2,1,0:T(8,128)(2,1)S(1)} %get-tuple-element.70), channel_id=1, source_target_pairs={{0,8},{1,9},{2,10},{3,11},{4,12},{5,13},{6,14},{7,15},{8,0},{9,1},... | collective-permute-start | bytes 786440 | tf_op jit(solution)/shard_map/ppermute | solution.py:185
  129.9 2.8 %collective-permute-done.23 = bf16[2,128,512]{2,1,0:T(8,128)(2,1)S(1)} collective-permute-done((bf16[2,128,512]{2,1,0:T(8,128)(2,1)S(1)}, bf16[2,128,512]{2,1,0:T(8,128)(2,1)S(1)}, u32[]{:S(2)}, u32[]{:S(2)}) %collective-permute-start.23) | collective-permute-done | bytes 262176 | tf_op jit(solution)/shard_map/ppermute | solution.py:185
  136.7 2.1 %collective-permute-start.27 = (bf16[2,128,512]{2,1,0:T(8,128)(2,1)S(1)}, bf16[2,128,512]{2,1,0:T(8,128)(2,1)S(1)}, u32[]{:S(2)}, u32[]{:S(2)}) collective-permute-start(bf16[2,128,512]{2,1,0:T(8,128)(2,1)S(1)} %fusion.2), channel_id=1, source_target_pairs={{0,64},{16,80},{32,96},{48,112},{64,0},{80,16},{96,32},{112,48},{1... | collective-permute-start | bytes 786440 | tf_op jit(solution)/shard_map/ppermute | solution.py:190
  142.2 5.4 %collective-permute-done.27 = bf16[2,128,512]{2,1,0:T(8,128)(2,1)S(1)} collective-permute-done((bf16[2,128,512]{2,1,0:T(8,128)(2,1)S(1)}, bf16[2,128,512]{2,1,0:T(8,128)(2,1)S(1)}, u32[]{:S(2)}, u32[]{:S(2)}) %collective-permute-start.27) | collective-permute-done | bytes 262176 | tf_op jit(solution)/shard_map/ppermute | solution.py:190
  148.8 3.3 %collective-permute-start.29 = (bf16[128,512]{1,0:T(8,128)(2,1)S(1)}, bf16[128,512]{1,0:T(8,128)(2,1)S(1)}, u32[]{:S(2)}, u32[]{:S(2)}) collective-permute-start(bf16[128,512]{1,0:T(8,128)(2,1)S(1)} %fusion.10), channel_id=1, source_target_pairs={{0,16},{16,0},{32,48},{48,32},{64,80},{80,64},{96,112},{112,96},{1... | collective-permute-start | bytes 393224 | tf_op jit(solution)/shard_map/ppermute | solution.py:194
  (84 shorter events, 33.7 us)
Async XLA Ops:
  1.7 10.7 %collective-permute-start = (bf16[2,128,512]{2,1,0:T(8,128)(2,1)S(1)}, bf16[2,128,512]{2,1,0:T(8,128)(2,1)S(1)}, u32[]{:S(2)}, u32[]{:S(2)}) collective-permute-start(bf16[2,128,512]{2,1,0:T(8,128)(2,1)S(1)} %broadcast_select_fusion), channel_id=1, source_target_pairs={{0,32},{16,48},{32,64},{48,80},{64,96},{80,112},{96,0},{112,16},{1... | collective-permute-start | bytes 786440 | tf_op jit(solution)/shard_map/ppermute | solution.py:190
  4.2 14.6 %collective-permute-start.1 = (bf16[2,128,512]{2,1,0:T(8,128)(2,1)S(1)}, bf16[2,128,512]{2,1,0:T(8,128)(2,1)S(1)}, u32[]{:S(2)}, u32[]{:S(2)}) collective-permute-start(bf16[2,128,512]{2,1,0:T(8,128)(2,1)S(1)} %broadcast_select_fusion), channel_id=1, source_target_pairs={{0,64},{16,80},{32,96},{48,112},{64,0},{80,16},{96,32},{112,48},{1... | collective-permute-start | bytes 786440 | tf_op jit(solution)/shard_map/ppermute | solution.py:190
  7.5 11.3 %collective-permute-start.2 = (bf16[2,128,512]{2,1,0:T(8,128)(2,1)S(1)}, bf16[2,128,512]{2,1,0:T(8,128)(2,1)S(1)}, u32[]{:S(2)}, u32[]{:S(2)}) collective-permute-start(bf16[2,128,512]{2,1,0:T(8,128)(2,1)S(1)} %broadcast_select_fusion), channel_id=1, source_target_pairs={{0,96},{16,112},{32,0},{48,16},{64,32},{80,48},{96,64},{112,80},{1... | collective-permute-start | bytes 786440 | tf_op jit(solution)/shard_map/ppermute | solution.py:190
  23.1 6.9 %collective-permute-start.5 = (bf16[2,128,512]{2,1,0:T(8,128)(2,1)S(1)}, bf16[2,128,512]{2,1,0:T(8,128)(2,1)S(1)}, u32[]{:S(2)}, u32[]{:S(2)}) collective-permute-start(bf16[2,128,512]{2,1,0:T(8,128)(2,1)S(1)} %get-tuple-element.96), channel_id=1, source_target_pairs={{0,4},{1,5},{2,6},{3,7},{4,8},{5,9},{6,10},{7,11},{8,12},{9,13},{1... | collective-permute-start | bytes 786440 | tf_op jit(solution)/shard_map/ppermute | solution.py:185
  24.5 7.6 %collective-permute-start.6 = (bf16[2,128,512]{2,1,0:T(8,128)(2,1)S(1)}, bf16[2,128,512]{2,1,0:T(8,128)(2,1)S(1)}, u32[]{:S(2)}, u32[]{:S(2)}) collective-permute-start(bf16[2,128,512]{2,1,0:T(8,128)(2,1)S(1)} %get-tuple-element.96), channel_id=1, source_target_pairs={{0,12},{1,13},{2,14},{3,15},{4,0},{5,1},{6,2},{7,3},{8,4},{9,5},{1... | collective-permute-start | bytes 786440 | tf_op jit(solution)/shard_map/ppermute | solution.py:185
  26.0 8.0 %collective-permute-start.4 = (bf16[2,128,512]{2,1,0:T(8,128)(2,1)S(1)}, bf16[2,128,512]{2,1,0:T(8,128)(2,1)S(1)}, u32[]{:S(2)}, u32[]{:S(2)}) collective-permute-start(bf16[2,128,512]{2,1,0:T(8,128)(2,1)S(1)} %get-tuple-element.96), channel_id=1, source_target_pairs={{0,8},{1,9},{2,10},{3,11},{4,12},{5,13},{6,14},{7,15},{8,0},{9,1},... | collective-permute-start | bytes 786440 | tf_op jit(solution)/shard_map/ppermute | solution.py:185
  34.2 10.0 %collective-permute-start.7 = (bf16[2,4,128,256]{3,2,1,0:T(8,128)(2,1)S(1)}, bf16[2,4,128,256]{3,2,1,0:T(8,128)(2,1)S(1)}, u32[]{:S(2)}, u32[]{:S(2)}) collective-permute-start(bf16[2,4,128,256]{3,2,1,0:T(8,128)(2,1)S(1)} %get-tuple-element.35.rest_0_), channel_id=1, source_target_pairs={{0,2},{1,3},{2,0},{3,1},{4,6},{5,7},{6,4},{7,5},{8,10},{9,11},{10,... | collective-permute-start | bytes 1572872 | tf_op jit(solution)/shard_map/ppermute | solution.py:185
  36.7 13.0 %collective-permute-start.8 = (bf16[2,4,128,256]{3,2,1,0:T(8,128)(2,1)S(1)}, bf16[2,4,128,256]{3,2,1,0:T(8,128)(2,1)S(1)}, u32[]{:S(2)}, u32[]{:S(2)}) collective-permute-start(bf16[2,4,128,256]{3,2,1,0:T(8,128)(2,1)S(1)} %get-tuple-element.35.rest_0_), channel_id=1, source_target_pairs={{0,1},{1,2},{2,3},{3,0},{4,5},{5,6},{6,7},{7,4},{8,9},{9,10},{10,1... | collective-permute-start | bytes 1572872 | tf_op jit(solution)/shard_map/ppermute | solution.py:185
  37.0 12.7 %collective-permute-start.9 = (bf16[2,4,128,256]{3,2,1,0:T(8,128)(2,1)S(1)}, bf16[2,4,128,256]{3,2,1,0:T(8,128)(2,1)S(1)}, u32[]{:S(2)}, u32[]{:S(2)}) collective-permute-start(bf16[2,4,128,256]{3,2,1,0:T(8,128)(2,1)S(1)} %get-tuple-element.35.rest_0_), channel_id=1, source_target_pairs={{0,3},{1,0},{2,1},{3,2},{4,7},{5,4},{6,5},{7,6},{8,11},{9,8},{10,9... | collective-permute-start | bytes 1572872 | tf_op jit(solution)/shard_map/ppermute | solution.py:185
  50.0 6.1 %collective-permute-start.10 = (bf16[4,4,128,256]{3,2,1,0:T(8,128)(2,1)S(1)}, bf16[4,4,128,256]{3,2,1,0:T(8,128)(2,1)S(1)}, u32[]{:S(2)}, u32[]{:S(2)}) collective-permute-start(bf16[4,4,128,256]{3,2,1,0:T(8,128)(2,1)S(1)} %pad_maximum_fusion.1), channel_id=1, source_target_pairs={{0,16},{16,0},{32,48},{48,32},{64,80},{80,64},{96,112},{112,96},{1... | collective-permute-start | bytes 3145736 | tf_op jit(solution)/shard_map/ppermute | solution.py:194
  52.1 25.2 %collective-permute-start.11 = (bf16[2,4,128,256]{3,2,1,0:T(8,128)(2,1)S(1)}, bf16[2,4,128,256]{3,2,1,0:T(8,128)(2,1)S(1)}, u32[]{:S(2)}, u32[]{:S(2)}) collective-permute-start(bf16[2,4,128,256]{3,2,1,0:T(8,128)(2,1)S(1)} %get-tuple-element.41.rest_0_), channel_id=1, source_target_pairs={{0,2},{1,3},{2,0},{3,1},{4,6},{5,7},{6,4},{7,5},{8,10},{9,11},{10,... | collective-permute-start | bytes 1572872 | tf_op jit(solution)/shard_map/ppermute | solution.py:185
  53.4 24.0 %collective-permute-start.12 = (bf16[2,4,128,256]{3,2,1,0:T(8,128)(2,1)S(1)}, bf16[2,4,128,256]{3,2,1,0:T(8,128)(2,1)S(1)}, u32[]{:S(2)}, u32[]{:S(2)}) collective-permute-start(bf16[2,4,128,256]{3,2,1,0:T(8,128)(2,1)S(1)} %get-tuple-element.41.rest_0_), channel_id=1, source_target_pairs={{0,1},{1,2},{2,3},{3,0},{4,5},{5,6},{6,7},{7,4},{8,9},{9,10},{10,1... | collective-permute-start | bytes 1572872 | tf_op jit(solution)/shard_map/ppermute | solution.py:185
  54.7 22.7 %collective-permute-start.13 = (bf16[2,4,128,256]{3,2,1,0:T(8,128)(2,1)S(1)}, bf16[2,4,128,256]{3,2,1,0:T(8,128)(2,1)S(1)}, u32[]{:S(2)}, u32[]{:S(2)}) collective-permute-start(bf16[2,4,128,256]{3,2,1,0:T(8,128)(2,1)S(1)} %get-tuple-element.41.rest_0_), channel_id=1, source_target_pairs={{0,3},{1,0},{2,1},{3,2},{4,7},{5,4},{6,5},{7,6},{8,11},{9,8},{10,9... | collective-permute-start | bytes 1572872 | tf_op jit(solution)/shard_map/ppermute | solution.py:185
  81.8 25.1 %collective-permute-start.18 = (bf16[2,4,128,256]{3,2,1,0:T(8,128)(2,1)S(1)}, bf16[2,4,128,256]{3,2,1,0:T(8,128)(2,1)S(1)}, u32[]{:S(2)}, u32[]{:S(2)}) collective-permute-start(bf16[2,4,128,256]{3,2,1,0:T(8,128)(2,1)S(1)} %pad_maximum_fusion.6), channel_id=1, source_target_pairs={{0,1},{1,2},{2,3},{3,0},{4,5},{5,6},{6,7},{7,4},{8,9},{9,10},{10,1... | collective-permute-start | bytes 1572872 | tf_op jit(solution)/shard_map/ppermute | solution.py:185
  83.0 23.8 %collective-permute-start.17 = (bf16[2,4,128,256]{3,2,1,0:T(8,128)(2,1)S(1)}, bf16[2,4,128,256]{3,2,1,0:T(8,128)(2,1)S(1)}, u32[]{:S(2)}, u32[]{:S(2)}) collective-permute-start(bf16[2,4,128,256]{3,2,1,0:T(8,128)(2,1)S(1)} %pad_maximum_fusion.5), channel_id=1, source_target_pairs={{0,3},{1,0},{2,1},{3,2},{4,7},{5,4},{6,5},{7,6},{8,11},{9,8},{10,9... | collective-permute-start | bytes 1572872 | tf_op jit(solution)/shard_map/ppermute | solution.py:185
  84.9 21.9 %collective-permute-start.16 = (bf16[2,4,128,256]{3,2,1,0:T(8,128)(2,1)S(1)}, bf16[2,4,128,256]{3,2,1,0:T(8,128)(2,1)S(1)}, u32[]{:S(2)}, u32[]{:S(2)}) collective-permute-start(bf16[2,4,128,256]{3,2,1,0:T(8,128)(2,1)S(1)} %pad_maximum_fusion.4), channel_id=1, source_target_pairs={{0,2},{1,3},{2,0},{3,1},{4,6},{5,7},{6,4},{7,5},{8,10},{9,11},{10,... | collective-permute-start | bytes 1572872 | tf_op jit(solution)/shard_map/ppermute | solution.py:185
  109.7 10.0 %collective-permute-start.20 = (bf16[2,4,128,256]{3,2,1,0:T(8,128)(2,1)S(1)}, bf16[2,4,128,256]{3,2,1,0:T(8,128)(2,1)S(1)}, u32[]{:S(2)}, u32[]{:S(2)}) collective-permute-start(bf16[2,4,128,256]{3,2,1,0:T(8,128)(2,1)S(1)} %pad_maximum_fusion.7), channel_id=1, source_target_pairs={{0,2},{1,3},{2,0},{3,1},{4,6},{5,7},{6,4},{7,5},{8,10},{9,11},{10,... | collective-permute-start | bytes 1572872 | tf_op jit(solution)/shard_map/ppermute | solution.py:185
  112.3 12.4 %collective-permute-start.21 = (bf16[2,4,128,256]{3,2,1,0:T(8,128)(2,1)S(1)}, bf16[2,4,128,256]{3,2,1,0:T(8,128)(2,1)S(1)}, u32[]{:S(2)}, u32[]{:S(2)}) collective-permute-start(bf16[2,4,128,256]{3,2,1,0:T(8,128)(2,1)S(1)} %pad_maximum_fusion.8), channel_id=1, source_target_pairs={{0,3},{1,0},{2,1},{3,2},{4,7},{5,4},{6,5},{7,6},{8,11},{9,8},{10,9... | collective-permute-start | bytes 1572872 | tf_op jit(solution)/shard_map/ppermute | solution.py:185
  113.6 11.6 %collective-permute-start.22 = (bf16[2,4,128,256]{3,2,1,0:T(8,128)(2,1)S(1)}, bf16[2,4,128,256]{3,2,1,0:T(8,128)(2,1)S(1)}, u32[]{:S(2)}, u32[]{:S(2)}) collective-permute-start(bf16[2,4,128,256]{3,2,1,0:T(8,128)(2,1)S(1)} %pad_maximum_fusion.9), channel_id=1, source_target_pairs={{0,1},{1,2},{2,3},{3,0},{4,5},{5,6},{6,7},{7,4},{8,9},{9,10},{10,1... | collective-permute-start | bytes 1572872 | tf_op jit(solution)/shard_map/ppermute | solution.py:185
  125.6 7.1 %collective-permute-start.23 = (bf16[2,128,512]{2,1,0:T(8,128)(2,1)S(1)}, bf16[2,128,512]{2,1,0:T(8,128)(2,1)S(1)}, u32[]{:S(2)}, u32[]{:S(2)}) collective-permute-start(bf16[2,128,512]{2,1,0:T(8,128)(2,1)S(1)} %get-tuple-element.70), channel_id=1, source_target_pairs={{0,8},{1,9},{2,10},{3,11},{4,12},{5,13},{6,14},{7,15},{8,0},{9,1},... | collective-permute-start | bytes 786440 | tf_op jit(solution)/shard_map/ppermute | solution.py:185
  128.6 7.0 %collective-permute-start.25 = (bf16[2,128,512]{2,1,0:T(8,128)(2,1)S(1)}, bf16[2,128,512]{2,1,0:T(8,128)(2,1)S(1)}, u32[]{:S(2)}, u32[]{:S(2)}) collective-permute-start(bf16[2,128,512]{2,1,0:T(8,128)(2,1)S(1)} %get-tuple-element.71), channel_id=1, source_target_pairs={{0,4},{1,5},{2,6},{3,7},{4,8},{5,9},{6,10},{7,11},{8,12},{9,13},{1... | collective-permute-start | bytes 786440 | tf_op jit(solution)/shard_map/ppermute | solution.py:185
  135.7 6.5 %collective-permute-start.26 = (bf16[2,128,512]{2,1,0:T(8,128)(2,1)S(1)}, bf16[2,128,512]{2,1,0:T(8,128)(2,1)S(1)}, u32[]{:S(2)}, u32[]{:S(2)}) collective-permute-start(bf16[2,128,512]{2,1,0:T(8,128)(2,1)S(1)} %fusion.2), channel_id=1, source_target_pairs={{0,32},{16,48},{32,64},{48,80},{64,96},{80,112},{96,0},{112,16},{1... | collective-permute-start | bytes 786440 | tf_op jit(solution)/shard_map/ppermute | solution.py:190
  136.7 10.9 %collective-permute-start.27 = (bf16[2,128,512]{2,1,0:T(8,128)(2,1)S(1)}, bf16[2,128,512]{2,1,0:T(8,128)(2,1)S(1)}, u32[]{:S(2)}, u32[]{:S(2)}) collective-permute-start(bf16[2,128,512]{2,1,0:T(8,128)(2,1)S(1)} %fusion.2), channel_id=1, source_target_pairs={{0,64},{16,80},{32,96},{48,112},{64,0},{80,16},{96,32},{112,48},{1... | collective-permute-start | bytes 786440 | tf_op jit(solution)/shard_map/ppermute | solution.py:190
  138.8 9.9 %collective-permute-start.28 = (bf16[2,128,512]{2,1,0:T(8,128)(2,1)S(1)}, bf16[2,128,512]{2,1,0:T(8,128)(2,1)S(1)}, u32[]{:S(2)}, u32[]{:S(2)}) collective-permute-start(bf16[2,128,512]{2,1,0:T(8,128)(2,1)S(1)} %fusion.2), channel_id=1, source_target_pairs={{0,96},{16,112},{32,0},{48,16},{64,32},{80,48},{96,64},{112,80},{1... | collective-permute-start | bytes 786440 | tf_op jit(solution)/shard_map/ppermute | solution.py:190
  (9 other events, 42.9 us)
